TPU v7x, 256 devices: a whole 4x4x8 slice. The times are simulated.
256 devices in a mesh: section: 2 (over z_hi), expert: 64 (over y, x, z_lo), tensor: 2 (over core).
Axes of the slice: x: 4, y: 4, z: 8 (z_hi: 2, z_lo: 4; z = z_hi * 4 + z_lo), core: 2. Of those that a mesh axis runs over, the one named last changes fastest.
Arguments:
- pre_kv: bfloat16 [4, 2, 2048, 8192], P(('section', 'tensor'), None, None, 'expert'), may hold values from -6 to 6
- pre_gate: float32 [4, 64, 2048], P(('section', 'tensor'), 'expert'), may hold values from -1 to 0, as said below
- pre_len: int32 [4], P(('section', 'tensor')), may hold values from 256 to 2048, as said below
- owners: int32 [4], P(('section', 'tensor')), may hold values from 0 to 7, as said below
- win_len: int32 [32], P(('section', 'tensor')), may hold values from 2 to 1024, as said below
- dec_qkv: bfloat16 [32, 3, 8192], P(('section', 'tensor'), None, 'expert'), may hold values from -256 to 256
- dec_gate: float32 [32, 64], P(('section', 'tensor'), 'expert'), may hold values from -1 to -0.05
- state_cache: bfloat16 [32, 64, 128, 128], P(('section', 'tensor'), 'expert'), may hold values from -12 to 12
- win_cache: bfloat16 [32, 2, 1024, 8192], P(('section', 'tensor'), None, None, 'expert'), may hold values from -7 to 7
- head_gain: float32 [2, 8192], P(None, 'expert'), may hold values from 0.1 to 1.9
- out_weight: bfloat16 [8192, 2048], P('expert'), may hold values from -0.1875 to 0.1875
- resid: bfloat16 [32, 2048], P(('section', 'tensor')), may hold values from -6 to 6
- moe_gain: float32 [2048], replicated, may hold values from 0.1 to 1.9
- router: bfloat16 [2048, 128], replicated, may hold values from -0.125 to 0.125
- routes: int32 [32, 8], replicated, may hold values from 0 to 127, all different within a row; in each aligned block of 32 rows (0 to 31, 32 to 63, ...) at most 4 rows name the same one
- w_in: bfloat16 [128, 2048, 2, 1024], P(('section', 'expert'), None, None, 'tensor'), may hold values from -0.125 to 0.125
- w_down: bfloat16 [128, 1024, 2048], P(('section', 'expert'), 'tensor'), may hold values from -0.75 to 0.75
Outputs:
- layer_out: bfloat16 [32, 2048], P(('section', 'tensor'), 'expert')
- new_state: float32 [32, 64, 128, 128], P(('section', 'tensor'), 'expert')
Inputs may be any that keep to these rules, and one draw needn't show every extreme that they name: `pre_gate`: log decays; some heads forget within some tens of positions. `pre_len`: some request has length 2048. `owners`: a row within the block of 8 decode rows. `win_len`: the live positions are the last ones of the 1024; in the row that takes an incoming request it equals min(1024, that request's pre_len). `routes`: each row names 8 different experts; every expert is named by 1 to 4 of the 32 rows, a bound that some block reaches.
All inputs are finite; a program needn't handle non-finite values.
Results may differ from a plain program's by a relative error of at most 0.006.
Values may be sent and summed in bfloat16 or wider, within the bound.
No kernel may reach another device: no remote copies, remote signals or barrier semaphores. Data moves between devices by JAX's collectives and lax.ppermute only.
A program may use at most 64 MiB of HBM per device.

v0:
```python
import jax
import jax.numpy as jnp
from jax import lax
from jax.sharding import PartitionSpec as P


def from_partner(shard, axis, apart):
    return lax.ppermute(shard, axis, [(i, i ^ 1 << apart) for i in range(lax.axis_size(axis))])


def norm_rows(values, gain_row):
    return values * lax.rsqrt(jnp.mean(values * values, axis=-1, keepdims=True) + 1e-06) * gain_row


def window_part(queries, window_kv, live_len, self_score):
    window_width = window_kv.shape[2]
    score_scale = queries.shape[-1] ** (-0.5)
    scores = (
        jnp.einsum("rd,rwd->rw", queries, window_kv[:, 0], preferred_element_type=jnp.float32)
        * score_scale
    )
    live_mask = jnp.arange(window_width)[None, :] >= (window_width - live_len)[:, None]
    row_peak = jnp.maximum(jnp.max(jnp.where(live_mask, scores, -jnp.inf), axis=1), self_score)
    probabilities = jnp.where(live_mask, jnp.exp(scores - row_peak[:, None]), 0.0).astype(
        jnp.bfloat16
    )
    probabilities = lax.optimization_barrier(probabilities)
    numerator = jnp.einsum(
        "rw,rwd->rd", probabilities, window_kv[:, 1], preferred_element_type=jnp.float32
    )
    denominator = jnp.sum(probabilities.astype(jnp.float32), axis=1)
    return (row_peak, numerator, denominator)


def expert_rows(rows_in, gates, w_in, w_down):
    half_units = w_in.shape[3]
    hidden_pre = jnp.dot(
        rows_in, w_in[0].reshape(w_in.shape[1], 2 * half_units), preferred_element_type=jnp.float32
    )
    activated = (jax.nn.silu(hidden_pre[:, :half_units]) * hidden_pre[:, half_units:]).astype(
        jnp.bfloat16
    )
    return gates[:, None] * jnp.dot(activated, w_down[0], preferred_element_type=jnp.float32)


def on_device(
    pre_kv,
    pre_gate,
    pre_len,
    owners,
    win_len,
    dec_qkv,
    dec_gate,
    state_cache,
    win_cache,
    head_gain,
    out_weight,
    resid,
    moe_gain,
    router,
    routes,
    w_in,
    w_down,
):
    prompt_kv = pre_kv[0]
    decays = pre_gate[0, 0]
    length = pre_len[0]
    positions = jnp.arange(prompt_kv.shape[1])
    live_mask = positions < length
    kept_decays = jnp.where(live_mask, decays, 0.0)
    suffix = jnp.sum(kept_decays) - jnp.cumsum(kept_decays)
    token_weights = jnp.where(live_mask, jnp.exp(suffix), 0.0)
    scaled_keys = (prompt_kv[0].astype(jnp.float32) * token_weights[:, None]).astype(jnp.bfloat16)
    fresh_state = jnp.einsum(
        "td,te->de", scaled_keys, prompt_kv[1], preferred_element_type=jnp.float32
    ).astype(jnp.bfloat16)
    window_width = win_cache.shape[2]
    padded = jnp.concatenate(
        [jnp.zeros((2, window_width, prompt_kv.shape[2]), prompt_kv.dtype), prompt_kv], axis=1
    )
    fresh_window = lax.dynamic_slice_in_dim(padded, length, window_width, 1)
    owner_slot = owners[0]
    queries = dec_qkv[:, 0]
    new_keys = dec_qkv[:, 1]
    new_values = dec_qkv[:, 2]
    score_scale = queries.shape[-1] ** (-0.5)
    self_score = (
        jnp.sum(queries.astype(jnp.float32) * new_keys.astype(jnp.float32), axis=1) * score_scale
    )
    row_count = dec_qkv.shape[0]
    taken_rows = jnp.arange(row_count) == owner_slot
    got_state, got_window = from_partner((fresh_state, fresh_window), "section", 0)
    window_kv = jnp.where(taken_rows[:, None, None, None], got_window[None], win_cache)
    row_peak, numerator, denominator = window_part(queries, window_kv, win_len, self_score)
    previous = jnp.where(taken_rows[:, None, None], got_state[None], state_cache[:, 0])
    self_prob = lax.optimization_barrier(
        jnp.exp(self_score - row_peak).astype(jnp.bfloat16)
    ).astype(jnp.float32)
    numerator = numerator + self_prob[:, None] * new_values.astype(jnp.float32)
    denominator = denominator + self_prob
    window_out = numerator / denominator[:, None]
    states = (
        jnp.exp(dec_gate)[:, :, None] * previous.astype(jnp.float32)
        + new_keys.astype(jnp.float32)[:, :, None] * new_values.astype(jnp.float32)[:, None, :]
    )
    linear_out = jnp.einsum(
        "rd,rde->re", queries.astype(jnp.float32), states, precision=lax.Precision.HIGHEST
    )
    head_out = (norm_rows(linear_out, head_gain[0]) + norm_rows(window_out, head_gain[1])).astype(
        jnp.bfloat16
    )
    partial_value = jnp.dot(head_out, out_weight, preferred_element_type=jnp.float32)
    attended = lax.psum(partial_value, "expert")
    hidden = (resid.astype(jnp.float32) + attended).astype(jnp.bfloat16)
    every_row = lax.all_gather(hidden, ("section", "tensor"), axis=0, tiled=True)
    normed = norm_rows(every_row.astype(jnp.float32), moe_gain).astype(jnp.bfloat16)
    logits = jnp.dot(normed, router, preferred_element_type=jnp.float32)
    expert_count = logits.shape[1]
    expert_ids = jnp.arange(expert_count, dtype=jnp.int32)
    picked = jnp.sum(
        jnp.where(routes[:, :, None] == expert_ids[None, None, :], logits[:, None, :], 0.0), axis=2
    )
    chosen = jax.nn.sigmoid(picked)
    shares = chosen / jnp.sum(chosen, axis=1, keepdims=True)
    expert_id = lax.axis_index("section") * lax.axis_size("expert") + lax.axis_index("expert")
    own_gate = jnp.sum(jnp.where(routes == expert_id, shares, 0.0), axis=1)
    expert_term = expert_rows(normed, own_gate, w_in, w_down)
    partial_rows = lax.psum_scatter(
        expert_term, ("section", "tensor"), scatter_dimension=0, tiled=True
    )
    mixture = lax.psum_scatter(partial_rows, "expert", scatter_dimension=1, tiled=True)
    column_count = mixture.shape[1]
    own_columns = lax.dynamic_slice_in_dim(
        hidden, lax.axis_index("expert") * column_count, column_count, 1
    )
    layer_out = (own_columns.astype(jnp.float32) + mixture).astype(jnp.bfloat16)
    return (layer_out, states[:, None])


def solution(mesh):
    placed = (
        P(("section", "tensor"), None, None, "expert"),
        P(("section", "tensor"), "expert", None),
        P(("section", "tensor")),
        P(("section", "tensor")),
        P(("section", "tensor")),
        P(("section", "tensor"), None, "expert"),
        P(("section", "tensor"), "expert"),
        P(("section", "tensor"), "expert", None, None),
        P(("section", "tensor"), None, None, "expert"),
        P(None, "expert"),
        P("expert", None),
        P(("section", "tensor"), None),
        P(),
        P(),
        P(),
        P(("section", "expert"), None, None, "tensor"),
        P(("section", "expert"), "tensor", None),
    )
    return jax.shard_map(
        on_device,
        mesh=mesh,
        in_specs=placed,
        out_specs=(
            P(("section", "tensor"), "expert"),
            P(("section", "tensor"), "expert", None, None),
        ),
        check_vma=False,
    )
```

profile of v0, /device:TPU:0, one launch (start us, length us, event | category | flops | bytes accessed | tf_op | source)
XLA Modules:
  0.0 1095.8 jit_solution(7324526848556141540)
XLA Ops:
  7.2 0.0 copy-start
  7.2 0.0 all-reduce.3.cloned.1.call-start
  8.0 1.2 pad_dynamic-slice_fusion
  9.2 5.6 collective-permute-start.1
  14.8 0.7 fusion.30
  15.5 0.3 reduce-window.9
  15.8 0.1 slice.55
  15.9 0.1 slice_reduce_fusion
  16.0 1.3 select_reduce_fusion.3
  17.3 0.7 bitcast_select_fusion.2
  18.1 1.9 convolution_convert_fusion
  19.9 0.5 collective-permute-start
  20.5 0.7 slice_bitcast_fusion.4
  21.2 0.8 multiply_reduce_fusion.1
  22.6 0.7 broadcast_subtract_fusion
  23.3 0.7 exponential_bitcast_fusion
  24.0 0.8 slice_bitcast_fusion.6
  24.7 5.0 collective-permute-done
  29.7 1.5 fusion.6
  31.1 0.1 multiply_reduce_fusion.2
  31.3 0.0 collective-permute-done.1
  31.3 2.7 broadcast_select_fusion
  34.0 0.0 copy-start.5
  34.0 0.0 copy-start.7
  34.0 0.6 fusion.1
  34.6 0.2 select_reduce_fusion.1
  34.9 0.1 select_convert_fusion
  35.0 0.1 convert_reduce_fusion
  35.1 0.4 fusion
  35.5 0.0 copy-done.5
  35.5 0.2 multiply_reduce_fusion
  35.7 0.0 copy-done.7
  35.7 0.9 fusion.33
  36.6 0.0 all-reduce.3.cloned.1.call-update
  36.6 0.0 reduce-scatter.5.cloned.1.call-start
  36.6 0.0 copy-start.6
  36.7 0.0 copy-start.4
  36.7 0.0 copy-start.3
  36.7 5.3 copy.31
  42.0 0.0 copy-done.6
  42.0 0.1 copy.22
  42.1 625.3 %all-reduce.3.cloned.1.call-done = f32[8,2048]{1,0:T(8,128)} async-done(((f32[8,2048]{1,0:T(8,128)}), f32[8,2048]{1,0:T(8,128)}) %all-reduce.3.cloned.1.call-update) | async-done | bytes 65552 | tf_op jit(solution)/shard_map/psum | solution.py:113
  667.4 0.0 copy-done.4
  667.4 0.8 add_convert_fusion
  668.2 9.3 all_gather.3
  677.6 0.1 fusion.14
  677.7 0.0 copy-done.3
  677.7 0.0 copy-start.2
  677.7 3.1 fusion.23
  680.8 0.3 fusion.25
  681.1 0.2 select_reduce_fusion
  681.3 0.1 divide_reduce_fusion
  681.4 0.2 select_reduce_fusion.2
  681.6 1.2 convolution_multiply_fusion
  682.8 0.0 reduce-scatter.5.cloned.1.call-update
  682.8 0.0 reduce-scatter.7.cloned.1.call-start
  682.9 32.4 %reduce-scatter.5.cloned.1.call-done = f32[8,2048]{1,0:T(8,128)} async-done(((f32[32,2048]{1,0:T(8,128)}), f32[8,2048]{1,0:T(8,128)}) %reduce-scatter.5.cloned.1.call-update) | async-done | bytes 65552 | tf_op jit(solution)/shard_map/reduce_scatter | solution.py:128
  715.3 2.2 copy.29
  717.5 0.0 reduce-scatter.7.cloned.1.call-update
  717.5 0.0 copy-done.2
  717.5 1.0 multiply_add_fusion
  718.5 369.3 %reduce-scatter.7.cloned.1.call-done = f32[32,8]{1,0:T(8,128)} async-done(((f32[2048,8]{1,0:T(8,128)}), f32[32,8]{1,0:T(8,128)}) %reduce-scatter.7.cloned.1.call-update) | async-done | bytes 1040
  1087.9 0.8 copy.30
  1088.7 0.7 add_convert_fusion.1
  (11 shorter events, 0.1 us)
Async XLA Ops:
  7.2 674.5 %copy-start = (bf16[1,512,2048]{2,1,0:T(8,128)(2,1)S(1)}, bf16[1,512,2048]{2,1,0:T(8,128)(2,1)}, u32[]{:S(2)}) copy-start(bf16[1,512,2048]{2,1,0:T(8,128)(2,1)} %param.33) | copy-start | bytes 6291460
  7.2 660.2 %all-reduce.3.cloned.1.call-start = ((), (), s32[]{:S(2)}) async-start(), calls=%async_computation.2 | async-start | bytes 131072 | tf_op jit(solution)/shard_map/psum | solution.py:113
  9.2 22.0 %collective-permute-start.1 = (bf16[2,1024,128]{2,1,0:T(8,128)(2,1)S(1)}, bf16[2,1024,128]{2,1,0:T(8,128)(2,1)S(1)}, u32[]{:S(2)}, u32[]{:S(2)}) collective-permute-start(bf16[2,1024,128]{2,1,0:T(8,128)(2,1)S(1)} %pad_dynamic-slice_fusion), channel_id=1, source_target_pairs={{0,128},{128,0},{1,129},{129,1},{2,130},{130,2},{3,131},{131,3},{4... | collective-permute-start | bytes 1572872 | tf_op jit(solution)/shard_map/ppermute | solution.py:8
  19.9 9.8 collective-permute-start
  34.0 1.5 copy-start.5
  34.0 1.7 copy-start.7
  36.6 678.7 %reduce-scatter.5.cloned.1.call-start = ((), (), s32[]{:S(2)}) async-start(), calls=%async_computation.3 | async-start | bytes 327680 | tf_op jit(solution)/shard_map/reduce_scatter | solution.py:128
  36.6 5.4 copy-start.6
  36.7 630.7 %copy-start.4 = (bf16[8,2048]{1,0:T(8,128)(2,1)S(1)}, bf16[8,2048]{1,0:T(8,128)(2,1)}, u32[]{:S(2)}) copy-start(bf16[8,2048]{1,0:T(8,128)(2,1)} %param.28) | copy-start | bytes 98308
  36.7 641.1 %copy-start.3 = (f32[2048]{0:T(1024)S(1)}, f32[2048]{0:T(1024)}, u32[]{:S(2)}) copy-start(f32[2048]{0:T(1024)} %param.29) | copy-start | bytes 24580
  42.0 638.8 %copy-start.1 = (bf16[2048,128]{1,0:T(8,128)(2,1)S(1)}, bf16[2048,128]{1,0:T(8,128)(2,1)}, u32[]{:S(2)}) copy-start(bf16[2048,128]{1,0:T(8,128)(2,1)} %param.30) | copy-start | bytes 1572868
  677.7 39.8 %copy-start.2 = (bf16[8,1,128,128]{3,2,1,0:T(8,128)(2,1)S(1)}, bf16[8,1,128,128]{3,2,1,0:T(8,128)(2,1)}, u32[]{:S(2)}) copy-start(bf16[8,1,128,128]{3,2,1,0:T(8,128)(2,1)} %param.24) | copy-start | bytes 786436
  682.8 405.1 %reduce-scatter.7.cloned.1.call-start = ((), (), s32[]{:S(2)}) async-start(), calls=%async_computation.4 | async-start | bytes 1064960
Sparse Core Ops, SparseCore 0:
  36.7 630.6 all-reduce.2
  682.9 32.3 reduce-scatter.4
  717.8 370.0 reduce-scatter.6
where the time goes:
time: 1100 us
  waiting for transfers between devices  1030 us (94%)
  between operations  15.4 us (1%)
  other arithmetic  11.9 us (1%)
  local copies, waits for them, and re-layouts  11.2 us (1%)
    psum x1, waiting for transfers between devices, on_device(): attended = lax.psum(partial_value, 'expert')  625 us
    unnamed x4, waiting for transfers between devices  369 us
    reduce_scatter x1, waiting for transfers between devices, on_device(): lax.psum_scatter(expert_term, ('section', 'tensor'), scatter_dimension=0,...  32.4 us
  transfers between devices with their start and end apart: 5, of which 4 were waited for; matrix products, arithmetic and copies ran while one was open for 2% of the time, Pallas kernels for 0%

commit v1 on v0

v1 whole, which is shorter than its diff:
```python
import jax
import jax.numpy as jnp
from jax import lax
from jax.sharding import Mesh, PartitionSpec as P

GRID = ("y", "x", "z")
BLOCKS = ("s", "t")
F32 = jnp.float32
BF16 = jnp.bfloat16


def swap(shard, axis, flip):
    return lax.ppermute(shard, axis, [(i, i ^ flip) for i in range(lax.axis_size(axis))])


def norm_rows(values, gain_row):
    return values * lax.rsqrt(jnp.mean(values * values, axis=-1, keepdims=True) + 1e-06) * gain_row


def prompt_state(prompt_kv, decays, length):
    positions = jnp.arange(prompt_kv.shape[1])
    live = positions < length
    kept = jnp.where(live, decays, 0.0)
    suffix = jnp.sum(kept) - jnp.cumsum(kept)
    weights = jnp.where(live, jnp.exp(suffix), 0.0)
    scaled = (prompt_kv[0].astype(F32) * weights[:, None]).astype(BF16)
    return jnp.einsum("td,te->de", scaled, prompt_kv[1], preferred_element_type=F32).astype(BF16)


def window_part(queries, keys, values, live, self_score, scale):
    scores = jnp.einsum("rd,rwd->rw", queries, keys, preferred_element_type=F32) * scale
    peak = jnp.maximum(jnp.max(jnp.where(live, scores, -jnp.inf), axis=1), self_score)
    prob = jnp.where(live, jnp.exp(scores - peak[:, None]), 0.0).astype(BF16)
    prob = lax.optimization_barrier(prob)
    numerator = jnp.einsum("rw,rwd->rd", prob, values, preferred_element_type=F32)
    return peak, numerator, jnp.sum(prob.astype(F32), axis=1)


def on_device(
    pre_kv, pre_gate, pre_len, owners, win_len, dec_qkv, dec_gate, state_cache, win_cache,
    head_gain, out_weight, resid, moe_gain, router, routes, w_in, w_down,
):
    section, core = lax.axis_index("s"), lax.axis_index("t")
    row, col, deep = lax.axis_index("y"), lax.axis_index("x"), lax.axis_index("z")
    block = section * 2 + core
    lane_tile = row * 4 + col
    head = lane_tile * 4 + deep

    owner = owners[0]
    piece_all = lax.dynamic_slice(resid, (0, lane_tile * 128), (8, 128))
    mine = lax.dynamic_slice_in_dim(dec_qkv, owner, 1, 0)[0].astype(F32)
    message = jnp.concatenate(
        [
            mine,
            jnp.broadcast_to(lax.dynamic_slice_in_dim(dec_gate, owner, 1, 0), (1, 128)),
            lax.dynamic_slice_in_dim(piece_all, owner, 1, 0).astype(F32),
            jnp.full((3, 128), owner.astype(F32)),
        ],
        axis=0,
    )
    got = swap(message, "s", 1)
    flag = jnp.full((8, 128), owner.astype(F32))
    beside = swap(flag, "t", 1)
    across = swap(flag, BLOCKS, 3)

    prompt_kv = pre_kv[0]
    length = pre_len[0]
    fresh_state = prompt_state(prompt_kv, pre_gate[0, 0], length)
    got_state = swap(fresh_state, "s", 1)

    taken = jnp.arange(8) == owner
    guest = got[:3].astype(BF16)
    qkv = jnp.where(taken[:, None, None], guest[None], dec_qkv)
    gate = jnp.where(taken[:, None], got[3, 0], dec_gate)
    queries, keys, values = qkv[:, 0], qkv[:, 1], qkv[:, 2]
    scale = 128 ** (-0.5)
    self_raw = jnp.sum(queries.astype(F32) * keys.astype(F32), axis=1)
    self_score = self_raw * scale

    width = win_cache.shape[2]
    live = jnp.arange(width)[None, :] >= (width - win_len)[:, None]
    peak, numerator, denominator = window_part(
        queries, win_cache[:, 0], win_cache[:, 1], live, self_score, scale
    )
    places = jnp.arange(prompt_kv.shape[1])[None, :]
    inside = (places < length) & (places >= length - width)
    guest_self = jnp.sum(got[0] * got[1])[None] * scale
    guest_peak, guest_num, guest_den = window_part(
        guest[0][None], prompt_kv[0][None], prompt_kv[1][None], inside, guest_self, scale
    )
    peak = jnp.where(taken, guest_peak[0], peak)
    numerator = jnp.where(taken[:, None], guest_num, numerator)
    denominator = jnp.where(taken, guest_den[0], denominator)
    self_prob = lax.optimization_barrier(jnp.exp(self_score - peak).astype(BF16)).astype(F32)
    numerator = numerator + self_prob[:, None] * values.astype(F32)
    denominator = denominator + self_prob
    window_out = numerator / denominator[:, None]

    cached = state_cache[:, 0]
    used = jnp.where(taken[:, None, None], fresh_state[None], cached)
    linear_out = (
        jnp.exp(gate) * jnp.einsum("rd,rde->re", queries, used, preferred_element_type=F32)
        + self_raw[:, None] * values.astype(F32)
    )
    head_out = (norm_rows(linear_out, head_gain[0]) + norm_rows(window_out, head_gain[1])).astype(BF16)
    partial = jnp.dot(head_out, out_weight, preferred_element_type=F32)

    pieces = partial.reshape(4, 2, 16, 128).transpose(2, 0, 1, 3).reshape(64, 2, 128)
    attended = lax.all_to_all(pieces, GRID, 0, 0).sum(0)
    own_resid = jnp.where(taken[:, None], got[4], piece_all.astype(F32))
    own_resid = lax.dynamic_slice_in_dim(own_resid, deep * 2, 2, 0)
    hidden = (own_resid + attended).astype(BF16)
    every = lax.all_to_all(
        jnp.broadcast_to(hidden[None], (256, 2, 128)), ("s", "t", "y", "x", "z"), 0, 0
    )
    every = every.reshape(4, 16, 4, 2, 128).transpose(0, 2, 3, 1, 4).reshape(32, 2048)

    partner_owner = got[5, 0].astype(jnp.int32)
    beside_owner = beside[0, 0].astype(jnp.int32)
    across_owner = across[0, 0].astype(jnp.int32)
    ids = jnp.arange(32)
    their_block, their_row = ids // 8, ids % 8
    held = jnp.where(
        their_block == block, owner,
        jnp.where(their_block == (block ^ 2), partner_owner,
                  jnp.where(their_block == (block ^ 1), beside_owner, across_owner)),
    )
    held_partner = jnp.where(
        their_block == block, partner_owner,
        jnp.where(their_block == (block ^ 2), owner,
                  jnp.where(their_block == (block ^ 1), across_owner, beside_owner)),
    )
    source = jnp.where(their_row == held, (their_block ^ 2) * 8 + held_partner, ids)
    order = (source[:, None] == ids[None, :]).astype(BF16)
    every = jnp.dot(order, every, preferred_element_type=F32)

    normed = norm_rows(every, moe_gain).astype(BF16)
    logits = jnp.dot(normed, router, preferred_element_type=F32)
    expert_ids = jnp.arange(logits.shape[1], dtype=jnp.int32)
    named = routes[:, :, None] == expert_ids[None, None, :]
    picked = jnp.sum(jnp.where(named, logits[:, None, :], 0.0), axis=2)
    chosen = jax.nn.sigmoid(picked)
    shares = chosen / jnp.sum(chosen, axis=1, keepdims=True)
    expert_id = section * 64 + head
    own_gate = jnp.sum(jnp.where(routes == expert_id, shares, 0.0), axis=1)

    member = jnp.any(named, axis=1)
    below = (ids[:, None] > ids[None, :]).astype(F32)
    rank = jnp.dot(below, member.astype(F32))
    slot = jnp.where(member, rank, -1.0)
    own_slot = jnp.sum(jnp.where(expert_ids[None, :] == expert_id, slot, 0.0), axis=1)
    chooser = own_slot[None, :] == jnp.arange(4, dtype=F32)[:, None]
    rows_in = jnp.dot(chooser.astype(BF16), normed, preferred_element_type=F32).astype(BF16)
    gates = jnp.sum(jnp.where(chooser, own_gate[None, :], 0.0), axis=1)

    units = w_in.shape[3]
    pre = jnp.dot(rows_in, w_in[0].reshape(w_in.shape[1], 2 * units), preferred_element_type=F32)
    act = (jax.nn.silu(pre[:, :units]) * pre[:, units:]).astype(BF16)
    term = gates[:, None] * jnp.dot(act, w_down[0], preferred_element_type=F32)
    term = term.reshape(4, 16, 4, 32).transpose(2, 1, 0, 3).reshape(1, 64, 1, 128)
    term = jnp.broadcast_to(term, (4, 64, 1, 128)).reshape(256, 1, 128)
    back = lax.all_to_all(term, ("s", "t", "z", "y", "x"), 0, 0)
    back = back.reshape(2, 2, 4, 16, 4, 32)

    own_slots = lax.dynamic_slice_in_dim(slot, block * 8, 8, 0)
    own_slots = own_slots.reshape(8, 2, 16, 4).transpose(0, 1, 3, 2)
    use = (own_slots[:, :, None, :, :, None] == jnp.arange(4, dtype=F32)).astype(F32)
    use = jnp.broadcast_to(use, (8, 2, 2, 4, 16, 4))
    mixture = jnp.einsum(
        "rn,nc->rc", use.reshape(8, 1024), back.reshape(1024, 32), precision=lax.Precision.HIGHEST
    )
    own = lax.dynamic_slice(every, (block * 8, head * 32), (8, 32))
    layer_out = (own + mixture).astype(BF16)

    previous = jnp.where(taken[:, None, None], got_state[None], cached).astype(F32)
    own_k, own_v = dec_qkv[:, 1].astype(F32), dec_qkv[:, 2].astype(F32)
    states = jnp.exp(dec_gate)[:, :, None] * previous + own_k[:, :, None] * own_v[:, None, :]
    return layer_out, states[:, None]


def solution(mesh):
    fine = Mesh(mesh.devices.reshape(2, 4, 4, 4, 2), ("s", "y", "x", "z", "t"))
    placed = (
        P(BLOCKS, None, None, GRID),
        P(BLOCKS, GRID, None),
        P(BLOCKS),
        P(BLOCKS),
        P(BLOCKS),
        P(BLOCKS, None, GRID),
        P(BLOCKS, GRID),
        P(BLOCKS, GRID, None, None),
        P(BLOCKS, None, None, GRID),
        P(None, GRID),
        P(GRID, None),
        P(BLOCKS, None),
        P(),
        P(),
        P(),
        P(("s",) + GRID, None, None, "t"),
        P(("s",) + GRID, "t", None),
    )
    return jax.shard_map(
        on_device,
        mesh=fine,
        in_specs=placed,
        out_specs=(P(BLOCKS, GRID), P(BLOCKS, GRID, None, None)),
        check_vma=False,
    )
```

time: 1100 us -> 119 us (0.11)
  the two profiles are of different devices: /device:TPU:0 before, /device:TPU:1 now
where the time goes in v1:
time: 119 us; the launch traced here: 118 us
  starting transfers between devices  41.2 us (35%)
  waiting for transfers between devices  21.7 us (18%)
  matrix products  18 us (15%)
  other arithmetic  15.9 us (13%)
  local copies, waits for them, and re-layouts  15.4 us (13%)
  between operations  5.46 us (5%)
    ppermute x4, starting transfers between devices, swap(): lax.ppermute(shard, axis, [(i, i ^ flip) for i in range(lax.axis_size(axi...  13.9 us
    all_to_all x1, starting transfers between devices, on_device(): back = lax.all_to_all(term, ('s', 't', 'z', 'y', 'x'), 0, 0)  10.9 us
    all_to_all x1, waiting for transfers between devices, on_device(): back = lax.all_to_all(term, ('s', 't', 'z', 'y', 'x'), 0, 0)  10.7 us
    all_to_all x1, starting transfers between devices, on_device(): attended = lax.all_to_all(pieces, GRID, 0, 0).sum(0)  9.03 us
    all_to_all x1, waiting for transfers between devices, on_device(): attended = lax.all_to_all(pieces, GRID, 0, 0).sum(0)  7.99 us
    all_to_all x1, starting transfers between devices, on_device(): lax.all_to_all(jnp.broadcast_to(hidden[None], (256, 2, 128)), ('s', 't',...  7.42 us
    unnamed x22, local copies, waits for them, and re-layouts  6.19 us
    dot_general x2, matrix products, window_part(): jnp.einsum('rd,rwd->rw', queries, keys, preferred_element_type=F32) * scale  3.51 us
  transfers between devices with their start and end apart: 7, of which 3 were waited for; matrix products, arithmetic and copies ran while one was open for 39% of the time, Pallas kernels for 0%

profile of v1, /device:TPU:1, one launch (start us, length us, event | category | flops | bytes accessed | tf_op | source)
XLA Modules:
  0.0 117.7 jit_solution(12481035268752672881)
XLA Ops:
  1.5 3.3 %collective-permute-start.1 = (f32[8,128]{1,0:T(8,128)S(1)}, f32[8,128]{1,0:T(8,128)}, u32[]{:S(2)}, u32[]{:S(2)}) collective-permute-start(f32[8,128]{1,0:T(8,128)S(1)} %broadcast_in_dim.241), channel_id=1, source_target_pairs={{0,1},{1,0},{2,3},{3,2},{4,5},{5,4},{6,7},{7,6},{8,9},{9,8},{10,11... | collective-permute-start | bytes 12296 | tf_op jit(solution)/shard_map/ppermute | solution.py:13
  4.8 5.2 %collective-permute-start.2 = (f32[8,128]{1,0:T(8,128)S(1)}, f32[8,128]{1,0:T(8,128)}, u32[]{:S(2)}, u32[]{:S(2)}) collective-permute-start(f32[8,128]{1,0:T(8,128)S(1)} %broadcast_in_dim.241), channel_id=1, source_target_pairs={{0,129},{1,128},{128,1},{129,0},{2,131},{3,130},{130,3},{131,2},{4... | collective-permute-start | bytes 12296 | tf_op jit(solution)/shard_map/ppermute | solution.py:13
  10.0 0.7 dynamic-slice_convert_fusion
  10.7 1.2 %constant_dynamic-slice_fusion.2 = f32[1,1]{0,1:T(1,128)} fusion(f32[8,1]{0,1:T(1,128)} %param.23, s32[]{:T(128)S(6)} %select_n.182), kind=kLoop, calls=%fused_computation.106 | loop fusion | bytes 12 | tf_op jit(solution)/shard_map/dynamic_slice | solution.py:55
  11.9 0.7 pad.1.clone
  12.7 0.8 dynamic-slice_convert_fusion.1
  13.6 0.2 collective-permute-start
  14.4 0.7 fusion.31
  15.1 0.3 reduce-window.9
  15.5 0.1 slice_reduce_fusion
  15.7 1.3 %select_reduce_fusion.5 = f32[]{:T(128)} fusion(f32[2048]{0:T(1024)} %bitcast.153, s32[]{:T(128)} %bitcast.126), kind=kLoop, calls=%fused_computation.63 | loop fusion | flops 6143 | bytes 8200 | tf_op jit(solution)/shard_map/reduce_sum | solution.py:24
  17.0 0.7 bitcast_select_fusion.2
  17.7 2.5 %convolution_convert_fusion.1 = bf16[128,128]{1,0:T(8,128)(2,1)} fusion(f32[2048]{0:T(1024)S(1)} %bitcast_select_fusion.2, bf16[1,2,2048,128]{3,2,1,0:T(8,128)(2,1)} %param.17), kind=kOutput, calls=%fused_computation.10 | convolution fusion | flops 67911680 | bytes 1089536 | tf_op jit(solution)/shard_map/td,te->de/dot_general | solution.py:27
  20.1 5.2 %collective-permute-start.3 = (bf16[128,128]{1,0:T(8,128)(2,1)}, bf16[128,128]{1,0:T(8,128)(2,1)}, u32[]{:S(2)}, u32[]{:S(2)}) collective-permute-start(bf16[128,128]{1,0:T(8,128)(2,1)} %convolution_convert_fusion.1), channel_id=1, source_target_pairs={{0,128},{128,0},{1,129},{129,1},{2,130},{130,2},{3,131},{131,3},{4... | collective-permute-start | bytes 98312 | tf_op jit(solution)/shard_map/ppermute | solution.py:13
  25.3 0.7 broadcast_subtract_fusion
  26.0 0.8 slice_bitcast_fusion.5
  26.7 0.8 copy.33
  27.5 0.1 fusion.23
  27.7 1.3 %fusion.11 = f32[1,2048]{1,0:T(1,128)S(1)} fusion(bf16[1,2,2048,128]{3,2,1,0:T(8,128)(2,1)} %param.17, bf16[8,128]{1,0:T(8,128)(2,1)S(1)} %convert.8), kind=kOutput, calls=%fused_computation.18 | convolution fusion | flops 524288 | bytes 532992 | tf_op jit(solution)/shard_map/rd,rwd->rw/dot_general | solution.py:31
  28.9 0.8 broadcast_select_fusion
  29.7 0.1 fusion.37
  29.8 0.6 slice_bitcast_fusion.6
  31.1 0.6 select_reduce_fusion.4
  32.4 0.6 convert_reduce_fusion.1
  33.0 1.2 %convolution_bitcast_fusion.1 = f32[128]{0:T(128)S(1)} fusion(bf16[1,2,2048,128]{3,2,1,0:T(8,128)(2,1)} %param.17, bf16[1,2048]{1,0:T(2,128)(2,1)S(1)} %convert_element_type.152), kind=kOutput, calls=%fused_computation.15 | convolution fusion | flops 524288 | bytes 528896 | tf_op jit(solution)/shard_map/rw,rwd->rd/dot_general | solution.py:35
  34.2 2.2 %fusion.3 = f32[8,1,1024]{2,1,0:T(1,128)S(1)} fusion(bf16[8,2,1024,128]{3,2,1,0:T(8,128)(2,1)} %param.25, bf16[8,128,1]{1,0,2:T(8,128)(2,1)S(1)} %slice_bitcast_fusion.2), kind=kOutput, calls=%fused_computation.5 | convolution fusion | flops 2097152 | bytes 2131968 | tf_op jit(solution)/shard_map/rd,rwd->rw/dot_general | solution.py:31
  36.5 0.2 select_reduce_fusion.1
  36.8 0.1 convert_reduce_fusion
  36.9 2.0 %fusion.1 = f32[8,1,128]{2,1,0:T(1,128)S(1)} fusion(bf16[8,2,1024,128]{3,2,1,0:T(8,128)(2,1)} %param.25, bf16[8,1024,1]{1,0,2:T(8,128)(2,1)S(1)} %bitcast.151), kind=kOutput, calls=%fused_computation.3 | convolution fusion | flops 2097152 | bytes 2117632 | tf_op jit(solution)/shard_map/rw,rwd->rd/dot_general | solution.py:35
  38.9 1.0 fusion.20
  39.9 0.5 fusion.59
  40.4 1.2 exponential_bitcast_fusion
  41.6 0.6 select_add_fusion
  42.2 0.9 multiply_reduce_fusion.1
  43.2 0.2 convolution_bitcast_fusion
  43.5 0.7 copy.32
  44.2 9.0 %all-to-all-start = ((f32[64,2,128]{2,1,0:T(2,128)}), f32[64,2,128]{2,1,0:T(2,128)S(1)}, u32[]{:S(2)}, u32[]{:S(2)}) async-start(f32[64,2,128]{2,1,0:T(2,128)} %copy.32), calls=%async_computation | async-start | bytes 131072 | tf_op jit(solution)/shard_map/all_to_all | solution.py:109
  53.2 0.7 select_reduce_fusion.3
  54.1 8.0 %all-to-all-done = f32[64,2,128]{2,1,0:T(2,128)S(1)} async-done(((f32[64,2,128]{2,1,0:T(2,128)}), f32[64,2,128]{2,1,0:T(2,128)S(1)}, u32[]{:S(2)}, u32[]{:S(2)}) %all-to-all-start) | async-done | bytes 65568 | tf_op jit(solution)/shard_map/all_to_all | solution.py:109
  62.2 0.7 broadcast_in_dim.259
  62.9 7.4 %all-to-all-start.1 = ((bf16[256,2,128]{2,1,0:T(2,128)(2,1)}), bf16[256,2,128]{2,1,0:T(2,128)(2,1)S(1)}, u32[]{:S(2)}, u32[]{:S(2)}) async-start(bf16[256,2,128]{2,1,0:T(2,128)(2,1)} %broadcast_in_dim.259), calls=%async_computation.1 | async-start | bytes 262144 | tf_op jit(solution)/shard_map/all_to_all | solution.py:113
  70.4 5.4 %copy.45 = bf16[256,8,2,512]{3,1,2,0:T(8,128)(2,1)} copy(bf16[256,8,2,512]{3,2,1,0:T(2,128)(2,1)} %bitcast.142) | data formatting | bytes 8388608
  76.3 1.2 %slice.80 = f32[1,1]{1,0:T(1,128)} slice(f32[8,128]{1,0:T(8,128)} %collective-permute-done.1), slice={[0:1], [0:1]} | slice | bytes 8 | tf_op jit(solution)/shard_map/slice | solution.py:119
  78.1 1.2 %slice.81 = f32[1,1]{1,0:T(1,128)} slice(f32[8,128]{1,0:T(8,128)} %collective-permute-done.2), slice={[0:1], [0:1]} | slice | bytes 8 | tf_op jit(solution)/shard_map/slice | solution.py:120
  79.8 0.5 compare_select_fusion.1
  80.3 3.0 %all-to-all-done.1 = bf16[256,2,128]{2,1,0:T(2,128)(2,1)S(1)} async-done(((bf16[256,2,128]{2,1,0:T(2,128)(2,1)}), bf16[256,2,128]{2,1,0:T(2,128)(2,1)S(1)}, u32[]{:S(2)}, u32[]{:S(2)}) %all-to-all-start.1) | async-done | bytes 131104 | tf_op jit(solution)/shard_map/all_to_all | solution.py:113
  83.3 0.9 multiply_reduce_fusion
  84.3 1.0 fusion.57
  85.3 0.2 select_reduce_fusion
  85.5 0.1 divide_reduce_fusion
  85.6 0.2 select_reduce_fusion.2
  85.8 3.0 %fusion.7 = f32[4,1024]{1,0:T(4,128)S(1)} fusion(bf16[2048,1024]{1,0:T(8,128)(2,1)} %bitcast.141, f32[32]{0:T(128)} %get-tuple-element.20, f32[32,2048]{1,0:T(8,128)S(1)} %get-tuple-element.19, f32[2048]{0:T(1024)} %param.29, f32[32]{0:T(128)S(1)} %add_rsqrt_fusion), kind=kOutput, calls=%fused_computation.12 | convolution fusion | flops 17506432 | bytes 4481280 | tf_op jit(solution)/shard_map/dot_general | solution.py:157
  88.8 0.8 select_reduce_fusion.6
  89.6 0.4 convolution_multiply_fusion
  90.0 0.1 reshape.257
  90.2 0.1 broadcast_in_dim.269
  90.3 0.6 broadcast_in_dim.270
  91.0 10.9 %all-to-all-start.2 = ((f32[256,1,128]{2,1,0:T(1,128)}), f32[256,1,128]{2,1,0:T(1,128)S(1)}, u32[]{:S(2)}, u32[]{:S(2)}) async-start(f32[256,1,128]{2,1,0:T(1,128)} %bitcast.45), calls=%async_computation.2 | async-start | bytes 262144 | tf_op jit(solution)/shard_map/all_to_all | solution.py:162
  101.9 1.8 %multiply_add_fusion = f32[8,1,128,128]{3,2,1,0:T(8,128)} fusion(f32[8,128]{1,0:T(8,128)S(1)} %get-tuple-element.5, f32[8,128]{1,0:T(8,128)S(1)} %get-tuple-element.4, bf16[8,1,128,128]{3,2,1,0:T(8,128)(2,1)S(1)} %copy-done.2, f32[8]{0:T(128)S(1)} %copy-done.6, pred[8]{0:T(512)(128)(4,1)S(1)} %copy-done.5, bf16[128,128]{1,0:T(8,128)(2,1)} %collective-permute-done.3), kind=kLoop, calls=%fused_computation.22 | loop fusion | flops 655360 | bytes 827432 | tf_op jit(solution)/shard_map/add | solution.py:177
  103.7 10.7 %all-to-all-done.2 = f32[256,1,128]{2,1,0:T(1,128)S(1)} async-done(((f32[256,1,128]{2,1,0:T(1,128)}), f32[256,1,128]{2,1,0:T(1,128)S(1)}, u32[]{:S(2)}, u32[]{:S(2)}) %all-to-all-start.2) | async-done | bytes 131104 | tf_op jit(solution)/shard_map/all_to_all | solution.py:162
  114.4 0.5 broadcast.284
  114.9 0.9 reduce.9
  115.9 0.2 reshape_reshape.3
  116.1 1.6 %fusion.8 = bf16[8,32]{1,0:T(8,128)(2,1)} fusion(f32[8,1024]{0,1:T(8,128)S(1)} %bitcast.143, f32[1024,32]{1,0:T(8,128)S(1)} %reshape_reshape.3, f32[32,2048]{1,0:T(8,128)S(1)} %get-tuple-element.19, s32[]{:T(128)S(6)} %select_n.208, s32[]{:T(128)S(6)} %select_n.209), kind=kOutput, calls=%fused_computation.14 | convolution fusion | flops 3146240 | bytes 165384 | tf_op jit(solution)/shard_map/rn,nc->rc/dot_general | solution.py:169
  (52 shorter events, 1.0 us)
Async XLA Ops:
  0.6 89.0 %copy-start = (bf16[1,512,2048]{2,1,0:T(8,128)(2,1)S(1)}, bf16[1,512,2048]{2,1,0:T(8,128)(2,1)}, u32[]{:S(2)}) copy-start(bf16[1,512,2048]{2,1,0:T(8,128)(2,1)} %param.33) | copy-start | bytes 6291460
  0.6 39.8 %copy-start.7 = (f32[8,1]{0,1:T(1,128)S(1)}, f32[8,1]{0,1:T(1,128)}, u32[]{:S(2)}) copy-start(f32[8,1]{0,1:T(1,128)} %param.23) | copy-start | bytes 100
  0.7 38.2 %copy-start.2 = (bf16[8,1,128,128]{3,2,1,0:T(8,128)(2,1)S(1)}, bf16[8,1,128,128]{3,2,1,0:T(8,128)(2,1)}, u32[]{:S(2)}) copy-start(bf16[8,1,128,128]{3,2,1,0:T(8,128)(2,1)} %param.24) | copy-start | bytes 786436
  0.7 42.5 %copy-start.8 = (bf16[128,2048]{1,0:T(8,128)(2,1)S(1)}, bf16[128,2048]{1,0:T(8,128)(2,1)}, u32[]{:S(2)}) copy-start(bf16[128,2048]{1,0:T(8,128)(2,1)} %param.27) | copy-start | bytes 1572868
  1.5 74.8 %collective-permute-start.1 = (f32[8,128]{1,0:T(8,128)S(1)}, f32[8,128]{1,0:T(8,128)}, u32[]{:S(2)}, u32[]{:S(2)}) collective-permute-start(f32[8,128]{1,0:T(8,128)S(1)} %broadcast_in_dim.241), channel_id=1, source_target_pairs={{0,1},{1,0},{2,3},{3,2},{4,5},{5,4},{6,7},{7,6},{8,9},{9,8},{10,11... | collective-permute-start | bytes 12296 | tf_op jit(solution)/shard_map/ppermute | solution.py:13
  4.8 73.2 %collective-permute-start.2 = (f32[8,128]{1,0:T(8,128)S(1)}, f32[8,128]{1,0:T(8,128)}, u32[]{:S(2)}, u32[]{:S(2)}) collective-permute-start(f32[8,128]{1,0:T(8,128)S(1)} %broadcast_in_dim.241), channel_id=1, source_target_pairs={{0,129},{1,128},{128,1},{129,0},{2,131},{3,130},{130,3},{131,2},{4... | collective-permute-start | bytes 12296 | tf_op jit(solution)/shard_map/ppermute | solution.py:13
  13.6 14.1 %collective-permute-start = (f32[8,128]{1,0:T(8,128)S(1)}, f32[8,128]{1,0:T(8,128)S(1)}, u32[]{:S(2)}, u32[]{:S(2)}) collective-permute-start(f32[8,128]{1,0:T(8,128)S(1)} %maximum_maximum_fusion), channel_id=1, source_target_pairs={{0,128},{128,0},{1,129},{129,1},{2,130},{130,2},{3,131},{131,3},{4... | collective-permute-start | bytes 12296 | tf_op jit(solution)/shard_map/ppermute | solution.py:13
  20.1 81.7 %collective-permute-start.3 = (bf16[128,128]{1,0:T(8,128)(2,1)}, bf16[128,128]{1,0:T(8,128)(2,1)}, u32[]{:S(2)}, u32[]{:S(2)}) collective-permute-start(bf16[128,128]{1,0:T(8,128)(2,1)} %convolution_convert_fusion.1), channel_id=1, source_target_pairs={{0,128},{128,0},{1,129},{129,1},{2,130},{130,2},{3,131},{131,3},{4... | collective-permute-start | bytes 98312 | tf_op jit(solution)/shard_map/ppermute | solution.py:13
  25.3 18.9 %copy-start.4 = (pred[8]{0:T(512)(128)(4,1)}, pred[8]{0:T(512)(128)(4,1)S(1)}, u32[]{:S(2)}) copy-start(pred[8]{0:T(512)(128)(4,1)S(1)} %iota_compare_fusion.13) | copy-start | bytes 28
  44.2 17.9 %all-to-all-start = ((f32[64,2,128]{2,1,0:T(2,128)}), f32[64,2,128]{2,1,0:T(2,128)S(1)}, u32[]{:S(2)}, u32[]{:S(2)}) async-start(f32[64,2,128]{2,1,0:T(2,128)} %copy.32), calls=%async_computation | async-start | bytes 131072 | tf_op jit(solution)/shard_map/all_to_all | solution.py:109
  62.9 20.5 %all-to-all-start.1 = ((bf16[256,2,128]{2,1,0:T(2,128)(2,1)}), bf16[256,2,128]{2,1,0:T(2,128)(2,1)S(1)}, u32[]{:S(2)}, u32[]{:S(2)}) async-start(bf16[256,2,128]{2,1,0:T(2,128)(2,1)} %broadcast_in_dim.259), calls=%async_computation.1 | async-start | bytes 262144 | tf_op jit(solution)/shard_map/all_to_all | solution.py:113
  70.4 13.9 %copy-start.1 = (bf16[2048,128]{1,0:T(8,128)(2,1)S(1)}, bf16[2048,128]{1,0:T(8,128)(2,1)}, u32[]{:S(2)}) copy-start(bf16[2048,128]{1,0:T(8,128)(2,1)} %param.30) | copy-start | bytes 1572868
  85.2 16.6 %copy-start.3 = (bf16[8,3,128]{2,0,1:T(8,128)(2,1)S(1)}, bf16[8,3,128]{2,0,1:T(8,128)(2,1)}, u32[]{:S(2)}) copy-start(bf16[8,3,128]{2,0,1:T(8,128)(2,1)} %param.22) | copy-start | bytes 18436
  85.3 16.6 %copy-start.5 = (pred[8]{0:T(512)(128)(4,1)S(1)}, pred[8]{0:T(512)(128)(4,1)}, u32[]{:S(2)}) copy-start(pred[8]{0:T(512)(128)(4,1)} %copy-done.4) | copy-start | bytes 28
  85.3 16.6 %copy-start.6 = (f32[8]{0:T(128)S(1)}, f32[8]{0:T(128)}, u32[]{:S(2)}) copy-start(f32[8]{0:T(128)} %get-tuple-element.16) | copy-start | bytes 100
  91.0 23.4 %all-to-all-start.2 = ((f32[256,1,128]{2,1,0:T(1,128)}), f32[256,1,128]{2,1,0:T(1,128)S(1)}, u32[]{:S(2)}, u32[]{:S(2)}) async-start(f32[256,1,128]{2,1,0:T(1,128)} %bitcast.45), calls=%async_computation.2 | async-start | bytes 262144 | tf_op jit(solution)/shard_map/all_to_all | solution.py:162

commit v2 on v1

v2 whole, which is shorter than its diff:
```python
import jax
import jax.numpy as jnp
from jax import lax
from jax.experimental import pallas as pl
from jax.experimental.pallas import tpu as pltpu
from jax.sharding import Mesh, PartitionSpec as P

GRID = ("y", "x", "z")
BLOCKS = ("s", "t")
F32 = jnp.float32
BF16 = jnp.bfloat16
EXACT = lax.Precision.HIGHEST
SCALE = 128 ** (-0.5)

ANY = pl.BlockSpec(memory_space=pl.ANY)
HBM = pl.BlockSpec(memory_space=pl.ANY)
VMEM = pl.BlockSpec(memory_space=pltpu.VMEM)
SMEM = pl.BlockSpec(memory_space=pltpu.SMEM)


def params(mib):
    return pltpu.CompilerParams(vmem_limit_bytes=int(mib * 1024 * 1024))


def stay(*arrays):
    return [pltpu.with_memory_space_constraint(a, pltpu.HBM) for a in arrays]


def swap(shard, axis, flip):
    return lax.ppermute(shard, axis, [(i, i ^ flip) for i in range(lax.axis_size(axis))])


def iota(shape, axis):
    return lax.broadcasted_iota(jnp.int32, shape, axis)


def norm_rows(values, gain_row):
    return values * lax.rsqrt(jnp.mean(values * values, axis=-1, keepdims=True) + 1e-06) * gain_row


def dot(a, b, precision=None):
    return jnp.dot(a, b, preferred_element_type=F32, precision=precision)


def dot_t(a, b):
    return lax.dot_general(a, b, (((1,), (1,)), ((), ())), preferred_element_type=F32)


def own_block():
    return lax.axis_index("s") * 2 + lax.axis_index("t")


def message_kernel(
    owner_ref, gate_hbm, qkv_hbm, resid_hbm, out_ref, gate_ref, qkv_ref, resid_ref, sems
):
    tile = lax.axis_index("y") * 4 + lax.axis_index("x")
    columns = pl.ds(pl.multiple_of(tile * 128, 128), 128)
    copies = [
        pltpu.make_async_copy(qkv_hbm, qkv_ref, sems.at[0]),
        pltpu.make_async_copy(resid_hbm.at[:, columns], resid_ref, sems.at[1]),
        pltpu.make_async_copy(gate_hbm, gate_ref, sems.at[2]),
    ]
    for copy in copies:
        copy.start()
    for copy in copies:
        copy.wait()
    owner = owner_ref[0]
    taken = iota((8, 128), 0) == owner
    out_ref[5:8, :] = jnp.full((3, 128), owner.astype(F32), F32)
    for part in range(3):
        rows = qkv_ref[part].astype(F32)
        out_ref[part : part + 1, :] = jnp.sum(jnp.where(taken, rows, 0.0), axis=0, keepdims=True)
    out_ref[3:4, :] = jnp.full((1, 128), gate_ref[owner], F32)
    piece = resid_ref[...].astype(F32)
    out_ref[4:5, :] = jnp.sum(jnp.where(taken, piece, 0.0), axis=0, keepdims=True)


def own_rows_kernel(
    length_ref, live_hbm, gate_hbm, decay_hbm, qkv_hbm, gain_hbm, kv_hbm, cache_hbm, state_hbm,
    head_ref, fresh_ref, live_ref, gate_ref, decay_ref, qkv_ref, gain_ref, kv_ref, cache_ref, state_ref,
    small_sem, kv_sem, cache_sem, state_sem,
):
    small = [
        (decay_hbm, decay_ref), (qkv_hbm, qkv_ref), (live_hbm, live_ref),
        (gate_hbm, gate_ref), (gain_hbm, gain_ref),
    ]
    small_copies = [pltpu.make_async_copy(a, b, small_sem.at[i]) for i, (a, b) in enumerate(small)]
    kv_copies = [pltpu.make_async_copy(kv_hbm.at[i], kv_ref.at[i], kv_sem.at[i]) for i in range(2)]
    state_copy = pltpu.make_async_copy(state_hbm, state_ref, state_sem)
    cache_copies = [
        pltpu.make_async_copy(cache_hbm.at[r], cache_ref.at[r], cache_sem.at[r]) for r in range(8)
    ]
    for copy in small_copies + kv_copies + cache_copies + [state_copy]:
        copy.start()

    for copy in small_copies:
        copy.wait()
    length = length_ref[0]
    places = iota((16, 128), 0) * 128 + iota((16, 128), 1)
    kept = jnp.where(places < length, decay_ref[...], 0.0)
    later = (iota((128, 128), 0) > iota((128, 128), 1)).astype(F32)
    later_rows = (iota((16, 16), 1) > iota((16, 16), 0)).astype(F32)
    totals = jnp.broadcast_to(jnp.sum(kept, axis=1, keepdims=True), (16, 128))
    suffix = dot(kept, later, EXACT) + dot(later_rows, totals, EXACT)
    weights = jnp.where(places < length, jnp.exp(suffix), 0.0)

    for copy in kv_copies:
        copy.wait()
    fresh = jnp.zeros((128, 128), F32)
    for i in range(16):
        rows = pl.ds(i * 128, 128)
        turned = kv_ref[0, rows, :].astype(F32).T
        scaled = (turned * weights[i : i + 1, :]).astype(BF16)
        fresh += dot(scaled, kv_ref[1, rows, :])
    fresh_ref[...] = fresh.astype(BF16)

    queries = qkv_ref[0]
    q32, k32, v32 = queries.astype(F32), qkv_ref[1].astype(F32), qkv_ref[2].astype(F32)
    self_raw = jnp.sum(q32 * k32, axis=1, keepdims=True)
    self_score = self_raw * SCALE
    scores = jnp.zeros((8, 1024), F32)
    live = jnp.zeros((8, 1024), jnp.int32)
    gate = jnp.zeros((8, 128), F32)
    for r in range(8):
        cache_copies[r].wait()
        scores = jnp.where(iota((8, 1024), 0) == r, dot_t(queries, cache_ref[r, 0]), scores)
        live = jnp.where(iota((8, 1024), 0) == r, live_ref[r], live)
        gate = jnp.where(iota((8, 128), 0) == r, gate_ref[r], gate)
    scores = scores * SCALE
    alive = iota((8, 1024), 1) >= 1024 - live
    peak = jnp.max(jnp.where(alive, scores, -jnp.inf), axis=1, keepdims=True)
    peak = jnp.maximum(peak, self_score)
    prob = jnp.where(alive, jnp.exp(scores - peak), 0.0).astype(BF16)
    self_prob = jnp.exp(self_score - peak).astype(BF16).astype(F32)
    below = jnp.sum(prob.astype(F32), axis=1, keepdims=True) + self_prob
    above = jnp.zeros((8, 128), F32)
    linear = jnp.zeros((8, 128), F32)
    state_copy.wait()
    for r in range(8):
        mine = iota((8, 128), 0) == r
        above = jnp.where(mine, dot(prob, cache_ref[r, 1]), above)
        linear = jnp.where(mine, dot(queries, state_ref[r]), linear)
    window_out = (above + self_prob * v32) / below
    linear_out = jnp.exp(gate) * linear + self_raw * v32
    head_ref[...] = norm_rows(linear_out, gain_ref[0:1, :]) + norm_rows(window_out, gain_ref[1:2, :])


def guest_kernel(
    owner_ref, length_ref, got_ref, head_ref, fresh_ref, gain_hbm, kv_hbm, weight_hbm,
    out_ref, pack_ref, gain_ref, kv_ref, weight_ref, small_sem, kv_sem, weight_sem,
):
    small_copies = [pltpu.make_async_copy(gain_hbm, gain_ref, small_sem)]
    kv_copies = [pltpu.make_async_copy(kv_hbm.at[i], kv_ref.at[i], kv_sem.at[i]) for i in range(2)]
    weight_copy = pltpu.make_async_copy(weight_hbm, weight_ref, weight_sem)
    for copy in small_copies + kv_copies + [weight_copy]:
        copy.start()
    for copy in small_copies:
        copy.wait()
    length = length_ref[0]
    mine = jnp.full((8, 128), owner_ref[0].astype(F32), F32)
    pack_ref[...] = jnp.where(iota((8, 128), 0) == 0, mine, got_ref[5:6, :])
    q32 = jnp.broadcast_to(got_ref[0:1, :], (8, 128))
    k32 = jnp.broadcast_to(got_ref[1:2, :], (8, 128))
    v32 = jnp.broadcast_to(got_ref[2:3, :], (8, 128))
    query = q32.astype(BF16)
    self_raw = jnp.sum(q32 * k32, axis=1, keepdims=True)
    self_score = self_raw * SCALE
    linear_out = jnp.exp(got_ref[3:4, :]) * dot(query, fresh_ref[...]) + self_raw * v32
    kv_copies[0].wait()
    scores = dot_t(query, kv_ref[0]) * SCALE
    places = iota((8, 2048), 1)
    alive = (places < length) & (places >= length - 1024)
    peak = jnp.max(jnp.where(alive, scores, -jnp.inf), axis=1, keepdims=True)
    peak = jnp.maximum(peak, self_score)
    prob = jnp.where(alive, jnp.exp(scores - peak), 0.0).astype(BF16)
    self_prob = jnp.exp(self_score - peak).astype(BF16).astype(F32)
    below = jnp.sum(prob.astype(F32), axis=1, keepdims=True) + self_prob
    kv_copies[1].wait()
    window_out = (dot(prob, kv_ref[1]) + self_prob * v32) / below
    head = norm_rows(linear_out, gain_ref[0:1, :]) + norm_rows(window_out, gain_ref[1:2, :])
    head = jnp.where(iota((8, 128), 0) == owner_ref[0], head, head_ref[...]).astype(BF16)
    weight_copy.wait()
    for c in range(16):
        out_ref[c] = dot(head, weight_ref[:, c * 128 : (c + 1) * 128])


def named_by(routes_ref):
    lanes = iota((32, 128), 1)
    member = jnp.zeros((32, 128), F32)
    for k in range(8):
        member = jnp.where(routes_ref[:, k : k + 1] == lanes, 1.0, member)
    return member


def own_expert():
    return lax.axis_index("s") * 64 + lax.axis_index("y") * 16 + lax.axis_index("x") * 4 + lax.axis_index("z")


def prepare_kernel(
    pack_ref, beside_ref, routes_ref, turned_ref, order_ref, chooser_ref, member_ref, spread_ref, use_ref
):
    block = own_block()
    owner, partner = pack_ref[0, 0], pack_ref[1, 0]
    beside, across = beside_ref[0, 0], beside_ref[1, 0]
    ids = iota((32, 32), 0)
    their_block, their_row = ids // 8, (ids % 8).astype(F32)

    def by_block(mine, other, side, cross):
        return jnp.where(
            their_block == block, mine,
            jnp.where(their_block == (block ^ 2), other, jnp.where(their_block == (block ^ 1), side, cross)),
        )

    held = by_block(owner, partner, beside, across)
    held_partner = by_block(partner, owner, across, beside)
    source = jnp.where(
        their_row == held, ((their_block ^ 2) * 8).astype(F32) + held_partner, ids.astype(F32)
    )
    order = (source == iota((32, 32), 1).astype(F32)).astype(F32)
    order_ref[...] = order

    expert = own_expert()
    names_own = jnp.max((turned_ref[...] == expert).astype(F32), axis=0, keepdims=True)
    names_own = jnp.broadcast_to(names_own, (8, 32))
    upper = (iota((32, 32), 0) < iota((32, 32), 1)).astype(F32)
    rank = dot(names_own, upper)
    slots = (iota((8, 32), 0) % 4).astype(F32)
    chooser_ref[...] = jnp.where(names_own > 0, (rank == slots).astype(F32), 0.0)

    member = named_by(routes_ref)
    member_ref[...] = member
    spread_ref[...] = (iota((128, 1024), 1) // 8 == iota((128, 1024), 0)).astype(BF16)

    lower = (iota((32, 32), 1) < iota((32, 32), 0)).astype(F32)
    slot = jnp.where(member > 0, dot(lower, member), -1.0)
    first = (iota((8, 32), 1) == iota((8, 32), 0) + block * 8).astype(F32)
    slot = dot(first, slot)
    src = iota((128, 256), 1)
    sender = src // 128 * 64 + src % 16 * 4 + src // 16 % 4
    slot = dot(slot, (sender == iota((128, 256), 0)).astype(F32))
    for k in range(4):
        use_ref[k * 8 : (k + 1) * 8, :] = (slot == float(k)).astype(F32)


NEAR = 1024
CHUNK = 1024


def fetch_kernel(after_ref, router_hbm, in_hbm, down_hbm, router_ref, in_ref, down_ref, sems):
    copies = [
        pltpu.make_async_copy(router_hbm, router_ref, sems.at[0]),
        pltpu.make_async_copy(in_hbm.at[pl.ds(0, NEAR)], in_ref, sems.at[1]),
        pltpu.make_async_copy(down_hbm, down_ref, sems.at[2]),
    ]
    for copy in copies:
        copy.start()
    for copy in copies:
        copy.wait()


def expert_kernel(
    order_ref, chooser_ref, member_ref, spread_ref, gain_ref, hidden_ref, router_ref, near_ref, down_ref, in_hbm,
    out_ref, own_ref, in_ref, turn_ref, in_sem,
):
    in_copies = [
        pltpu.make_async_copy(
            in_hbm.at[pl.ds(NEAR + i * CHUNK, CHUNK)], in_ref.at[pl.ds(i * CHUNK, CHUNK)], in_sem.at[i]
        )
        for i in range((16384 - NEAR) // CHUNK)
    ]
    for copy in in_copies:
        copy.start()
    block = own_block()
    expert = own_expert()
    order, chooser, member = order_ref[...], chooser_ref[...], member_ref[...]

    scales = []
    for b in range(4):
        total = jnp.zeros((8, 128), F32)
        for c in range(16):
            x = hidden_ref[b * 16 + c].astype(F32)
            total += x * x
        scales.append(lax.rsqrt(jnp.sum(total, axis=1, keepdims=True) * (1.0 / 2048) + 1e-06))
    tiles = []
    for c in range(16):
        gain = gain_ref[:, c * 128 : (c + 1) * 128]
        parts = [hidden_ref[b * 16 + c].astype(F32) * scales[b] * gain for b in range(4)]
        tiles.append(jnp.concatenate(parts, axis=0).astype(BF16))
    normed = jnp.concatenate(tiles, axis=1)

    choose_gathered = dot(chooser, order)
    rows_in = dot(choose_gathered.astype(BF16), normed)

    logits = dot(order, dot(normed, router_ref[...]), EXACT)
    lanes = iota((32, 128), 1)
    chosen = member / (1.0 + jnp.exp(-logits))
    chosen = jnp.where(member > 0, chosen, 0.0)
    share = jnp.sum(jnp.where(lanes == expert, chosen, 0.0), axis=1, keepdims=True)
    share = share / jnp.sum(chosen, axis=1, keepdims=True)
    gates = dot(chooser, jnp.broadcast_to(share, (32, 128)), EXACT)

    stacked = jnp.concatenate([rows_in[:, c * 128 : (c + 1) * 128] for c in range(16)], axis=0)
    repeated = dot(stacked.astype(BF16), spread_ref[...])
    kind = iota((8, 1024), 1) % 8 - iota((8, 1024), 0) // 4
    pre = jnp.zeros((32, 128), F32)
    for c in range(16):
        piece = repeated[c * 8 : (c + 1) * 8, :]
        left = jnp.concatenate([jnp.where(kind == 2 * p, piece, 0.0) for p in range(4)], axis=0)
        start = c * 1024 - NEAR
        if start >= 0 and start % CHUNK == 0:
            in_copies[start // CHUNK].wait()
        right = near_ref[c * 1024 : (c + 1) * 1024, :] if start < 0 else in_ref[start : start + 1024, :]
        pre += dot(left.astype(BF16), right)
    acts = []
    for p in range(4):
        both = pre[p * 8 : (p + 1) * 8, :]
        acts.append(both / (1.0 + jnp.exp(-both)) * pltpu.roll(both, 4, 0))
    act = jnp.concatenate(acts, axis=1).astype(BF16)
    for c in range(16):
        turn_ref[c] = dot(act, down_ref[:, c * 128 : (c + 1) * 128]) * gates

    lane_block = iota((16, 128), 1) // 32
    by_slot = [turn_ref[:, k, :] for k in range(4)]
    for q in range(4):
        piece = jnp.zeros((16, 128), F32)
        for k in range(4):
            shift = (k - q) * 32 % 128
            moved = by_slot[k] if shift == 0 else pltpu.roll(by_slot[k], shift, 1)
            piece = jnp.where(lane_block == k, moved, piece)
        for b in range(4):
            out_ref[b * 64 + q * 16 : b * 64 + (q + 1) * 16, :] = piece

    tile = lax.axis_index("y") * 4 + lax.axis_index("x")
    raw = jnp.concatenate([hidden_ref[b * 16 + tile].astype(F32) for b in range(4)], axis=0)
    first = (iota((8, 32), 1) == iota((8, 32), 0) + block * 8).astype(F32)
    mine = dot(dot(first, order).astype(BF16), raw.astype(BF16))
    deep = lax.axis_index("z")
    own = mine
    for q in range(1, 4):
        own = jnp.where(deep == q, pltpu.roll(mine, 128 - q * 32, 1), own)
    own_ref[...] = own


def finish_kernel(use_ref, back_ref, own_ref, out_ref):
    back = back_ref[...]
    high = back.astype(BF16)
    low = (back - high.astype(F32)).astype(BF16)
    use = use_ref[...].astype(BF16)
    total = dot(use, high) + dot(use, low)
    out = own_ref[:, 0:32]
    for k in range(4):
        out += total[k * 8 : (k + 1) * 8, k * 32 : (k + 1) * 32]
    out_ref[...] = out.astype(BF16)


def on_device(
    pre_kv, pre_gate, pre_len, owners, win_len, dec_qkv, dec_gate, state_cache, win_cache,
    head_gain, out_weight, resid, moe_gain, router, routes, w_in, w_down,
):
    lane_tile = lax.axis_index("y") * 4 + lax.axis_index("x")
    deep = lax.axis_index("z")
    qkv = dec_qkv.transpose(1, 0, 2)
    gates = dec_gate.reshape(8)

    message = pl.pallas_call(
        message_kernel,
        out_shape=jax.ShapeDtypeStruct((8, 128), F32),
        in_specs=[SMEM] + [HBM] * 3,
        out_specs=VMEM,
        scratch_shapes=[
            pltpu.SMEM((8,), F32),
            pltpu.VMEM((3, 8, 128), BF16),
            pltpu.VMEM((8, 128), BF16),
            pltpu.SemaphoreType.DMA((3,)),
        ],
        compiler_params=params(2),
        name="message",
    )(owners, *stay(gates, qkv, resid))
    got = swap(message, "s", 1)

    own_heads, fresh_state = pl.pallas_call(
        own_rows_kernel,
        out_shape=(jax.ShapeDtypeStruct((8, 128), F32), jax.ShapeDtypeStruct((128, 128), BF16)),
        in_specs=[SMEM] + [HBM] * 8,
        out_specs=(VMEM, VMEM),
        scratch_shapes=[
            pltpu.SMEM((8,), jnp.int32),
            pltpu.SMEM((8,), F32),
            pltpu.VMEM((16, 128), F32),
            pltpu.VMEM((3, 8, 128), BF16),
            pltpu.VMEM((2, 128), F32),
            pltpu.VMEM((2, 2048, 128), BF16),
            pltpu.VMEM((8, 2, 1024, 128), BF16),
            pltpu.VMEM((8, 128, 128), BF16),
            pltpu.SemaphoreType.DMA((5,)),
            pltpu.SemaphoreType.DMA((2,)),
            pltpu.SemaphoreType.DMA((8,)),
            pltpu.SemaphoreType.DMA,
        ],
        compiler_params=params(14),
        name="own_rows",
    )(
        pre_len,
        *stay(
            win_len, gates, pre_gate.reshape(16, 128), qkv, head_gain,
            pre_kv[0], win_cache, state_cache[:, 0],
        )
    )
    got_state = swap(fresh_state, "s", 1)

    partial, pack = pl.pallas_call(
        guest_kernel,
        out_shape=(jax.ShapeDtypeStruct((16, 8, 128), F32), jax.ShapeDtypeStruct((8, 128), F32)),
        in_specs=[SMEM] * 2 + [VMEM] * 3 + [HBM] * 3,
        out_specs=(VMEM, VMEM),
        scratch_shapes=[
            pltpu.VMEM((2, 128), F32),
            pltpu.VMEM((2, 2048, 128), BF16),
            pltpu.VMEM((128, 2048), BF16),
            pltpu.SemaphoreType.DMA,
            pltpu.SemaphoreType.DMA((2,)),
            pltpu.SemaphoreType.DMA,
        ],
        compiler_params=params(8),
        name="guest",
    )(owners, pre_len, got, own_heads, fresh_state, *stay(head_gain, pre_kv[0], out_weight))
    beside = swap(pack, "t", 1)

    expert_in = w_in[0].reshape(2048, 2, 4, 128).transpose(0, 2, 1, 3).reshape(16384, 128)
    router_near, in_near, down_near = pl.pallas_call(
        fetch_kernel,
        out_shape=(
            pltpu.VMEM((2048, 128), BF16),
            pltpu.VMEM((NEAR, 128), BF16),
            pltpu.VMEM((512, 2048), BF16),
        ),
        in_specs=[ANY] + [HBM] * 3,
        out_specs=(VMEM,) * 3,
        scratch_shapes=[pltpu.SemaphoreType.DMA((3,))],
        compiler_params=params(2),
        name="fetch",
    )(pack, *stay(router, expert_in, w_down[0]))

    attended = lax.all_to_all(partial.reshape(64, 2, 128), GRID, 0, 0, tiled=True).sum(0)
    taken = jnp.arange(8) == owners[0]
    own_resid = lax.dynamic_slice(resid, (0, lane_tile * 128), (8, 128)).astype(F32)
    own_resid = jnp.where(taken[:, None], got[4], own_resid)
    own_resid = lax.dynamic_slice_in_dim(own_resid, deep * 2, 2, 0)
    hidden = (own_resid + attended).astype(BF16)
    hidden, router_near, in_near, down_near, beside = lax.optimization_barrier(
        (hidden, router_near, in_near, down_near, beside)
    )
    every = lax.all_to_all(
        jnp.broadcast_to(hidden[None], (256, 2, 128)), ("s", "t", "y", "x", "z"), 0, 0, tiled=True
    )

    order, chooser, member, spread, use = pl.pallas_call(
        prepare_kernel,
        out_shape=(
            jax.ShapeDtypeStruct((32, 32), F32),
            jax.ShapeDtypeStruct((8, 32), F32),
            jax.ShapeDtypeStruct((32, 128), F32),
            jax.ShapeDtypeStruct((128, 1024), BF16),
            jax.ShapeDtypeStruct((32, 256), F32),
        ),
        in_specs=[VMEM] * 4,
        out_specs=(VMEM,) * 5,
        compiler_params=params(4),
        name="prepare",
    )(pack, beside, routes, routes.T)
    term, own = pl.pallas_call(
        expert_kernel,
        out_shape=(jax.ShapeDtypeStruct((256, 128), F32), jax.ShapeDtypeStruct((8, 128), F32)),
        in_specs=[VMEM] * 9 + [HBM],
        out_specs=(VMEM, VMEM),
        scratch_shapes=[
            pltpu.VMEM((16384 - NEAR, 128), BF16),
            pltpu.VMEM((16, 8, 128), F32),
            pltpu.SemaphoreType.DMA(((16384 - NEAR) // CHUNK,)),
        ],
        compiler_params=params(12),
        name="experts",
    )(
        order, chooser, member, spread, moe_gain.reshape(1, 2048), every.reshape(64, 8, 128),
        router_near, in_near, down_near, *stay(expert_in),
    )
    back = lax.all_to_all(term.reshape(256, 1, 128), ("s", "t", "z", "y", "x"), 0, 0, tiled=True)
    layer_out = pl.pallas_call(
        finish_kernel,
        out_shape=jax.ShapeDtypeStruct((8, 32), BF16),
        in_specs=[VMEM] * 3,
        out_specs=VMEM,
        compiler_params=params(2),
        name="finish",
    )(use, back.reshape(256, 128), own)

    previous = jnp.where(taken[:, None, None], got_state[None], state_cache[:, 0]).astype(F32)
    own_k, own_v = dec_qkv[:, 1].astype(F32), dec_qkv[:, 2].astype(F32)
    states = jnp.exp(dec_gate)[:, :, None] * previous + own_k[:, :, None] * own_v[:, None, :]
    return layer_out, states[:, None]


def solution(mesh):
    fine = Mesh(mesh.devices.reshape(2, 4, 4, 4, 2), ("s", "y", "x", "z", "t"))
    placed = (
        P(BLOCKS, None, None, GRID),
        P(BLOCKS, GRID, None),
        P(BLOCKS),
        P(BLOCKS),
        P(BLOCKS),
        P(BLOCKS, None, GRID),
        P(BLOCKS, GRID),
        P(BLOCKS, GRID, None, None),
        P(BLOCKS, None, None, GRID),
        P(None, GRID),
        P(GRID, None),
        P(BLOCKS, None),
        P(),
        P(),
        P(),
        P(("s",) + GRID, None, None, "t"),
        P(("s",) + GRID, "t", None),
    )
    return jax.shard_map(
        on_device,
        mesh=fine,
        in_specs=placed,
        out_specs=(P(BLOCKS, GRID), P(BLOCKS, GRID, None, None)),
        check_vma=False,
    )
```

time: 119 us -> 82.7 us (0.69)
  matrix products: 18 us -> 0 us
  Pallas kernels: 0 us -> 17 us
  local copies, waits for them, and re-layouts: 15.4 us -> 0.83 us
  other arithmetic: 15.9 us -> 2.84 us
  between operations: 5.46 us -> 2.08 us
  starting transfers between devices: 41.2 us -> 37.9 us
    dot_general x13 -> x0, matrix products: 18 us -> none  [the longest x2 3.51 us: window_part(): jnp.einsum('rd,rwd->rw', queries, keys, preferred_element_type=F32) * scale]
    pallas_call x0 -> x7, Pallas kernels: none -> 17 us  [the longest x1 5.24 us: on_device(): pl.pallas_call(own_rows_kernel, out_shape=(jax.ShapeDtypeStruct((8, 128),...]
    unnamed x22 -> x9, local copies, waits for them, and re-layouts: 6.19 us -> 0.1 us
    all_to_all x2, starting transfers between devices: 19.9 us -> 14.9 us  [the longest x1 9.04 us: on_device(): lax.all_to_all(partial.reshape(64, 2, 128), GRID, 0, 0, tiled=True).sum(0)]
    reduce_sum x10 -> x1, other arithmetic: 4.41 us -> 0.08 us  [on_device(): lax.all_to_all(partial.reshape(64, 2, 128), GRID, 0, 0, tiled=True).sum(0)]
    all_to_all x2, waiting for transfers between devices: 18.7 us -> 15.5 us  [the longest x1 10.7 us: on_device(): lax.all_to_all(term.reshape(256, 1, 128), ('s', 't', 'z', 'y', 'x'), 0, 0...]
    all_to_all x1, waiting for transfers between devices: 3 us -> 6.04 us  [on_device(): lax.all_to_all(jnp.broadcast_to(hidden[None], (256, 2, 128)), ('s', 't',...]
    slice x5 -> x0, local copies, waits for them, and re-layouts: 2.97 us -> none  [the longest x1 1.19 us: on_device(): beside_owner = beside[0, 0].astype(jnp.int32)]
  transfers between devices with their start and end apart: 7 -> 6, of which waited for: 3 -> 3; matrix products, arithmetic and copies ran while one was open for 39% -> 4% of each run, Pallas kernels for 0% -> 15%
where the time goes in v2:
time: 82.7 us; the launch traced here: 82.3 us
  starting transfers between devices  37.9 us (46%)
  waiting for transfers between devices  21.6 us (26%)
  Pallas kernels  17 us (21%)
  other arithmetic  2.84 us (3%)
  between operations  2.08 us (3%)
  local copies, waits for them, and re-layouts  0.83 us (1%)
    ppermute x3, starting transfers between devices, swap(): lax.ppermute(shard, axis, [(i, i ^ flip) for i in range(lax.axis_size(axi...  15.6 us
    all_to_all x1, waiting for transfers between devices, on_device(): lax.all_to_all(term.reshape(256, 1, 128), ('s', 't', 'z', 'y', 'x'), 0, 0...  10.7 us
    all_to_all x1, starting transfers between devices, on_device(): lax.all_to_all(partial.reshape(64, 2, 128), GRID, 0, 0, tiled=True).sum(0)  9.04 us
    all_to_all x1, starting transfers between devices, on_device(): lax.all_to_all(jnp.broadcast_to(hidden[None], (256, 2, 128)), ('s', 't',...  7.39 us
    all_to_all x1, waiting for transfers between devices, on_device(): lax.all_to_all(jnp.broadcast_to(hidden[None], (256, 2, 128)), ('s', 't',...  6.04 us
    all_to_all x1, starting transfers between devices, on_device(): lax.all_to_all(term.reshape(256, 1, 128), ('s', 't', 'z', 'y', 'x'), 0, 0...  5.89 us
    pallas_call x1, Pallas kernels, on_device(): pl.pallas_call(own_rows_kernel, out_shape=(jax.ShapeDtypeStruct((8, 128),...  5.24 us
    pallas_call x1, Pallas kernels, on_device(): pl.pallas_call(expert_kernel, out_shape=(jax.ShapeDtypeStruct((256, 128),...  5.13 us
  transfers between devices with their start and end apart: 6, of which 3 were waited for; matrix products, arithmetic and copies ran while one was open for 4% of the time, Pallas kernels for 15%

profile of v2, /device:TPU:1, one launch (start us, length us, event | category | flops | bytes accessed | tf_op | source)
XLA Modules:
  0.0 82.3 jit_solution(11489428811323553049)
XLA Ops:
  1.3 0.8 %message.1 = f32[8,128]{1,0:T(8,128)S(1)} custom-call(s32[1]{0:T(128)} %copy.25.owner_ref, f32[8]{0:T(128)} %bitcast.44, bf16[3,8,128]{2,1,0:T(8,128)(2,1)} %bitcast.41, bf16[8,2048]{1,0:T(8,128)(2,1)} %resid_hbm.1), custom_call_target="tpu_custom_call" | custom-call | tf_op jit(solution)/shard_map/message/pallas_call | solution.py:365
  2.1 7.8 %collective-permute-start = (f32[8,128]{1,0:T(8,128)S(1)}, f32[8,128]{1,0:T(8,128)S(1)}, u32[]{:S(2)}, u32[]{:S(2)}) collective-permute-start(f32[8,128]{1,0:T(8,128)S(1)} %message.1), channel_id=1, source_target_pairs={{0,128},{128,0},{1,129},{129,1},{2,130},{130,2},{3,131},{131,3},{4... | collective-permute-start | bytes 12296 | tf_op jit(solution)/shard_map/ppermute | solution.py:30
  10.6 5.2 %own_rows.1 = (f32[8,128]{1,0:T(8,128)S(1)}, bf16[128,128]{1,0:T(8,128)(2,1)S(1)}) custom-call(s32[1]{0:T(128)S(6)} %copy.24.length_ref, s32[8]{0:T(128)} %live_hbm.1, f32[8]{0:T(128)} %bitcast.45, f32[16,128]{1,0:T(8,128)} %bitcast.43, bf16[3,8,128]{2,1,0:T(8,128)(2,1)} %bitcast.42, f32[2,128]{1,0:T(2,128)} %gain_hbm.3, bf16[2,2048,128]{2,1,0:T(8,128)(2,1)} %bitcast.37, ...), custom_call_target="tpu_custom_call" | custom-call | tf_op jit(solution)/shard_map/own_rows/pallas_call | solution.py:381
  15.9 0.0 collective-permute-done.got_ref
  15.9 0.0 copy-start
  15.9 0.0 copy-start.2
  15.9 0.0 copy-start.1
  15.9 2.7 %guest.1 = (f32[16,8,128]{2,1,0:T(8,128)}, f32[8,128]{1,0:T(8,128)S(1)}) custom-call(s32[1]{0:T(128)} %copy.25.owner_ref, s32[1]{0:T(128)S(6)} %copy.24.length_ref, f32[8,128]{1,0:T(8,128)S(1)} %collective-permute-done.got_ref, f32[8,128]{1,0:T(8,128)S(1)} %get-tuple-element.21.head_ref, bf16[128,128]{1,0:T(8,128)(2,1)S(1)} %get-tuple-element.22.fresh_ref, ...), custom_call_target="tpu_custom_call" | custom-call | tf_op jit(solution)/shard_map/guest/pallas_call | solution.py:411
  18.6 9.0 %all-to-all-start = ((f32[64,2,128]{2,1,0:T(2,128)}), f32[64,2,128]{2,1,0:T(2,128)S(1)}, u32[]{:S(2)}, u32[]{:S(2)}) async-start(f32[64,2,128]{2,1,0:T(2,128)} %bitcast.7), calls=%async_computation | async-start | bytes 131072 | tf_op jit(solution)/shard_map/all_to_all | solution.py:444
  27.6 1.3 %collective-permute-start.1 = (f32[8,128]{1,0:T(8,128)S(1)}, f32[8,128]{1,0:T(8,128)S(1)}, u32[]{:S(2)}, u32[]{:S(2)}) collective-permute-start(f32[8,128]{1,0:T(8,128)S(1)} %get-tuple-element.23.after_ref.pack_ref), channel_id=1, source_target_pairs={{0,1},{1,0},{2,3},{3,2},{4,5},{5,4},{6,7},{7,6},{8,9},{9,8},{10,11... | collective-permute-start | bytes 12296 | tf_op jit(solution)/shard_map/ppermute | solution.py:30
  29.0 1.9 %fetch.1 = (bf16[2048,128]{1,0:T(8,128)(2,1)S(1)}, bf16[1024,128]{1,0:T(8,128)(2,1)S(1)}, bf16[512,2048]{1,0:T(8,128)(2,1)S(1)}) custom-call(f32[8,128]{1,0:T(8,128)S(1)} %get-tuple-element.23.after_ref.pack_ref, bf16[2048,128]{1,0:T(8,128)(2,1)} %router_hbm.1, bf16[16384,128]{1,0:T(8,128)(2,1)} %bitcast.35, bf16[512,2048]{1,0:T(8,128)(2,1)} %bitcast.39), custom_call_target="tpu_custom_call" | custom-call | tf_op jit(solution)/shard_map/fetch/pallas_call | solution.py:430
  30.8 0.0 copy-start.3
  30.9 0.8 convert_select_fusion
  31.6 4.9 %all-to-all-done = f32[64,2,128]{2,1,0:T(2,128)S(1)} async-done(((f32[64,2,128]{2,1,0:T(2,128)}), f32[64,2,128]{2,1,0:T(2,128)S(1)}, u32[]{:S(2)}, u32[]{:S(2)}) %all-to-all-start) | async-done | bytes 65568 | tf_op jit(solution)/shard_map/all_to_all | solution.py:444
  36.5 0.1 reduce_sum.9
  36.6 0.0 collective-permute-done.1.beside_ref
  36.6 0.7 broadcast_in_dim.43
  37.3 7.4 %all-to-all-start.1 = ((bf16[256,2,128]{2,1,0:T(2,128)(2,1)}), bf16[256,2,128]{2,1,0:T(2,128)(2,1)S(1)}, u32[]{:S(2)}, u32[]{:S(2)}) async-start(bf16[256,2,128]{2,1,0:T(2,128)(2,1)} %broadcast_in_dim.43), calls=%async_computation.1 | async-start | bytes 262144 | tf_op jit(solution)/shard_map/all_to_all | solution.py:453
  44.7 6.4 %collective-permute-start.2 = (bf16[128,128]{1,0:T(8,128)(2,1)S(1)}, bf16[128,128]{1,0:T(8,128)(2,1)S(1)}, u32[]{:S(2)}, u32[]{:S(2)}) collective-permute-start(bf16[128,128]{1,0:T(8,128)(2,1)S(1)} %get-tuple-element.22.fresh_ref), channel_id=1, source_target_pairs={{0,128},{128,0},{1,129},{129,1},{2,130},{130,2},{3,131},{131,3},{4... | collective-permute-start | bytes 98312 | tf_op jit(solution)/shard_map/ppermute | solution.py:30
  51.2 0.0 copy-done
  51.2 0.1 copy.22.routes_ref
  51.2 0.0 copy-done.2
  51.3 0.5 prepare.1
  51.7 6.0 %all-to-all-done.1 = bf16[256,2,128]{2,1,0:T(2,128)(2,1)S(1)} async-done(((bf16[256,2,128]{2,1,0:T(2,128)(2,1)}), bf16[256,2,128]{2,1,0:T(2,128)(2,1)S(1)}, u32[]{:S(2)}, u32[]{:S(2)}) %all-to-all-start.1) | async-done | bytes 131104 | tf_op jit(solution)/shard_map/all_to_all | solution.py:453
  57.8 0.0 copy-done.1
  57.8 5.1 %experts.1 = (f32[256,128]{1,0:T(8,128)}, f32[8,128]{1,0:T(8,128)S(1)}) custom-call(f32[32,32]{1,0:T(8,128)S(1)} %get-tuple-element.30.order_ref, f32[8,32]{1,0:T(8,128)S(1)} %get-tuple-element.31.chooser_ref, f32[32,128]{1,0:T(8,128)S(1)} %get-tuple-element.32.member_ref, bf16[128,1024]{1,0:T(8,128)(2,1)S(1)} %get-tuple-element.33.spread_ref, ...), custom_call_target="tpu_custom_call" | custom-call | tf_op jit(solution)/shard_map/experts/pallas_call | solution.py:471
  62.9 5.9 %all-to-all-start.2 = ((f32[256,1,128]{2,1,0:T(1,128)}), f32[256,1,128]{2,1,0:T(1,128)S(1)}, u32[]{:S(2)}, u32[]{:S(2)}) async-start(f32[256,1,128]{2,1,0:T(1,128)} %bitcast.18), calls=%async_computation.2 | async-start | bytes 262144 | tf_op jit(solution)/shard_map/all_to_all | solution.py:487
  68.8 0.0 copy-done.3
  68.8 0.0 collective-permute-done.2
  68.8 2.0 %multiply_add_fusion = f32[8,1,128,128]{3,2,1,0:T(8,128)} fusion(f32[8,128]{1,0:T(8,128)S(1)} %get-tuple-element.41, f32[8,128]{1,0:T(8,128)S(1)} %get-tuple-element.40, bf16[8,1,128,128]{3,2,1,0:T(8,128)(2,1)} %param.24, f32[8]{0:T(128)S(1)} %exponential_bitcast_fusion, pred[8]{0:T(512)(128)(4,1)S(1)} %iota_compare_fusion, ...), kind=kLoop, calls=%fused_computation | loop fusion | flops 655360 | bytes 827432 | tf_op jit(solution)/shard_map/add | solution.py:499
  70.8 10.7 %all-to-all-done.2 = f32[256,1,128]{2,1,0:T(1,128)S(1)} async-done(((f32[256,1,128]{2,1,0:T(1,128)}), f32[256,1,128]{2,1,0:T(1,128)S(1)}, u32[]{:S(2)}, u32[]{:S(2)}) %all-to-all-start.2) | async-done | bytes 131104 | tf_op jit(solution)/shard_map/all_to_all | solution.py:487
  81.5 0.8 finish.1
  (5 shorter events, 0.0 us)
Async XLA Ops:
  2.1 13.7 %collective-permute-start = (f32[8,128]{1,0:T(8,128)S(1)}, f32[8,128]{1,0:T(8,128)S(1)}, u32[]{:S(2)}, u32[]{:S(2)}) collective-permute-start(f32[8,128]{1,0:T(8,128)S(1)} %message.1), channel_id=1, source_target_pairs={{0,128},{128,0},{1,129},{129,1},{2,130},{130,2},{3,131},{131,3},{4... | collective-permute-start | bytes 12296 | tf_op jit(solution)/shard_map/ppermute | solution.py:30
  15.9 35.3 %copy-start = (s32[32,8]{0,1:T(8,128)S(1)}, s32[32,8]{0,1:T(8,128)}, u32[]{:S(2)}) copy-start(s32[32,8]{0,1:T(8,128)} %param.31) | copy-start | bytes 3076
  15.9 35.4 %copy-start.2 = (bf16[8,3,128]{2,0,1:T(8,128)(2,1)S(1)}, bf16[8,3,128]{2,0,1:T(8,128)(2,1)}, u32[]{:S(2)}) copy-start(bf16[8,3,128]{2,0,1:T(8,128)(2,1)} %param.22) | copy-start | bytes 18436
  15.9 41.9 %copy-start.1 = (f32[2048]{0:T(1024)S(1)}, f32[2048]{0:T(1024)}, u32[]{:S(2)}) copy-start(f32[2048]{0:T(1024)} %param.29) | copy-start | bytes 24580
  18.6 17.9 %all-to-all-start = ((f32[64,2,128]{2,1,0:T(2,128)}), f32[64,2,128]{2,1,0:T(2,128)S(1)}, u32[]{:S(2)}, u32[]{:S(2)}) async-start(f32[64,2,128]{2,1,0:T(2,128)} %bitcast.7), calls=%async_computation | async-start | bytes 131072 | tf_op jit(solution)/shard_map/all_to_all | solution.py:444
  27.6 8.9 %collective-permute-start.1 = (f32[8,128]{1,0:T(8,128)S(1)}, f32[8,128]{1,0:T(8,128)S(1)}, u32[]{:S(2)}, u32[]{:S(2)}) collective-permute-start(f32[8,128]{1,0:T(8,128)S(1)} %get-tuple-element.23.after_ref.pack_ref), channel_id=1, source_target_pairs={{0,1},{1,0},{2,3},{3,2},{4,5},{5,4},{6,7},{7,6},{8,9},{9,8},{10,11... | collective-permute-start | bytes 12296 | tf_op jit(solution)/shard_map/ppermute | solution.py:30
  30.8 38.0 %copy-start.3 = (f32[8,1]{0,1:T(1,128)S(1)}, f32[8,1]{0,1:T(1,128)}, u32[]{:S(2)}) copy-start(f32[8,1]{0,1:T(1,128)} %param.23) | copy-start | bytes 100
  37.3 20.4 %all-to-all-start.1 = ((bf16[256,2,128]{2,1,0:T(2,128)(2,1)}), bf16[256,2,128]{2,1,0:T(2,128)(2,1)S(1)}, u32[]{:S(2)}, u32[]{:S(2)}) async-start(bf16[256,2,128]{2,1,0:T(2,128)(2,1)} %broadcast_in_dim.43), calls=%async_computation.1 | async-start | bytes 262144 | tf_op jit(solution)/shard_map/all_to_all | solution.py:453
  44.7 24.1 %collective-permute-start.2 = (bf16[128,128]{1,0:T(8,128)(2,1)S(1)}, bf16[128,128]{1,0:T(8,128)(2,1)S(1)}, u32[]{:S(2)}, u32[]{:S(2)}) collective-permute-start(bf16[128,128]{1,0:T(8,128)(2,1)S(1)} %get-tuple-element.22.fresh_ref), channel_id=1, source_target_pairs={{0,128},{128,0},{1,129},{129,1},{2,130},{130,2},{3,131},{131,3},{4... | collective-permute-start | bytes 98312 | tf_op jit(solution)/shard_map/ppermute | solution.py:30
  62.9 18.6 %all-to-all-start.2 = ((f32[256,1,128]{2,1,0:T(1,128)}), f32[256,1,128]{2,1,0:T(1,128)S(1)}, u32[]{:S(2)}, u32[]{:S(2)}) async-start(f32[256,1,128]{2,1,0:T(1,128)} %bitcast.18), calls=%async_computation.2 | async-start | bytes 262144 | tf_op jit(solution)/shard_map/all_to_all | solution.py:487

commit v3 on v2

v3 whole, which is shorter than its diff:
```python
import jax
import jax.numpy as jnp
from jax import lax
from jax.experimental import pallas as pl
from jax.experimental.pallas import tpu as pltpu
from jax.sharding import Mesh, PartitionSpec as P

GRID = ("y", "x", "z")
BLOCKS = ("s", "t")
F32 = jnp.float32
BF16 = jnp.bfloat16
EXACT = lax.Precision.HIGHEST
SCALE = 128 ** (-0.5)

ANY = pl.BlockSpec(memory_space=pl.ANY)
HBM = pl.BlockSpec(memory_space=pl.ANY)
VMEM = pl.BlockSpec(memory_space=pltpu.VMEM)
SMEM = pl.BlockSpec(memory_space=pltpu.SMEM)


def params(mib):
    return pltpu.CompilerParams(vmem_limit_bytes=int(mib * 1024 * 1024))


def stay(*arrays):
    return [pltpu.with_memory_space_constraint(a, pltpu.HBM) for a in arrays]


def swap(shard, axis, flip):
    return lax.ppermute(shard, axis, [(i, i ^ flip) for i in range(lax.axis_size(axis))])


def iota(shape, axis):
    return lax.broadcasted_iota(jnp.int32, shape, axis)


def norm_rows(values, gain_row):
    return values * lax.rsqrt(jnp.mean(values * values, axis=-1, keepdims=True) + 1e-06) * gain_row


def dot(a, b, precision=None):
    return jnp.dot(a, b, preferred_element_type=F32, precision=precision)


def dot_t(a, b):
    return lax.dot_general(a, b, (((1,), (1,)), ((), ())), preferred_element_type=F32)


def beside(*parts):
    return jnp.concatenate(parts, axis=1)


def split_rows(queries):
    odd = iota((8, 128), 0) % 2 == 1
    return beside(jnp.where(odd, 0.0, queries), jnp.where(odd, queries, 0.0)).astype(BF16)


def own_block():
    return lax.axis_index("s") * 2 + lax.axis_index("t")


def picked(rows, index):
    return jnp.sum(jnp.where(iota(rows.shape, 0) == index, rows, 0.0), axis=0, keepdims=True)


def message_kernel(owner_hbm, gate_hbm, qkv_hbm, resid_hbm, out_ref, owner_ref, gate_ref, qkv_ref, resid_ref, sems):
    pairs = [(owner_hbm, owner_ref), (gate_hbm, gate_ref), (qkv_hbm, qkv_ref), (resid_hbm, resid_ref)]
    copies = [pltpu.make_async_copy(a, b, sems.at[i]) for i, (a, b) in enumerate(pairs)]
    for copy in copies:
        copy.start()
    for copy in copies:
        copy.wait()
    owner = owner_ref[...]
    for part in range(3):
        out_ref[part : part + 1, :] = picked(qkv_ref[part].astype(F32), owner)
    gate = jnp.sum(jnp.where(iota((1, 8), 1) == owner, gate_ref[...], 0.0), axis=1, keepdims=True)
    out_ref[3:4, :] = jnp.broadcast_to(gate, (1, 128))
    out_ref[4:8, :] = jnp.broadcast_to(owner.astype(F32), (4, 128))
    row = picked(resid_ref[...].astype(F32), owner)
    for c in range(16):
        out_ref[8 + c : 9 + c, :] = row[:, c * 128 : (c + 1) * 128]


def own_rows_kernel(
    length_ref, live_hbm, gate_hbm, decay_hbm, qkv_hbm, gain_hbm, kv_hbm, cache_hbm, state_hbm,
    head_ref, fresh_ref, live_ref, gate_ref, decay_ref, qkv_ref, gain_ref, kv_ref, cache_ref, state_ref,
    small_sem, kv_sem, cache_sem, state_sem,
):
    small = [
        (decay_hbm, decay_ref), (qkv_hbm, qkv_ref), (live_hbm, live_ref),
        (gate_hbm, gate_ref), (gain_hbm, gain_ref),
    ]
    small_copies = [pltpu.make_async_copy(a, b, small_sem.at[i]) for i, (a, b) in enumerate(small)]
    kv_copies = [pltpu.make_async_copy(kv_hbm, kv_ref, kv_sem.at[0])]
    state_copy = pltpu.make_async_copy(state_hbm, state_ref, state_sem)
    cache_copies = [
        pltpu.make_async_copy(cache_hbm.at[pl.ds(2 * p, 2)], cache_ref.at[pl.ds(2 * p, 2)], cache_sem.at[p]) for p in range(4)
    ]
    for copy in small_copies + kv_copies + cache_copies + [state_copy]:
        copy.start()

    for copy in small_copies:
        copy.wait()
    length = length_ref[0]
    places = iota((16, 128), 0) * 128 + iota((16, 128), 1)
    kept = jnp.where(places < length, decay_ref[...], 0.0)
    later = (iota((128, 128), 0) > iota((128, 128), 1)).astype(F32)
    later_rows = (iota((16, 16), 1) > iota((16, 16), 0)).astype(F32)
    totals = jnp.broadcast_to(jnp.sum(kept, axis=1, keepdims=True), (16, 128))
    suffix = dot(kept, later, EXACT) + dot(later_rows, totals, EXACT)
    weights = jnp.where(places < length, jnp.exp(suffix), 0.0)

    for copy in kv_copies:
        copy.wait()
    fresh = jnp.zeros((128, 128), F32)
    for i in range(8):
        parts = []
        for j in (2 * i, 2 * i + 1):
            turned = kv_ref[0, j * 128 : (j + 1) * 128, :].T.astype(F32)
            parts.append((turned * weights[j : j + 1, :]).astype(BF16))
        fresh += dot(beside(*parts), kv_ref[1, i * 256 : (i + 1) * 256, :])
    fresh_ref[...] = fresh.astype(BF16)

    queries = qkv_ref[0]
    q32, k32, v32 = queries.astype(F32), qkv_ref[1].astype(F32), qkv_ref[2].astype(F32)
    self_raw = jnp.sum(q32 * k32, axis=1, keepdims=True)
    self_score = self_raw * SCALE
    scores = jnp.zeros((8, 1024), F32)
    live = jnp.zeros((8, 1024), jnp.int32)
    gate = jnp.zeros((8, 128), F32)
    halves = split_rows(q32)
    for r in range(8):
        live = jnp.where(iota((8, 1024), 0) == r, live_ref[r], live)
        gate = jnp.where(iota((8, 128), 0) == r, gate_ref[r], gate)
    for p in range(4):
        cache_copies[p].wait()
        both = dot_t(halves, beside(cache_ref[2 * p, 0], cache_ref[2 * p + 1, 0]))
        scores = jnp.where(iota((8, 1024), 0) // 2 == p, both, scores)
    scores = scores * SCALE
    alive = iota((8, 1024), 1) >= 1024 - live
    peak = jnp.max(jnp.where(alive, scores, -jnp.inf), axis=1, keepdims=True)
    peak = jnp.maximum(peak, self_score)
    prob = jnp.where(alive, jnp.exp(scores - peak), 0.0).astype(BF16)
    self_prob = jnp.exp(self_score - peak).astype(BF16).astype(F32)
    below = jnp.sum(prob.astype(F32), axis=1, keepdims=True) + self_prob
    above = jnp.zeros((8, 128), F32)
    linear = jnp.zeros((8, 128), F32)
    state_copy.wait()
    row = iota((8, 128), 0)
    for p in range(4):
        both = dot(prob, beside(cache_ref[2 * p, 1], cache_ref[2 * p + 1, 1]))
        above = jnp.where(row == 2 * p, both[:, :128], jnp.where(row == 2 * p + 1, both[:, 128:], above))
    for p in range(2):
        a, b, c, d = (state_ref[4 * p + i] for i in range(4))
        both = dot(halves, jnp.concatenate([beside(a, c), beside(b, d)], axis=0))
        linear = jnp.where(row // 2 == 2 * p, both[:, :128], jnp.where(row // 2 == 2 * p + 1, both[:, 128:], linear))
    window_out = (above + self_prob * v32) / below
    linear_out = jnp.exp(gate) * linear + self_raw * v32
    head_ref[...] = norm_rows(linear_out, gain_ref[0:1, :]) + norm_rows(window_out, gain_ref[1:2, :])


def guest_kernel(
    length_ref, message_ref, got_ref, head_ref, fresh_ref, gain_hbm, kv_ref, weight_ref,
    out_ref, pack_ref, gain_ref, gain_sem,
):
    gain_copy = pltpu.make_async_copy(gain_hbm, gain_ref, gain_sem)
    gain_copy.start()
    owner = message_ref[4:5, :]
    rows = iota((8, 128), 0).astype(F32)
    pack_ref[...] = jnp.where(rows == 0.0, owner, got_ref[4:5, :])
    q32, k32, v32 = got_ref[0:1, :], got_ref[1:2, :], got_ref[2:3, :]
    self_raw = jnp.sum(q32 * k32, axis=1, keepdims=True)
    self_score = self_raw * SCALE
    query = jnp.broadcast_to(q32, (8, 128))
    linear_out = jnp.exp(got_ref[3:4, :]) * dot(query.astype(BF16), fresh_ref[...])[0:1, :] + self_raw * v32

    scores = dot_t(split_rows(query), beside(kv_ref[0, 0:1024, :], kv_ref[0, 1024:2048, :])) * SCALE
    places = iota((8, 1024), 1) + iota((8, 1024), 0) % 2 * 1024
    length = length_ref[0]
    alive = (places < length) & (places >= length - 1024)
    peak = jnp.max(jnp.where(alive, scores, -jnp.inf), axis=1, keepdims=True)
    peak = jnp.maximum(jnp.maximum(peak[0:1, :], peak[1:2, :]), self_score)
    prob = jnp.where(alive, jnp.exp(scores - peak), 0.0).astype(BF16)
    self_prob = jnp.exp(self_score - peak).astype(BF16).astype(F32)
    total = jnp.sum(prob.astype(F32), axis=1, keepdims=True)
    below = total[0:1, :] + total[1:2, :] + self_prob
    both = dot(prob, beside(kv_ref[1, 0:1024, :], kv_ref[1, 1024:2048, :]))
    window_out = (both[0:1, :128] + both[1:2, 128:] + self_prob * v32) / below
    gain_copy.wait()
    head = norm_rows(linear_out, gain_ref[0:1, :]) + norm_rows(window_out, gain_ref[1:2, :])
    head = jnp.where(rows == owner, head, head_ref[...]).astype(BF16)
    for c in range(8):
        part = dot(head, weight_ref[:, c * 256 : (c + 1) * 256])
        out_ref[2 * c] = part[:, :128]
        out_ref[2 * c + 1] = part[:, 128:]


def named_by(turned_ref):
    turned = turned_ref[...]
    experts = iota((128, 32), 0)
    member = jnp.zeros((128, 32), F32)
    for k in range(8):
        member = jnp.where(turned[k : k + 1, :] == experts, 1.0, member)
    same = (iota((32, 32), 0) == iota((32, 32), 1)).astype(F32)
    return dot_t(same, member)


def own_expert():
    return lax.axis_index("s") * 64 + lax.axis_index("y") * 16 + lax.axis_index("x") * 4 + lax.axis_index("z")


def prepare_kernel(
    pack_ref, beside_ref, turned_ref, order_ref, chooser_ref, member_ref, spread_ref, use_ref
):
    block = own_block()
    owners = [pack_ref[0, 0], pack_ref[1, 0], beside_ref[0, 0], beside_ref[1, 0]]
    blocks = [block, block ^ 2, block ^ 1, block ^ 3]
    ids = iota((32, 32), 1)
    place, row = ids // 8, (ids % 8).astype(F32)
    target = jnp.zeros((32, 32), F32)
    for j in range(4):
        own = (blocks[j] * 8).astype(F32) + row
        other = (blocks[j ^ 1] * 8).astype(F32) + owners[j ^ 1]
        target = jnp.where(place == j, jnp.where(row == owners[j], other, own), target)
    order = (target == iota((32, 32), 0).astype(F32)).astype(F32)
    order_ref[...] = order

    expert = own_expert()
    names_own = jnp.max((turned_ref[...] == expert).astype(F32), axis=0, keepdims=True)
    names_own = jnp.broadcast_to(names_own, (8, 32))
    upper = (iota((32, 32), 0) < iota((32, 32), 1)).astype(F32)
    rank = dot(names_own, upper)
    slots = (iota((8, 32), 0) % 4).astype(F32)
    chooser_ref[...] = jnp.where(names_own > 0, (rank == slots).astype(F32), 0.0)

    member = named_by(turned_ref)
    member_ref[...] = member
    spread_ref[...] = (iota((128, 1024), 1) // 8 == iota((128, 1024), 0)).astype(BF16)

    lower = (iota((32, 32), 1) < iota((32, 32), 0)).astype(F32)
    slot = jnp.where(member > 0, dot(lower, member), -1.0)
    first = (iota((8, 32), 1) == iota((8, 32), 0) + block * 8).astype(F32)
    slot = dot(first, slot)
    src = iota((128, 256), 1)
    sender = src // 128 * 64 + src % 16 * 4 + src // 16 % 4
    slot = dot(slot, (sender == iota((128, 256), 0)).astype(F32))
    for k in range(4):
        use_ref[k * 8 : (k + 1) * 8, :] = (slot == float(k)).astype(F32)


def fetch_kernel(after_ref, router_hbm, in_hbm, router_ref, near_ref, sems):
    copies = [
        pltpu.make_async_copy(router_hbm, router_ref, sems.at[0]),
        pltpu.make_async_copy(in_hbm.at[pl.ds(0, 4096)], near_ref.at[pl.ds(0, 4096)], sems.at[1]),
        pltpu.make_async_copy(in_hbm.at[pl.ds(8192, 4096)], near_ref.at[pl.ds(4096, 4096)], sems.at[2]),
    ]
    for copy in copies:
        copy.start()
    for copy in copies:
        copy.wait()


def hidden_kernel(total_ref, message_ref, got_ref, resid_ref, fresh_ref, out_ref):
    taken = iota((8, 128), 0).astype(F32) == message_ref[4:5, :]
    for pair in range(8):
        parts = []
        for c in (2 * pair, 2 * pair + 1):
            rows = resid_ref[:, c * 128 : (c + 1) * 128].astype(F32)
            parts.append(jnp.where(taken, got_ref[8 + c : 9 + c, :], rows) + total_ref[c])
        out_ref[pair * 16 : (pair + 1) * 16, :] = jnp.concatenate(parts, axis=0).astype(BF16)
    out_ref[128:256, :] = fresh_ref[...]


def expert_kernel(
    order_ref, chooser_ref, member_ref, spread_ref, gain_ref, packet_ref, theirs_ref, next_ref, cross_ref, router_ref,
    near_ref, in_hbm, down_hbm,
    out_ref, own_ref, turn_ref, far_ref, down_ref, far_sem, down_sem,
):
    far_copies = []
    for half in range(2):
        for i in range(2):
            source = in_hbm.at[pl.ds(half * 8192 + 4096 + i * 2048, 2048)]
            target = far_ref.at[pl.ds(half * 4096 + i * 2048, 2048)]
            far_copies.append(pltpu.make_async_copy(source, target, far_sem.at[half * 2 + i]))
    down_copies = [
        pltpu.make_async_copy(down_hbm.at[pl.ds(i * 128, 128)], down_ref.at[pl.ds(i * 128, 128)], down_sem.at[i])
        for i in range(4)
    ]
    for i in (0, 2, 1, 3):
        far_copies[i].start()
    for copy in down_copies:
        copy.start()
    block = own_block()
    expert = own_expert()
    order, chooser, member = order_ref[...], chooser_ref[...], member_ref[...]

    hidden = []
    for ref in (packet_ref, theirs_ref, next_ref, cross_ref):
        two = [ref[pair * 16 : (pair + 1) * 16, :].astype(F32) for pair in range(8)]
        hidden.append([half for both in two for half in (both[:8, :], both[8:, :])])
    scales = []
    for rows in hidden:
        total = jnp.zeros((8, 128), F32)
        for x in rows:
            total += x * x
        scales.append(lax.rsqrt(jnp.sum(total, axis=1, keepdims=True) * (1.0 / 2048) + 1e-06))
    tiles = []
    for c in range(16):
        gain = gain_ref[:, c * 128 : (c + 1) * 128]
        parts = [hidden[j][c] * scales[j] * gain for j in range(4)]
        tiles.append(jnp.concatenate(parts, axis=0).astype(BF16))
    normed = jnp.concatenate(tiles, axis=1)

    choose_gathered = dot(chooser, order)
    rows_in = dot(choose_gathered.astype(BF16), normed)

    logits = dot(order, dot(normed, router_ref[...]), EXACT)
    lanes = iota((32, 128), 1)
    chosen = member / (1.0 + jnp.exp(-logits))
    chosen = jnp.where(member > 0, chosen, 0.0)
    share = jnp.sum(jnp.where(lanes == expert, chosen, 0.0), axis=1, keepdims=True)
    share = share / jnp.sum(chosen, axis=1, keepdims=True)
    gates = dot(chooser, jnp.broadcast_to(share, (32, 128)), EXACT)

    stacked = jnp.concatenate([rows_in[:, c * 128 : (c + 1) * 128] for c in range(16)], axis=0)
    repeated = dot(stacked.astype(BF16), spread_ref[...])
    kind = iota((8, 1024), 1) % 8 - iota((8, 1024), 0) // 4
    pre = jnp.zeros((64, 256), F32)
    for c in range(8):
        halves = [repeated[i * 8 : (i + 1) * 8, :] for i in (c, c + 8)]
        left = jnp.concatenate([jnp.where(kind == 2 * p, half, 0.0) for half in halves for p in range(4)], axis=0)
        if c >= 4 and c % 2 == 0:
            far_copies[c // 2 - 2].wait()
            far_copies[c // 2].wait()
        source, start = (near_ref, c * 1024) if c < 4 else (far_ref, (c - 4) * 1024)
        right = beside(source[start : start + 1024, :], source[start + 4096 : start + 5120, :])
        pre += dot(left.astype(BF16), right)
    pre = pre[:32, :128] + pre[32:, 128:]
    acts = []
    for p in range(4):
        both = pre[p * 8 : (p + 1) * 8, :]
        acts.append(both / (1.0 + jnp.exp(-both)) * pltpu.roll(both, 4, 0))
    act = jnp.concatenate(acts, axis=1).astype(BF16)
    for copy in down_copies:
        copy.wait()
    for c in range(8):
        part = dot(act, down_ref[:, c * 256 : (c + 1) * 256])
        turn_ref[2 * c] = part[:, :128] * gates
        turn_ref[2 * c + 1] = part[:, 128:] * gates

    lane_block = iota((16, 128), 1) // 32
    by_slot = [turn_ref[:, k, :] for k in range(4)]
    for q in range(4):
        piece = jnp.zeros((16, 128), F32)
        for k in range(4):
            shift = (k - q) * 32 % 128
            moved = by_slot[k] if shift == 0 else pltpu.roll(by_slot[k], shift, 1)
            piece = jnp.where(lane_block == k, moved, piece)
        for b in range(4):
            out_ref[b * 64 + q * 16 : b * 64 + (q + 1) * 16, :] = piece

    tile = lax.axis_index("y") * 4 + lax.axis_index("x")
    rows = pl.ds(pl.multiple_of(tile // 2 * 16, 16), 16)
    raw = []
    for ref in (packet_ref, theirs_ref, next_ref, cross_ref):
        both = ref[rows, :].astype(F32)
        raw.append(jnp.where(tile % 2 == 0, both[:8, :], both[8:, :]))
    raw = jnp.concatenate(raw, axis=0)
    first = (iota((8, 32), 1) == iota((8, 32), 0) + block * 8).astype(F32)
    mine = dot(dot(first, order).astype(BF16), raw.astype(BF16))
    deep = lax.axis_index("z")
    own = mine
    for q in range(1, 4):
        own = jnp.where(deep == q, pltpu.roll(mine, 128 - q * 32, 1), own)
    own_ref[...] = own


def finish_kernel(use_ref, back_ref, own_ref, out_ref):
    back = back_ref[...]
    high = back.astype(BF16)
    low = (back - high.astype(F32)).astype(BF16)
    use = use_ref[...].astype(BF16)
    total = dot(use, high) + dot(use, low)
    out = own_ref[:, 0:32]
    for k in range(4):
        out += total[k * 8 : (k + 1) * 8, k * 32 : (k + 1) * 32]
    out_ref[...] = out.astype(BF16)


def on_device(
    pre_kv, pre_gate, pre_len, owners, win_len, dec_qkv, dec_gate, state_cache, win_cache,
    head_gain, out_weight, resid, moe_gain, router, routes, w_in, w_down,
):
    qkv = dec_qkv.transpose(1, 0, 2)
    gates = dec_gate.reshape(8)

    message = pl.pallas_call(
        message_kernel,
        out_shape=jax.ShapeDtypeStruct((24, 128), F32),
        in_specs=[ANY] + [HBM] * 3,
        out_specs=VMEM,
        scratch_shapes=[
            pltpu.VMEM((1, 1), jnp.int32),
            pltpu.VMEM((1, 8), F32),
            pltpu.VMEM((3, 8, 128), BF16),
            pltpu.VMEM((8, 2048), BF16),
            pltpu.SemaphoreType.DMA((4,)),
        ],
        compiler_params=params(2),
        name="message",
    )(owners.reshape(1, 1), *stay(gates.reshape(1, 8), qkv, resid))
    got = swap(message, "s", 1)

    own_heads, fresh_state = pl.pallas_call(
        own_rows_kernel,
        out_shape=(jax.ShapeDtypeStruct((8, 128), F32), jax.ShapeDtypeStruct((128, 128), BF16)),
        in_specs=[SMEM] + [HBM] * 8,
        out_specs=(VMEM, VMEM),
        scratch_shapes=[
            pltpu.SMEM((8,), jnp.int32),
            pltpu.SMEM((8,), F32),
            pltpu.VMEM((16, 128), F32),
            pltpu.VMEM((3, 8, 128), BF16),
            pltpu.VMEM((2, 128), F32),
            pltpu.VMEM((2, 2048, 128), BF16),
            pltpu.VMEM((8, 2, 1024, 128), BF16),
            pltpu.VMEM((8, 128, 128), BF16),
            pltpu.SemaphoreType.DMA((5,)),
            pltpu.SemaphoreType.DMA((1,)),
            pltpu.SemaphoreType.DMA((4,)),
            pltpu.SemaphoreType.DMA,
        ],
        compiler_params=params(14),
        name="own_rows",
    )(
        pre_len,
        *stay(
            win_len, gates, pre_gate.reshape(16, 128), qkv, head_gain,
            pre_kv[0], win_cache, state_cache[:, 0],
        )
    )

    partial, pack = pl.pallas_call(
        guest_kernel,
        out_shape=(jax.ShapeDtypeStruct((16, 8, 128), F32), jax.ShapeDtypeStruct((8, 128), F32)),
        in_specs=[SMEM] + [VMEM] * 4 + [HBM] + [VMEM] * 2,
        out_specs=(VMEM, VMEM),
        scratch_shapes=[pltpu.VMEM((2, 128), F32), pltpu.SemaphoreType.DMA],
        compiler_params=params(8),
        name="guest",
    )(pre_len, message, got, own_heads, fresh_state, *stay(head_gain), pre_kv[0], out_weight)

    expert_in = w_in[0].reshape(2048, 2, 4, 128).transpose(0, 2, 1, 3).reshape(16384, 128)
    total = partial
    for axis in ("x", "y", "z"):
        parts = [swap(total, axis, flip) for flip in (1, 2, 3)]
        total = (total + parts[0]) + (parts[1] + parts[2])
    packet = pl.pallas_call(
        hidden_kernel,
        out_shape=jax.ShapeDtypeStruct((256, 128), BF16),
        in_specs=[VMEM] * 5,
        out_specs=VMEM,
        compiler_params=params(2),
        name="hidden",
    )(total, message, got, resid, fresh_state)
    packet, pack = lax.optimization_barrier((packet, pack))
    theirs = swap(packet, "s", 1)
    next_door = swap(pack, "t", 1)
    router_near, in_near = pl.pallas_call(
        fetch_kernel,
        out_shape=(pltpu.VMEM((2048, 128), BF16), pltpu.VMEM((8192, 128), BF16)),
        in_specs=[ANY] + [HBM] * 2,
        out_specs=(VMEM,) * 2,
        scratch_shapes=[pltpu.SemaphoreType.DMA((3,))],
        compiler_params=params(2),
        name="fetch",
    )(packet, *stay(router, expert_in))

    beyond = swap(packet, "t", 1)
    order, chooser, member, spread, use = pl.pallas_call(
        prepare_kernel,
        out_shape=(
            jax.ShapeDtypeStruct((32, 32), F32),
            jax.ShapeDtypeStruct((8, 32), F32),
            jax.ShapeDtypeStruct((32, 128), F32),
            jax.ShapeDtypeStruct((128, 1024), BF16),
            jax.ShapeDtypeStruct((32, 256), F32),
        ),
        in_specs=[VMEM] * 3,
        out_specs=(VMEM,) * 5,
        compiler_params=params(4),
        name="prepare",
    )(pack, next_door, routes.T)
    theirs, router_near, in_near, order, chooser, member, spread, use = lax.optimization_barrier(
        (theirs, router_near, in_near, order, chooser, member, spread, use)
    )
    cross = swap(theirs, "t", 1)
    term, own = pl.pallas_call(
        expert_kernel,
        out_shape=(jax.ShapeDtypeStruct((256, 128), F32), jax.ShapeDtypeStruct((8, 128), F32)),
        in_specs=[VMEM] * 11 + [HBM] * 2,
        out_specs=(VMEM, VMEM),
        scratch_shapes=[
            pltpu.VMEM((16, 8, 128), F32),
            pltpu.VMEM((8192, 128), BF16),
            pltpu.VMEM((512, 2048), BF16),
            pltpu.SemaphoreType.DMA((4,)),
            pltpu.SemaphoreType.DMA((4,)),
        ],
        compiler_params=params(12),
        name="experts",
    )(
        order, chooser, member, spread, moe_gain.reshape(1, 2048), packet, theirs, beyond, cross,
        router_near, in_near, *stay(expert_in, w_down[0]),
    )
    back = lax.all_to_all(term.reshape(256, 1, 128), ("s", "t", "z", "y", "x"), 0, 0, tiled=True)
    layer_out = pl.pallas_call(
        finish_kernel,
        out_shape=jax.ShapeDtypeStruct((8, 32), BF16),
        in_specs=[VMEM] * 3,
        out_specs=VMEM,
        compiler_params=params(2),
        name="finish",
    )(use, back.reshape(256, 128), own)

    late_qkv, late_gate, late_state, late_pack, _ = lax.optimization_barrier(
        (dec_qkv, dec_gate, state_cache, pack, own)
    )
    taken = jnp.arange(8, dtype=F32) == late_pack[0, :8]
    previous = jnp.where(taken[:, None, None], theirs[None, 128:], late_state[:, 0]).astype(F32)
    own_k, own_v = late_qkv[:, 1].astype(F32), late_qkv[:, 2].astype(F32)
    states = jnp.exp(late_gate)[:, :, None] * previous + own_k[:, :, None] * own_v[:, None, :]
    return layer_out, states[:, None]


def solution(mesh):
    fine = Mesh(mesh.devices.reshape(2, 4, 4, 4, 2), ("s", "y", "x", "z", "t"))
    placed = (
        P(BLOCKS, None, None, GRID),
        P(BLOCKS, GRID, None),
        P(BLOCKS),
        P(BLOCKS),
        P(BLOCKS),
        P(BLOCKS, None, GRID),
        P(BLOCKS, GRID),
        P(BLOCKS, GRID, None, None),
        P(BLOCKS, None, None, GRID),
        P(None, GRID),
        P(GRID, None),
        P(BLOCKS, None),
        P(),
        P(),
        P(),
        P(("s",) + GRID, None, None, "t"),
        P(("s",) + GRID, "t", None),
    )
    return jax.shard_map(
        on_device,
        mesh=fine,
        in_specs=placed,
        out_specs=(P(BLOCKS, GRID), P(BLOCKS, GRID, None, None)),
        check_vma=False,
    )
```

time: 82.7 us -> 78.7 us (0.952)
  Pallas kernels: 17 us -> 14 us
  waiting for transfers between devices: 21.6 us -> 23.9 us
  other arithmetic: 2.84 us -> 1.09 us
    all_to_all x2 -> x0, starting transfers between devices: 16.4 us -> none  [the longest x1 9.04 us: on_device(): lax.all_to_all(partial.reshape(64, 2, 128), GRID, 0, 0, tiled=True).sum(0)]
    ppermute x3 -> x14, starting transfers between devices: 15.6 us -> 29.7 us  [swap(): lax.ppermute(shard, axis, [(i, i ^ flip) for i in range(lax.axis_size(axi...]
    ppermute x3 -> x14, waiting for transfers between devices: 0.01 us -> 12.4 us  [swap(): lax.ppermute(shard, axis, [(i, i ^ flip) for i in range(lax.axis_size(axi...]
    all_to_all x2 -> x0, waiting for transfers between devices: 10.9 us -> none  [the longest x1 6.04 us: on_device(): lax.all_to_all(jnp.broadcast_to(hidden[None], (256, 2, 128)), ('s', 't',...]
    all_to_all x1, starting transfers between devices: 5.89 us -> 7.45 us  [on_device(): lax.all_to_all(term.reshape(256, 1, 128), ('s', 't', 'z', 'y', 'x'), 0, 0...]
    pallas_call x1, Pallas kernels: 2.68 us -> 1.35 us  [on_device(): pl.pallas_call(guest_kernel, out_shape=(jax.ShapeDtypeStruct((16, 8, 128)...]
    add x1 -> x4, other arithmetic: 1.98 us -> 1.08 us  [the longest x1 1.03 us: on_device(): jnp.exp(late_gate)[:, :, None] * previous]
    pallas_call x1, Pallas kernels: 5.13 us -> 4.25 us  [on_device(): pl.pallas_call(expert_kernel, out_shape=(jax.ShapeDtypeStruct((256, 128),...]
  transfers between devices with their start and end apart: 6 -> 15, of which waited for: 3 -> 9; matrix products, arithmetic and copies ran while one was open for 4% -> 1% of each run, Pallas kernels for 15% -> 8%
where the time goes in v3:
time: 78.7 us; the launch traced here: 78.5 us
  starting transfers between devices  37.2 us (47%)
  waiting for transfers between devices  23.9 us (30%)
  Pallas kernels  14 us (18%)
  between operations  2.26 us (3%)
  other arithmetic  1.09 us (1%)
    ppermute x14, starting transfers between devices, swap(): lax.ppermute(shard, axis, [(i, i ^ flip) for i in range(lax.axis_size(axi...  29.7 us
    ppermute x14, waiting for transfers between devices, swap(): lax.ppermute(shard, axis, [(i, i ^ flip) for i in range(lax.axis_size(axi...  12.4 us
    all_to_all x1, waiting for transfers between devices, on_device(): lax.all_to_all(term.reshape(256, 1, 128), ('s', 't', 'z', 'y', 'x'), 0, 0...  11.4 us
    all_to_all x1, starting transfers between devices, on_device(): lax.all_to_all(term.reshape(256, 1, 128), ('s', 't', 'z', 'y', 'x'), 0, 0...  7.45 us
    pallas_call x1, Pallas kernels, on_device(): pl.pallas_call(own_rows_kernel, out_shape=(jax.ShapeDtypeStruct((8, 128),...  4.4 us
    pallas_call x1, Pallas kernels, on_device(): pl.pallas_call(expert_kernel, out_shape=(jax.ShapeDtypeStruct((256, 128),...  4.25 us
    pallas_call x1, Pallas kernels, on_device(): pl.pallas_call(fetch_kernel, out_shape=(pltpu.VMEM((2048, 128), BF16), pl...  1.73 us
  transfers between devices with their start and end apart: 15, of which 9 were waited for; matrix products, arithmetic and copies ran while one was open for 1% of the time, Pallas kernels for 8%

profile of v3, /device:TPU:1, one launch (start us, length us, event | category | flops | bytes accessed | tf_op | source)
XLA Modules:
  0.0 78.5 jit_solution(7378524770013563326)
XLA Ops:
  0.6 0.0 copy-start.2
  0.6 0.0 copy-start
  0.7 0.0 copy-start.1
  1.4 1.0 %message.1.message_ref = f32[24,128]{1,0:T(8,128)S(1)} custom-call(s32[1,1]{1,0:T(1,128)} %bitcast.29.owner_hbm, f32[1,8]{1,0:T(1,128)} %bitcast.42, bf16[3,8,128]{2,1,0:T(8,128)(2,1)} %bitcast.39, bf16[8,2048]{1,0:T(8,128)(2,1)} %resid_ref.1), custom_call_target="tpu_custom_call" | custom-call | tf_op jit(solution)/shard_map/message/pallas_call | solution.py:397
  2.4 7.8 %collective-permute-start = (f32[24,128]{1,0:T(8,128)S(1)}, f32[24,128]{1,0:T(8,128)S(1)}, u32[]{:S(2)}, u32[]{:S(2)}) collective-permute-start(f32[24,128]{1,0:T(8,128)S(1)} %message.1.message_ref), channel_id=1, source_target_pairs={{0,128},{128,0},{1,129},{129,1},{2,130},{130,2},{3,131},{131,3},{4... | collective-permute-start | bytes 36872 | tf_op jit(solution)/shard_map/ppermute | solution.py:30
  10.9 4.4 %own_rows.1 = (f32[8,128]{1,0:T(8,128)S(1)}, bf16[128,128]{1,0:T(8,128)(2,1)S(1)}) custom-call(s32[1]{0:T(128)S(6)} %copy.22.length_ref, s32[8]{0:T(128)} %live_hbm.1, f32[8]{0:T(128)} %bitcast.43, f32[16,128]{1,0:T(8,128)} %bitcast.41, bf16[3,8,128]{2,1,0:T(8,128)(2,1)} %bitcast.40, f32[2,128]{1,0:T(2,128)} %gain_hbm.3, bf16[2,2048,128]{2,1,0:T(8,128)(2,1)} %bitcast.30, ...), custom_call_target="tpu_custom_call" | custom-call | tf_op jit(solution)/shard_map/own_rows/pallas_call | solution.py:414
  15.3 0.0 copy-start.4
  15.3 0.0 copy-start.3
  15.3 0.0 collective-permute-done.got_ref
  15.3 0.0 copy-done
  15.3 0.0 copy-done.1
  15.4 1.4 %guest.1 = (f32[16,8,128]{2,1,0:T(8,128)S(1)}, f32[8,128]{1,0:T(8,128)S(1)}) custom-call(s32[1]{0:T(128)S(6)} %copy.22.length_ref, f32[24,128]{1,0:T(8,128)S(1)} %message.1.message_ref, f32[24,128]{1,0:T(8,128)S(1)} %collective-permute-done.got_ref, f32[8,128]{1,0:T(8,128)S(1)} %get-tuple-element.29.head_ref, ...), custom_call_target="tpu_custom_call" | custom-call | tf_op jit(solution)/shard_map/guest/pallas_call | solution.py:443
  16.7 2.8 %collective-permute-start.2 = (f32[16,8,128]{2,1,0:T(8,128)S(1)}, f32[16,8,128]{2,1,0:T(8,128)S(1)}, u32[]{:S(2)}, u32[]{:S(2)}) collective-permute-start(f32[16,8,128]{2,1,0:T(8,128)S(1)} %get-tuple-element.31), channel_id=1, source_target_pairs={{0,16},{8,24},{16,0},{24,8},{1,17},{9,25},{17,1},{25,9},{2,18},{10... | collective-permute-start | bytes 196616 | tf_op jit(solution)/shard_map/ppermute | solution.py:30
  19.5 0.9 %collective-permute-start.3 = (f32[16,8,128]{2,1,0:T(8,128)S(1)}, f32[16,8,128]{2,1,0:T(8,128)S(1)}, u32[]{:S(2)}, u32[]{:S(2)}) collective-permute-start(f32[16,8,128]{2,1,0:T(8,128)S(1)} %get-tuple-element.31), channel_id=1, source_target_pairs={{0,24},{8,16},{16,8},{24,0},{1,25},{9,17},{17,9},{25,1},{2,26},{10... | collective-permute-start | bytes 196616 | tf_op jit(solution)/shard_map/ppermute | solution.py:30
  20.4 0.0 collective-permute-start.1
  20.4 1.0 %collective-permute-done.2 = f32[16,8,128]{2,1,0:T(8,128)S(1)} collective-permute-done((f32[16,8,128]{2,1,0:T(8,128)S(1)}, f32[16,8,128]{2,1,0:T(8,128)S(1)}, u32[]{:S(2)}, u32[]{:S(2)}) %collective-permute-start.2) | collective-permute-done | bytes 65568 | tf_op jit(solution)/shard_map/ppermute | solution.py:30
  21.4 2.4 %collective-permute-done.3 = f32[16,8,128]{2,1,0:T(8,128)S(1)} collective-permute-done((f32[16,8,128]{2,1,0:T(8,128)S(1)}, f32[16,8,128]{2,1,0:T(8,128)S(1)}, u32[]{:S(2)}, u32[]{:S(2)}) %collective-permute-start.3) | collective-permute-done | bytes 65568 | tf_op jit(solution)/shard_map/ppermute | solution.py:30
  23.9 0.0 collective-permute-done.1
  23.9 3.0 %collective-permute-start.5 = (f32[16,8,128]{2,1,0:T(8,128)S(1)}, f32[16,8,128]{2,1,0:T(8,128)S(1)}, u32[]{:S(2)}, u32[]{:S(2)}) collective-permute-start(f32[16,8,128]{2,1,0:T(8,128)S(1)} %add_add_fusion.2), channel_id=1, source_target_pairs={{0,64},{32,96},{64,0},{96,32},{1,65},{33,97},{65,1},{97,33},{2,66}... | collective-permute-start | bytes 196616 | tf_op jit(solution)/shard_map/ppermute | solution.py:30
  26.9 0.8 collective-permute-start.6
  27.7 0.0 collective-permute-start.4
  27.7 0.9 %collective-permute-done.5 = f32[16,8,128]{2,1,0:T(8,128)S(1)} collective-permute-done((f32[16,8,128]{2,1,0:T(8,128)S(1)}, f32[16,8,128]{2,1,0:T(8,128)S(1)}, u32[]{:S(2)}, u32[]{:S(2)}) %collective-permute-start.5) | collective-permute-done | bytes 65568 | tf_op jit(solution)/shard_map/ppermute | solution.py:30
  28.6 3.3 %collective-permute-done.6 = f32[16,8,128]{2,1,0:T(8,128)S(1)} collective-permute-done((f32[16,8,128]{2,1,0:T(8,128)S(1)}, f32[16,8,128]{2,1,0:T(8,128)S(1)}, u32[]{:S(2)}, u32[]{:S(2)}) %collective-permute-start.6) | collective-permute-done | bytes 65568 | tf_op jit(solution)/shard_map/ppermute | solution.py:30
  31.9 0.0 collective-permute-done.4
  32.0 1.3 %collective-permute-start.8 = (f32[16,8,128]{2,1,0:T(8,128)S(1)}, f32[16,8,128]{2,1,0:T(8,128)S(1)}, u32[]{:S(2)}, u32[]{:S(2)}) collective-permute-start(f32[16,8,128]{2,1,0:T(8,128)S(1)} %add_add_fusion.1), channel_id=1, source_target_pairs={{0,4},{2,6},{4,0},{6,2},{1,5},{3,7},{5,1},{7,3},{8,12},{10,14},{12... | collective-permute-start | bytes 196616 | tf_op jit(solution)/shard_map/ppermute | solution.py:30
  33.2 1.6 %collective-permute-start.9 = (f32[16,8,128]{2,1,0:T(8,128)S(1)}, f32[16,8,128]{2,1,0:T(8,128)S(1)}, u32[]{:S(2)}, u32[]{:S(2)}) collective-permute-start(f32[16,8,128]{2,1,0:T(8,128)S(1)} %add_add_fusion.1), channel_id=1, source_target_pairs={{0,6},{2,4},{4,2},{6,0},{1,7},{3,5},{5,3},{7,1},{8,14},{10,12},{12... | collective-permute-start | bytes 196616 | tf_op jit(solution)/shard_map/ppermute | solution.py:30
  34.9 0.0 collective-permute-start.7
  34.9 1.9 %collective-permute-done.8 = f32[16,8,128]{2,1,0:T(8,128)S(1)} collective-permute-done((f32[16,8,128]{2,1,0:T(8,128)S(1)}, f32[16,8,128]{2,1,0:T(8,128)S(1)}, u32[]{:S(2)}, u32[]{:S(2)}) %collective-permute-start.8) | collective-permute-done | bytes 65568 | tf_op jit(solution)/shard_map/ppermute | solution.py:30
  36.8 1.5 %collective-permute-done.9 = f32[16,8,128]{2,1,0:T(8,128)S(1)} collective-permute-done((f32[16,8,128]{2,1,0:T(8,128)S(1)}, f32[16,8,128]{2,1,0:T(8,128)S(1)}, u32[]{:S(2)}, u32[]{:S(2)}) %collective-permute-start.9) | collective-permute-done | bytes 65568 | tf_op jit(solution)/shard_map/ppermute | solution.py:30
  38.3 0.4 collective-permute-done.7
  38.7 0.0 copy-done.2
  38.7 2.2 %collective-permute-start.10 = (bf16[256,128]{1,0:T(8,128)(2,1)S(1)}, bf16[256,128]{1,0:T(8,128)(2,1)S(1)}, u32[]{:S(2)}, u32[]{:S(2)}) collective-permute-start(bf16[256,128]{1,0:T(8,128)(2,1)S(1)} %hidden.1.after_ref.packet_ref), channel_id=1, source_target_pairs={{0,128},{128,0},{1,129},{129,1},{2,130},{130,2},{3,131},{131,3},{4... | collective-permute-start | bytes 196616 | tf_op jit(solution)/shard_map/ppermute | solution.py:30
  41.0 5.1 %collective-permute-start.11 = (f32[8,128]{1,0:T(8,128)S(1)}, f32[8,128]{1,0:T(8,128)S(1)}, u32[]{:S(2)}, u32[]{:S(2)}) collective-permute-start(f32[8,128]{1,0:T(8,128)S(1)} %get-tuple-element.53.pack_ref), channel_id=1, source_target_pairs={{0,1},{1,0},{2,3},{3,2},{4,5},{5,4},{6,7},{7,6},{8,9},{9,8},{10,11... | collective-permute-start | bytes 12296 | tf_op jit(solution)/shard_map/ppermute | solution.py:30
  46.0 0.0 collective-permute-start.12
  46.0 1.7 %fetch.1 = (bf16[2048,128]{1,0:T(8,128)(2,1)S(1)}, bf16[8192,128]{1,0:T(8,128)(2,1)S(1)}) custom-call(bf16[256,128]{1,0:T(8,128)(2,1)S(1)} %hidden.1.after_ref.packet_ref, bf16[2048,128]{1,0:T(8,128)(2,1)} %router_hbm.1, bf16[16384,128]{1,0:T(8,128)(2,1)} %bitcast.35), custom_call_target="tpu_custom_call" | custom-call | tf_op jit(solution)/shard_map/fetch/pallas_call | solution.py:469
  47.8 0.0 collective-permute-done.11.beside_ref
  47.8 0.0 copy-done.4
  47.8 0.5 prepare.1
  48.3 0.0 collective-permute-done.10.theirs_ref
  48.3 4.2 %collective-permute-start.13 = (bf16[256,128]{1,0:T(8,128)(2,1)S(1)}, bf16[256,128]{1,0:T(8,128)(2,1)S(1)}, u32[]{:S(2)}, u32[]{:S(2)}) collective-permute-start(bf16[256,128]{1,0:T(8,128)(2,1)S(1)} %collective-permute-done.10.theirs_ref), channel_id=1, source_target_pairs={{0,1},{1,0},{2,3},{3,2},{4,5},{5,4},{6,7},{7,6},{8,9},{9,8},{10,11... | collective-permute-start | bytes 196616 | tf_op jit(solution)/shard_map/ppermute | solution.py:30
  52.5 0.0 collective-permute-done.12.next_ref
  52.5 0.9 %collective-permute-done.13.cross_ref = bf16[256,128]{1,0:T(8,128)(2,1)S(1)} collective-permute-done((bf16[256,128]{1,0:T(8,128)(2,1)S(1)}, bf16[256,128]{1,0:T(8,128)(2,1)S(1)}, u32[]{:S(2)}, u32[]{:S(2)}) %collective-permute-start.13) | collective-permute-done | bytes 65568 | tf_op jit(solution)/shard_map/ppermute | solution.py:30
  53.4 0.0 copy-done.3
  53.4 0.0 copy-start.6
  53.4 0.0 copy-start.7
  53.4 0.0 copy-start.5
  53.4 4.2 %experts.1 = (f32[256,128]{1,0:T(8,128)}, f32[8,128]{1,0:T(8,128)S(1)}) custom-call(f32[32,32]{1,0:T(8,128)S(1)} %get-tuple-element.43.order_ref, f32[8,32]{1,0:T(8,128)S(1)} %get-tuple-element.44.chooser_ref, f32[32,128]{1,0:T(8,128)S(1)} %get-tuple-element.45.member_ref, bf16[128,1024]{1,0:T(8,128)(2,1)S(1)} %get-tuple-element.46.spread_ref, ...), custom_call_target="tpu_custom_call" | custom-call | tf_op jit(solution)/shard_map/experts/pallas_call | solution.py:498
  57.7 7.5 %all-to-all-start = ((f32[256,1,128]{2,1,0:T(1,128)}), f32[256,1,128]{2,1,0:T(1,128)S(1)}, u32[]{:S(2)}, u32[]{:S(2)}) async-start(f32[256,1,128]{2,1,0:T(1,128)} %bitcast.16), calls=%async_computation | async-start | bytes 262144 | tf_op jit(solution)/shard_map/all_to_all | solution.py:516
  65.2 0.0 copy-done.6
  65.2 0.0 copy-done.7
  65.2 0.0 copy-done.5
  65.2 1.0 %multiply_add_fusion = f32[8,1,128,128]{3,2,1,0:T(8,128)} fusion(f32[8,128]{1,0:T(8,128)S(1)} %get-tuple-element.57, f32[8,128]{1,0:T(8,128)S(1)} %get-tuple-element.56, bf16[8,1,128,128]{3,2,1,0:T(8,128)(2,1)S(1)} %copy-done.5, f32[8]{0:T(128)S(1)} %exponential_bitcast_fusion, pred[8]{0:T(512)(128)(4,1)S(1)} %bitcast_compare_fusion, bf16[128,128]{1,0:T(8,128)(2,1)S(1)} %slice.13), kind=kLoop, calls=%fused_computation | loop fusion | flops 655360 | bytes 827432 | tf_op jit(solution)/shard_map/add | solution.py:532
  66.3 11.4 %all-to-all-done = f32[256,1,128]{2,1,0:T(1,128)S(1)} async-done(((f32[256,1,128]{2,1,0:T(1,128)}), f32[256,1,128]{2,1,0:T(1,128)S(1)}, u32[]{:S(2)}, u32[]{:S(2)}) %all-to-all-start) | async-done | bytes 131104 | tf_op jit(solution)/shard_map/all_to_all | solution.py:516
  77.7 0.8 %finish.1 = bf16[8,32]{1,0:T(8,128)(2,1)} custom-call(f32[32,256]{1,0:T(8,128)S(1)} %get-tuple-element.42.use_ref, f32[256,128]{1,0:T(8,128)S(1)} %bitcast.32, f32[8,128]{1,0:T(8,128)S(1)} %get-tuple-element.51.own_ref), custom_call_target="tpu_custom_call" | custom-call | tf_op jit(solution)/shard_map/finish/pallas_call | solution.py:517
  (8 shorter events, 0.1 us)
Async XLA Ops:
  0.6 38.1 %copy-start.2 = (bf16[8,2048]{1,0:T(8,128)(2,1)S(1)}, bf16[8,2048]{1,0:T(8,128)(2,1)}, u32[]{:S(2)}) copy-start(bf16[8,2048]{1,0:T(8,128)(2,1)} %resid_ref.1) | copy-start | bytes 98308
  0.6 14.7 %copy-start = (bf16[1,2,2048,128]{3,2,1,0:T(8,128)(2,1)S(1)}, bf16[1,2,2048,128]{3,2,1,0:T(8,128)(2,1)}, u32[]{:S(2)}) copy-start(bf16[1,2,2048,128]{3,2,1,0:T(8,128)(2,1)} %param.17) | copy-start | bytes 3145732
  0.7 14.7 %copy-start.1 = (bf16[128,2048]{1,0:T(8,128)(2,1)S(1)}, bf16[128,2048]{1,0:T(8,128)(2,1)}, u32[]{:S(2)}) copy-start(bf16[128,2048]{1,0:T(8,128)(2,1)} %weight_ref.1) | copy-start | bytes 1572868
  2.4 12.9 %collective-permute-start = (f32[24,128]{1,0:T(8,128)S(1)}, f32[24,128]{1,0:T(8,128)S(1)}, u32[]{:S(2)}, u32[]{:S(2)}) collective-permute-start(f32[24,128]{1,0:T(8,128)S(1)} %message.1.message_ref), channel_id=1, source_target_pairs={{0,128},{128,0},{1,129},{129,1},{2,130},{130,2},{3,131},{131,3},{4... | collective-permute-start | bytes 36872 | tf_op jit(solution)/shard_map/ppermute | solution.py:30
  15.3 32.5 %copy-start.4 = (s32[32,8]{0,1:T(8,128)S(1)}, s32[32,8]{0,1:T(8,128)}, u32[]{:S(2)}) copy-start(s32[32,8]{0,1:T(8,128)} %param.31) | copy-start | bytes 3076
  15.3 38.1 %copy-start.3 = (f32[2048]{0:T(1024)S(1)}, f32[2048]{0:T(1024)}, u32[]{:S(2)}) copy-start(f32[2048]{0:T(1024)} %param.29) | copy-start | bytes 24580
  16.7 4.7 %collective-permute-start.2 = (f32[16,8,128]{2,1,0:T(8,128)S(1)}, f32[16,8,128]{2,1,0:T(8,128)S(1)}, u32[]{:S(2)}, u32[]{:S(2)}) collective-permute-start(f32[16,8,128]{2,1,0:T(8,128)S(1)} %get-tuple-element.31), channel_id=1, source_target_pairs={{0,16},{8,24},{16,0},{24,8},{1,17},{9,25},{17,1},{25,9},{2,18},{10... | collective-permute-start | bytes 196616 | tf_op jit(solution)/shard_map/ppermute | solution.py:30
  19.5 4.3 %collective-permute-start.3 = (f32[16,8,128]{2,1,0:T(8,128)S(1)}, f32[16,8,128]{2,1,0:T(8,128)S(1)}, u32[]{:S(2)}, u32[]{:S(2)}) collective-permute-start(f32[16,8,128]{2,1,0:T(8,128)S(1)} %get-tuple-element.31), channel_id=1, source_target_pairs={{0,24},{8,16},{16,8},{24,0},{1,25},{9,17},{17,9},{25,1},{2,26},{10... | collective-permute-start | bytes 196616 | tf_op jit(solution)/shard_map/ppermute | solution.py:30
  20.4 3.5 %collective-permute-start.1 = (f32[16,8,128]{2,1,0:T(8,128)S(1)}, f32[16,8,128]{2,1,0:T(8,128)S(1)}, u32[]{:S(2)}, u32[]{:S(2)}) collective-permute-start(f32[16,8,128]{2,1,0:T(8,128)S(1)} %get-tuple-element.31), channel_id=1, source_target_pairs={{0,8},{8,0},{16,24},{24,16},{1,9},{9,1},{17,25},{25,17},{2,10},{10... | collective-permute-start | bytes 196616 | tf_op jit(solution)/shard_map/ppermute | solution.py:30
  23.9 4.7 %collective-permute-start.5 = (f32[16,8,128]{2,1,0:T(8,128)S(1)}, f32[16,8,128]{2,1,0:T(8,128)S(1)}, u32[]{:S(2)}, u32[]{:S(2)}) collective-permute-start(f32[16,8,128]{2,1,0:T(8,128)S(1)} %add_add_fusion.2), channel_id=1, source_target_pairs={{0,64},{32,96},{64,0},{96,32},{1,65},{33,97},{65,1},{97,33},{2,66}... | collective-permute-start | bytes 196616 | tf_op jit(solution)/shard_map/ppermute | solution.py:30
  26.9 5.0 %collective-permute-start.6 = (f32[16,8,128]{2,1,0:T(8,128)S(1)}, f32[16,8,128]{2,1,0:T(8,128)S(1)}, u32[]{:S(2)}, u32[]{:S(2)}) collective-permute-start(f32[16,8,128]{2,1,0:T(8,128)S(1)} %add_add_fusion.2), channel_id=1, source_target_pairs={{0,96},{32,64},{64,32},{96,0},{1,97},{33,65},{65,33},{97,1},{2,98}... | collective-permute-start | bytes 196616 | tf_op jit(solution)/shard_map/ppermute | solution.py:30
  27.7 4.3 %collective-permute-start.4 = (f32[16,8,128]{2,1,0:T(8,128)S(1)}, f32[16,8,128]{2,1,0:T(8,128)S(1)}, u32[]{:S(2)}, u32[]{:S(2)}) collective-permute-start(f32[16,8,128]{2,1,0:T(8,128)S(1)} %add_add_fusion.2), channel_id=1, source_target_pairs={{0,32},{32,0},{64,96},{96,64},{1,33},{33,1},{65,97},{97,65},{2,34}... | collective-permute-start | bytes 196616 | tf_op jit(solution)/shard_map/ppermute | solution.py:30
  32.0 4.8 %collective-permute-start.8 = (f32[16,8,128]{2,1,0:T(8,128)S(1)}, f32[16,8,128]{2,1,0:T(8,128)S(1)}, u32[]{:S(2)}, u32[]{:S(2)}) collective-permute-start(f32[16,8,128]{2,1,0:T(8,128)S(1)} %add_add_fusion.1), channel_id=1, source_target_pairs={{0,4},{2,6},{4,0},{6,2},{1,5},{3,7},{5,1},{7,3},{8,12},{10,14},{12... | collective-permute-start | bytes 196616 | tf_op jit(solution)/shard_map/ppermute | solution.py:30
  33.2 5.0 %collective-permute-start.9 = (f32[16,8,128]{2,1,0:T(8,128)S(1)}, f32[16,8,128]{2,1,0:T(8,128)S(1)}, u32[]{:S(2)}, u32[]{:S(2)}) collective-permute-start(f32[16,8,128]{2,1,0:T(8,128)S(1)} %add_add_fusion.1), channel_id=1, source_target_pairs={{0,6},{2,4},{4,2},{6,0},{1,7},{3,5},{5,3},{7,1},{8,14},{10,12},{12... | collective-permute-start | bytes 196616 | tf_op jit(solution)/shard_map/ppermute | solution.py:30
  34.9 3.8 %collective-permute-start.7 = (f32[16,8,128]{2,1,0:T(8,128)S(1)}, f32[16,8,128]{2,1,0:T(8,128)S(1)}, u32[]{:S(2)}, u32[]{:S(2)}) collective-permute-start(f32[16,8,128]{2,1,0:T(8,128)S(1)} %add_add_fusion.1), channel_id=1, source_target_pairs={{0,2},{2,0},{4,6},{6,4},{1,3},{3,1},{5,7},{7,5},{8,10},{10,8},{12,... | collective-permute-start | bytes 196616 | tf_op jit(solution)/shard_map/ppermute | solution.py:30
  38.7 9.6 %collective-permute-start.10 = (bf16[256,128]{1,0:T(8,128)(2,1)S(1)}, bf16[256,128]{1,0:T(8,128)(2,1)S(1)}, u32[]{:S(2)}, u32[]{:S(2)}) collective-permute-start(bf16[256,128]{1,0:T(8,128)(2,1)S(1)} %hidden.1.after_ref.packet_ref), channel_id=1, source_target_pairs={{0,128},{128,0},{1,129},{129,1},{2,130},{130,2},{3,131},{131,3},{4... | collective-permute-start | bytes 196616 | tf_op jit(solution)/shard_map/ppermute | solution.py:30
  41.0 6.8 %collective-permute-start.11 = (f32[8,128]{1,0:T(8,128)S(1)}, f32[8,128]{1,0:T(8,128)S(1)}, u32[]{:S(2)}, u32[]{:S(2)}) collective-permute-start(f32[8,128]{1,0:T(8,128)S(1)} %get-tuple-element.53.pack_ref), channel_id=1, source_target_pairs={{0,1},{1,0},{2,3},{3,2},{4,5},{5,4},{6,7},{7,6},{8,9},{9,8},{10,11... | collective-permute-start | bytes 12296 | tf_op jit(solution)/shard_map/ppermute | solution.py:30
  46.0 6.5 %collective-permute-start.12 = (bf16[256,128]{1,0:T(8,128)(2,1)S(1)}, bf16[256,128]{1,0:T(8,128)(2,1)S(1)}, u32[]{:S(2)}, u32[]{:S(2)}) collective-permute-start(bf16[256,128]{1,0:T(8,128)(2,1)S(1)} %hidden.1.after_ref.packet_ref), channel_id=1, source_target_pairs={{0,1},{1,0},{2,3},{3,2},{4,5},{5,4},{6,7},{7,6},{8,9},{9,8},{10,11... | collective-permute-start | bytes 196616 | tf_op jit(solution)/shard_map/ppermute | solution.py:30
  48.3 5.1 %collective-permute-start.13 = (bf16[256,128]{1,0:T(8,128)(2,1)S(1)}, bf16[256,128]{1,0:T(8,128)(2,1)S(1)}, u32[]{:S(2)}, u32[]{:S(2)}) collective-permute-start(bf16[256,128]{1,0:T(8,128)(2,1)S(1)} %collective-permute-done.10.theirs_ref), channel_id=1, source_target_pairs={{0,1},{1,0},{2,3},{3,2},{4,5},{5,4},{6,7},{7,6},{8,9},{9,8},{10,11... | collective-permute-start | bytes 196616 | tf_op jit(solution)/shard_map/ppermute | solution.py:30
  53.4 11.7 %copy-start.6 = (bf16[8,3,128]{2,0,1:T(8,128)(2,1)S(1)}, bf16[8,3,128]{2,0,1:T(8,128)(2,1)}, u32[]{:S(2)}) copy-start(bf16[8,3,128]{2,0,1:T(8,128)(2,1)} %param.22) | copy-start | bytes 18436
  53.4 11.8 %copy-start.7 = (f32[8,1]{0,1:T(1,128)S(1)}, f32[8,1]{0,1:T(1,128)}, u32[]{:S(2)}) copy-start(f32[8,1]{0,1:T(1,128)} %param.23) | copy-start | bytes 100
  53.4 11.8 %copy-start.5 = (bf16[8,1,128,128]{3,2,1,0:T(8,128)(2,1)S(1)}, bf16[8,1,128,128]{3,2,1,0:T(8,128)(2,1)}, u32[]{:S(2)}) copy-start(bf16[8,1,128,128]{3,2,1,0:T(8,128)(2,1)} %param.24) | copy-start | bytes 786436
  57.7 20.0 %all-to-all-start = ((f32[256,1,128]{2,1,0:T(1,128)}), f32[256,1,128]{2,1,0:T(1,128)S(1)}, u32[]{:S(2)}, u32[]{:S(2)}) async-start(f32[256,1,128]{2,1,0:T(1,128)} %bitcast.16), calls=%async_computation | async-start | bytes 262144 | tf_op jit(solution)/shard_map/all_to_all | solution.py:516

commit v4 on v3

--- a/solution.py
+++ b/solution.py
@@ -210,7 +210,7 @@
 
 
 def prepare_kernel(
-    pack_ref, beside_ref, turned_ref, order_ref, chooser_ref, member_ref, spread_ref, use_ref
+    pack_ref, beside_ref, turned_ref, own_rows_ref, chooser_ref, member_ref, spread_ref, use_ref
 ):
     block = own_block()
     owners = [pack_ref[0, 0], pack_ref[1, 0], beside_ref[0, 0], beside_ref[1, 0]]
@@ -223,7 +223,6 @@
         other = (blocks[j ^ 1] * 8).astype(F32) + owners[j ^ 1]
         target = jnp.where(place == j, jnp.where(row == owners[j], other, own), target)
     order = (target == iota((32, 32), 0).astype(F32)).astype(F32)
-    order_ref[...] = order
 
     expert = own_expert()
     names_own = jnp.max((turned_ref[...] == expert).astype(F32), axis=0, keepdims=True)
@@ -231,10 +230,20 @@
     upper = (iota((32, 32), 0) < iota((32, 32), 1)).astype(F32)
     rank = dot(names_own, upper)
     slots = (iota((8, 32), 0) % 4).astype(F32)
-    chooser_ref[...] = jnp.where(names_own > 0, (rank == slots).astype(F32), 0.0)
-
+    chooser = jnp.where(names_own > 0, (rank == slots).astype(F32), 0.0)
+    gathered = dot(chooser, order)
     member = named_by(turned_ref)
-    member_ref[...] = member
+    member_ref[...] = dot(chooser, member)
+
+    tile_row = iota((32, 64), 1) // 16 * 8 + iota((32, 64), 1) % 8
+    widen = (tile_row == iota((32, 64), 0)).astype(F32)
+    wide = dot(gathered, widen)
+    odd = iota((8, 64), 1) // 8 % 2 == 1
+    chooser_ref[...] = jnp.concatenate([jnp.where(odd, 0.0, wide), jnp.where(odd, wide, 0.0)], axis=0).astype(BF16)
+    first = (iota((8, 32), 1) == iota((8, 32), 0) + block * 8).astype(F32)
+    own_wide = dot(dot(first, order), widen)
+    tile = lax.axis_index("y") * 4 + lax.axis_index("x")
+    own_rows_ref[...] = jnp.where(odd == (tile % 2 == 1), own_wide, 0.0).astype(BF16)
     spread_ref[...] = (iota((128, 1024), 1) // 8 == iota((128, 1024), 0)).astype(BF16)
 
     lower = (iota((32, 32), 1) < iota((32, 32), 0)).astype(F32)
@@ -248,92 +257,67 @@
         use_ref[k * 8 : (k + 1) * 8, :] = (slot == float(k)).astype(F32)
 
 
-def fetch_kernel(after_ref, router_hbm, in_hbm, router_ref, near_ref, sems):
-    copies = [
-        pltpu.make_async_copy(router_hbm, router_ref, sems.at[0]),
-        pltpu.make_async_copy(in_hbm.at[pl.ds(0, 4096)], near_ref.at[pl.ds(0, 4096)], sems.at[1]),
-        pltpu.make_async_copy(in_hbm.at[pl.ds(8192, 4096)], near_ref.at[pl.ds(4096, 4096)], sems.at[2]),
-    ]
+def fetch_kernel(after_ref, router_hbm, in_hbm, down_hbm, router_ref, in_ref, down_ref, sems):
+    pairs = [(router_hbm, router_ref, 1), (in_hbm, in_ref, 8), (down_hbm, down_ref, 4)]
+    copies = []
+    for source, target, cuts in pairs:
+        rows = source.shape[0] // cuts
+        for i in range(cuts):
+            part = pl.ds(i * rows, rows)
+            copies.append(pltpu.make_async_copy(source.at[part], target.at[part], sems.at[len(copies)]))
     for copy in copies:
         copy.start()
     for copy in copies:
         copy.wait()
 
 
-def hidden_kernel(total_ref, message_ref, got_ref, resid_ref, fresh_ref, out_ref):
+def sum_kernel(two_ref, three_ref, one_ref, total_ref, out_ref):
+    out_ref[...] = (total_ref[...] + one_ref[...]) + (two_ref[...] + three_ref[...])
+
+
+def hidden_kernel(three_ref, two_ref, one_ref, total_ref, message_ref, got_ref, resid_ref, fresh_ref, out_ref):
     taken = iota((8, 128), 0).astype(F32) == message_ref[4:5, :]
     for pair in range(8):
         parts = []
         for c in (2 * pair, 2 * pair + 1):
             rows = resid_ref[:, c * 128 : (c + 1) * 128].astype(F32)
-            parts.append(jnp.where(taken, got_ref[8 + c : 9 + c, :], rows) + total_ref[c])
+            total = (total_ref[c] + one_ref[c]) + (two_ref[c] + three_ref[c])
+            parts.append(jnp.where(taken, got_ref[8 + c : 9 + c, :], rows) + total)
         out_ref[pair * 16 : (pair + 1) * 16, :] = jnp.concatenate(parts, axis=0).astype(BF16)
     out_ref[128:256, :] = fresh_ref[...]
 
 
 def expert_kernel(
-    order_ref, chooser_ref, member_ref, spread_ref, gain_ref, packet_ref, theirs_ref, next_ref, cross_ref, router_ref,
-    near_ref, in_hbm, down_hbm,
-    out_ref, own_ref, turn_ref, far_ref, down_ref, far_sem, down_sem,
+    own_rows_ref, chooser_ref, member_ref, spread_ref, gain_ref, packet_ref, theirs_ref, next_ref, cross_ref,
+    router_ref, in_ref, down_ref, out_ref, own_ref, turn_ref,
 ):
-    far_copies = []
-    for half in range(2):
-        for i in range(2):
-            source = in_hbm.at[pl.ds(half * 8192 + 4096 + i * 2048, 2048)]
-            target = far_ref.at[pl.ds(half * 4096 + i * 2048, 2048)]
-            far_copies.append(pltpu.make_async_copy(source, target, far_sem.at[half * 2 + i]))
-    down_copies = [
-        pltpu.make_async_copy(down_hbm.at[pl.ds(i * 128, 128)], down_ref.at[pl.ds(i * 128, 128)], down_sem.at[i])
-        for i in range(4)
-    ]
-    for i in (0, 2, 1, 3):
-        far_copies[i].start()
-    for copy in down_copies:
-        copy.start()
-    block = own_block()
     expert = own_expert()
-    order, chooser, member = order_ref[...], chooser_ref[...], member_ref[...]
-
-    hidden = []
-    for ref in (packet_ref, theirs_ref, next_ref, cross_ref):
-        two = [ref[pair * 16 : (pair + 1) * 16, :].astype(F32) for pair in range(8)]
-        hidden.append([half for both in two for half in (both[:8, :], both[8:, :])])
-    scales = []
-    for rows in hidden:
-        total = jnp.zeros((8, 128), F32)
-        for x in rows:
-            total += x * x
-        scales.append(lax.rsqrt(jnp.sum(total, axis=1, keepdims=True) * (1.0 / 2048) + 1e-06))
-    tiles = []
-    for c in range(16):
-        gain = gain_ref[:, c * 128 : (c + 1) * 128]
-        parts = [hidden[j][c] * scales[j] * gain for j in range(4)]
-        tiles.append(jnp.concatenate(parts, axis=0).astype(BF16))
-    normed = jnp.concatenate(tiles, axis=1)
-
-    choose_gathered = dot(chooser, order)
-    rows_in = dot(choose_gathered.astype(BF16), normed)
-
-    logits = dot(order, dot(normed, router_ref[...]), EXACT)
-    lanes = iota((32, 128), 1)
-    chosen = member / (1.0 + jnp.exp(-logits))
-    chosen = jnp.where(member > 0, chosen, 0.0)
-    share = jnp.sum(jnp.where(lanes == expert, chosen, 0.0), axis=1, keepdims=True)
+    packets = (packet_ref, theirs_ref, next_ref, cross_ref)
+
+    right = beside(*(jnp.concatenate([ref[p * 16 : (p + 1) * 16, :] for ref in packets], axis=0) for p in range(8)))
+    both = dot(chooser_ref[...], right)
+    tiles = [both[c % 2 * 8 : c % 2 * 8 + 8, c // 2 * 128 : (c // 2 + 1) * 128] for c in range(16)]
+    squares = tiles[0] * tiles[0]
+    for x in tiles[1:]:
+        squares += x * x
+    scale = lax.rsqrt(jnp.sum(squares, axis=1, keepdims=True) * (1.0 / 2048) + 1e-06)
+    tiles = [x * scale * gain_ref[:, c * 128 : (c + 1) * 128] for c, x in enumerate(tiles)]
+
+    logits = dot(beside(*tiles).astype(BF16), router_ref[...])
+    member = member_ref[...]
+    chosen = jnp.where(member > 0, 1.0 / (1.0 + jnp.exp(-logits)), 0.0)
+    share = jnp.sum(jnp.where(iota((8, 128), 1) == expert, chosen, 0.0), axis=1, keepdims=True)
     share = share / jnp.sum(chosen, axis=1, keepdims=True)
-    gates = dot(chooser, jnp.broadcast_to(share, (32, 128)), EXACT)
-
-    stacked = jnp.concatenate([rows_in[:, c * 128 : (c + 1) * 128] for c in range(16)], axis=0)
+    gates = jnp.where(jnp.sum(member, axis=1, keepdims=True) > 0, share, 0.0)
+
+    stacked = jnp.concatenate(tiles, axis=0)
     repeated = dot(stacked.astype(BF16), spread_ref[...])
     kind = iota((8, 1024), 1) % 8 - iota((8, 1024), 0) // 4
     pre = jnp.zeros((64, 256), F32)
     for c in range(8):
         halves = [repeated[i * 8 : (i + 1) * 8, :] for i in (c, c + 8)]
         left = jnp.concatenate([jnp.where(kind == 2 * p, half, 0.0) for half in halves for p in range(4)], axis=0)
-        if c >= 4 and c % 2 == 0:
-            far_copies[c // 2 - 2].wait()
-            far_copies[c // 2].wait()
-        source, start = (near_ref, c * 1024) if c < 4 else (far_ref, (c - 4) * 1024)
-        right = beside(source[start : start + 1024, :], source[start + 4096 : start + 5120, :])
+        right = beside(in_ref[c * 1024 : (c + 1) * 1024, :], in_ref[(c + 8) * 1024 : (c + 9) * 1024, :])
         pre += dot(left.astype(BF16), right)
     pre = pre[:32, :128] + pre[32:, 128:]
     acts = []
@@ -341,8 +325,6 @@
         both = pre[p * 8 : (p + 1) * 8, :]
         acts.append(both / (1.0 + jnp.exp(-both)) * pltpu.roll(both, 4, 0))
     act = jnp.concatenate(acts, axis=1).astype(BF16)
-    for copy in down_copies:
-        copy.wait()
     for c in range(8):
         part = dot(act, down_ref[:, c * 256 : (c + 1) * 256])
         turn_ref[2 * c] = part[:, :128] * gates
@@ -361,13 +343,7 @@
 
     tile = lax.axis_index("y") * 4 + lax.axis_index("x")
     rows = pl.ds(pl.multiple_of(tile // 2 * 16, 16), 16)
-    raw = []
-    for ref in (packet_ref, theirs_ref, next_ref, cross_ref):
-        both = ref[rows, :].astype(F32)
-        raw.append(jnp.where(tile % 2 == 0, both[:8, :], both[8:, :]))
-    raw = jnp.concatenate(raw, axis=0)
-    first = (iota((8, 32), 1) == iota((8, 32), 0) + block * 8).astype(F32)
-    mine = dot(dot(first, order).astype(BF16), raw.astype(BF16))
+    mine = dot(own_rows_ref[...], jnp.concatenate([ref[rows, :] for ref in packets], axis=0))
     deep = lax.axis_index("z")
     own = mine
     for q in range(1, 4):
@@ -454,35 +430,47 @@
     total = partial
     for axis in ("x", "y", "z"):
         parts = [swap(total, axis, flip) for flip in (1, 2, 3)]
-        total = (total + parts[0]) + (parts[1] + parts[2])
+        if axis != "z":
+            total = pl.pallas_call(
+                sum_kernel,
+                out_shape=pltpu.VMEM((16, 8, 128), F32),
+                in_specs=[VMEM] * 4,
+                out_specs=VMEM,
+                compiler_params=params(2),
+                name="sum_" + axis,
+            )(parts[1], parts[2], parts[0], total)
     packet = pl.pallas_call(
         hidden_kernel,
         out_shape=jax.ShapeDtypeStruct((256, 128), BF16),
-        in_specs=[VMEM] * 5,
+        in_specs=[VMEM] * 8,
         out_specs=VMEM,
         compiler_params=params(2),
         name="hidden",
-    )(total, message, got, resid, fresh_state)
+    )(*parts[::-1], total, message, got, resid, fresh_state)
     packet, pack = lax.optimization_barrier((packet, pack))
     theirs = swap(packet, "s", 1)
     next_door = swap(pack, "t", 1)
-    router_near, in_near = pl.pallas_call(
+    router_near, in_near, down_near = pl.pallas_call(
         fetch_kernel,
-        out_shape=(pltpu.VMEM((2048, 128), BF16), pltpu.VMEM((8192, 128), BF16)),
-        in_specs=[ANY] + [HBM] * 2,
-        out_specs=(VMEM,) * 2,
-        scratch_shapes=[pltpu.SemaphoreType.DMA((3,))],
+        out_shape=(
+            pltpu.VMEM((2048, 128), BF16),
+            pltpu.VMEM((16384, 128), BF16),
+            pltpu.VMEM((512, 2048), BF16),
+        ),
+        in_specs=[ANY] + [HBM] * 3,
+        out_specs=(VMEM,) * 3,
+        scratch_shapes=[pltpu.SemaphoreType.DMA((13,))],
         compiler_params=params(2),
         name="fetch",
-    )(packet, *stay(router, expert_in))
+    )(packet, *stay(router, expert_in, w_down[0]))
 
     beyond = swap(packet, "t", 1)
-    order, chooser, member, spread, use = pl.pallas_call(
+    own_rows, chooser, member, spread, use = pl.pallas_call(
         prepare_kernel,
         out_shape=(
-            jax.ShapeDtypeStruct((32, 32), F32),
-            jax.ShapeDtypeStruct((8, 32), F32),
-            jax.ShapeDtypeStruct((32, 128), F32),
+            jax.ShapeDtypeStruct((8, 64), BF16),
+            jax.ShapeDtypeStruct((16, 64), BF16),
+            jax.ShapeDtypeStruct((8, 128), F32),
             jax.ShapeDtypeStruct((128, 1024), BF16),
             jax.ShapeDtypeStruct((32, 256), F32),
         ),
@@ -491,27 +479,21 @@
         compiler_params=params(4),
         name="prepare",
     )(pack, next_door, routes.T)
-    theirs, router_near, in_near, order, chooser, member, spread, use = lax.optimization_barrier(
-        (theirs, router_near, in_near, order, chooser, member, spread, use)
+    theirs, router_near, in_near, down_near, own_rows, chooser, member, spread, use = lax.optimization_barrier(
+        (theirs, router_near, in_near, down_near, own_rows, chooser, member, spread, use)
     )
     cross = swap(theirs, "t", 1)
     term, own = pl.pallas_call(
         expert_kernel,
         out_shape=(jax.ShapeDtypeStruct((256, 128), F32), jax.ShapeDtypeStruct((8, 128), F32)),
-        in_specs=[VMEM] * 11 + [HBM] * 2,
+        in_specs=[VMEM] * 12,
         out_specs=(VMEM, VMEM),
-        scratch_shapes=[
-            pltpu.VMEM((16, 8, 128), F32),
-            pltpu.VMEM((8192, 128), BF16),
-            pltpu.VMEM((512, 2048), BF16),
-            pltpu.SemaphoreType.DMA((4,)),
-            pltpu.SemaphoreType.DMA((4,)),
-        ],
+        scratch_shapes=[pltpu.VMEM((16, 8, 128), F32)],
         compiler_params=params(12),
         name="experts",
     )(
-        order, chooser, member, spread, moe_gain.reshape(1, 2048), packet, theirs, beyond, cross,
-        router_near, in_near, *stay(expert_in, w_down[0]),
+        own_rows, chooser, member, spread, moe_gain.reshape(1, 2048), packet, theirs, beyond, cross,
+        router_near, in_near, down_near,
     )
     back = lax.all_to_all(term.reshape(256, 1, 128), ("s", "t", "z", "y", "x"), 0, 0, tiled=True)
     layer_out = pl.pallas_call(

time: 78.7 us -> 77.3 us (0.982)
  waiting for transfers between devices: 23.9 us -> 22.8 us
    ppermute x14, starting transfers between devices: 29.7 us -> 27.6 us  [swap(): lax.ppermute(shard, axis, [(i, i ^ flip) for i in range(lax.axis_size(axi...]
    all_to_all x1, starting transfers between devices: 7.45 us -> 8.98 us  [on_device(): lax.all_to_all(term.reshape(256, 1, 128), ('s', 't', 'z', 'y', 'x'), 0, 0...]
    pallas_call x1, Pallas kernels: 4.25 us -> 2.93 us  [on_device(): pl.pallas_call(expert_kernel, out_shape=(jax.ShapeDtypeStruct((256, 128),...]
    pallas_call x1, Pallas kernels: 1.73 us -> 3.04 us  [on_device(): pl.pallas_call(fetch_kernel, out_shape=(pltpu.VMEM((2048, 128), BF16), pl...]
    ppermute x14, waiting for transfers between devices: 12.4 us -> 11.4 us  [swap(): lax.ppermute(shard, axis, [(i, i ^ flip) for i in range(lax.axis_size(axi...]
  transfers between devices with their start and end apart: 15 -> 15, of which waited for: 9 -> 8; matrix products, arithmetic and copies ran while one was open for 1% -> 1% of each run, Pallas kernels for 8% -> 11%
where the time goes in v4:
time: 77.3 us; the launch traced here: 77.1 us
  starting transfers between devices  36.6 us (47%)
  waiting for transfers between devices  22.8 us (29%)
  Pallas kernels  14.3 us (18%)
  between operations  2.26 us (3%)
  other arithmetic  1.05 us (1%)
    ppermute x14, starting transfers between devices, swap(): lax.ppermute(shard, axis, [(i, i ^ flip) for i in range(lax.axis_size(axi...  27.6 us
    all_to_all x1, waiting for transfers between devices, on_device(): lax.all_to_all(term.reshape(256, 1, 128), ('s', 't', 'z', 'y', 'x'), 0, 0...  11.4 us
    ppermute x14, waiting for transfers between devices, swap(): lax.ppermute(shard, axis, [(i, i ^ flip) for i in range(lax.axis_size(axi...  11.4 us
    all_to_all x1, starting transfers between devices, on_device(): lax.all_to_all(term.reshape(256, 1, 128), ('s', 't', 'z', 'y', 'x'), 0, 0...  8.98 us
    pallas_call x1, Pallas kernels, on_device(): pl.pallas_call(own_rows_kernel, out_shape=(jax.ShapeDtypeStruct((8, 128),...  4.4 us
    pallas_call x1, Pallas kernels, on_device(): pl.pallas_call(fetch_kernel, out_shape=(pltpu.VMEM((2048, 128), BF16), pl...  3.04 us
    pallas_call x1, Pallas kernels, on_device(): pl.pallas_call(expert_kernel, out_shape=(jax.ShapeDtypeStruct((256, 128),...  2.93 us
  transfers between devices with their start and end apart: 15, of which 8 were waited for; matrix products, arithmetic and copies ran while one was open for 1% of the time, Pallas kernels for 11%

profile of v4, /device:TPU:1, one launch (start us, length us, event | category | flops | bytes accessed | tf_op | source)
XLA Modules:
  0.0 77.1 jit_solution(2241120131078282866)
XLA Ops:
  0.6 0.0 copy-start.2
  0.6 0.0 copy-start
  0.7 0.0 copy-start.1
  1.4 1.0 %message.1.message_ref = f32[24,128]{1,0:T(8,128)S(1)} custom-call(s32[1,1]{1,0:T(1,128)} %bitcast.29.owner_hbm, f32[1,8]{1,0:T(1,128)} %bitcast.41, bf16[3,8,128]{2,1,0:T(8,128)(2,1)} %bitcast.38, bf16[8,2048]{1,0:T(8,128)(2,1)} %resid_ref.1), custom_call_target="tpu_custom_call" | custom-call | tf_op jit(solution)/shard_map/message/pallas_call | solution.py:373
  2.4 7.8 %collective-permute-start = (f32[24,128]{1,0:T(8,128)S(1)}, f32[24,128]{1,0:T(8,128)S(1)}, u32[]{:S(2)}, u32[]{:S(2)}) collective-permute-start(f32[24,128]{1,0:T(8,128)S(1)} %message.1.message_ref), channel_id=1, source_target_pairs={{0,128},{128,0},{1,129},{129,1},{2,130},{130,2},{3,131},{131,3},{4... | collective-permute-start | bytes 36872 | tf_op jit(solution)/shard_map/ppermute | solution.py:30
  10.9 4.4 %own_rows.1 = (f32[8,128]{1,0:T(8,128)S(1)}, bf16[128,128]{1,0:T(8,128)(2,1)S(1)}) custom-call(s32[1]{0:T(128)S(6)} %copy.22.length_ref, s32[8]{0:T(128)} %live_hbm.1, f32[8]{0:T(128)} %bitcast.42, f32[16,128]{1,0:T(8,128)} %bitcast.40, bf16[3,8,128]{2,1,0:T(8,128)(2,1)} %bitcast.39, f32[2,128]{1,0:T(2,128)} %gain_hbm.3, bf16[2,2048,128]{2,1,0:T(8,128)(2,1)} %bitcast.30, ...), custom_call_target="tpu_custom_call" | custom-call | tf_op jit(solution)/shard_map/own_rows/pallas_call | solution.py:390
  15.3 0.0 collective-permute-done.got_ref
  15.3 0.0 copy-done
  15.3 0.0 copy-done.1
  15.3 1.4 %guest.1 = (f32[16,8,128]{2,1,0:T(8,128)S(1)}, f32[8,128]{1,0:T(8,128)S(1)}) custom-call(s32[1]{0:T(128)S(6)} %copy.22.length_ref, f32[24,128]{1,0:T(8,128)S(1)} %message.1.message_ref, f32[24,128]{1,0:T(8,128)S(1)} %collective-permute-done.got_ref, f32[8,128]{1,0:T(8,128)S(1)} %get-tuple-element.31.head_ref, ...), custom_call_target="tpu_custom_call" | custom-call | tf_op jit(solution)/shard_map/guest/pallas_call | solution.py:419
  16.7 0.0 copy-start.4
  16.7 0.0 copy-start.3
  16.7 2.8 %collective-permute-start.1 = (f32[16,8,128]{2,1,0:T(8,128)S(1)}, f32[16,8,128]{2,1,0:T(8,128)S(1)}, u32[]{:S(2)}, u32[]{:S(2)}) collective-permute-start(f32[16,8,128]{2,1,0:T(8,128)S(1)} %get-tuple-element.33.total_ref), channel_id=1, source_target_pairs={{0,16},{8,24},{16,0},{24,8},{1,17},{9,25},{17,1},{25,9},{2,18},{10... | collective-permute-start | bytes 196616 | tf_op jit(solution)/shard_map/ppermute | solution.py:30
  19.5 0.9 %collective-permute-start.2 = (f32[16,8,128]{2,1,0:T(8,128)S(1)}, f32[16,8,128]{2,1,0:T(8,128)S(1)}, u32[]{:S(2)}, u32[]{:S(2)}) collective-permute-start(f32[16,8,128]{2,1,0:T(8,128)S(1)} %get-tuple-element.33.total_ref), channel_id=1, source_target_pairs={{0,24},{8,16},{16,8},{24,0},{1,25},{9,17},{17,9},{25,1},{2,26},{10... | collective-permute-start | bytes 196616 | tf_op jit(solution)/shard_map/ppermute | solution.py:30
  20.4 0.0 collective-permute-start.3
  20.4 1.0 %collective-permute-done.1.two_ref = f32[16,8,128]{2,1,0:T(8,128)S(1)} collective-permute-done((f32[16,8,128]{2,1,0:T(8,128)S(1)}, f32[16,8,128]{2,1,0:T(8,128)S(1)}, u32[]{:S(2)}, u32[]{:S(2)}) %collective-permute-start.1) | collective-permute-done | bytes 65568 | tf_op jit(solution)/shard_map/ppermute | solution.py:30
  21.4 2.4 %collective-permute-done.2.three_ref = f32[16,8,128]{2,1,0:T(8,128)S(1)} collective-permute-done((f32[16,8,128]{2,1,0:T(8,128)S(1)}, f32[16,8,128]{2,1,0:T(8,128)S(1)}, u32[]{:S(2)}, u32[]{:S(2)}) %collective-permute-start.2) | collective-permute-done | bytes 65568 | tf_op jit(solution)/shard_map/ppermute | solution.py:30
  23.9 0.0 collective-permute-done.3.one_ref
  23.9 3.0 %collective-permute-start.4 = (f32[16,8,128]{2,1,0:T(8,128)S(1)}, f32[16,8,128]{2,1,0:T(8,128)S(1)}, u32[]{:S(2)}, u32[]{:S(2)}) collective-permute-start(f32[16,8,128]{2,1,0:T(8,128)S(1)} %sum_x.1.total_ref), channel_id=1, source_target_pairs={{0,64},{32,96},{64,0},{96,32},{1,65},{33,97},{65,1},{97,33},{2,66}... | collective-permute-start | bytes 196616 | tf_op jit(solution)/shard_map/ppermute | solution.py:30
  26.9 0.8 %collective-permute-start.5 = (f32[16,8,128]{2,1,0:T(8,128)S(1)}, f32[16,8,128]{2,1,0:T(8,128)S(1)}, u32[]{:S(2)}, u32[]{:S(2)}) collective-permute-start(f32[16,8,128]{2,1,0:T(8,128)S(1)} %sum_x.1.total_ref), channel_id=1, source_target_pairs={{0,96},{32,64},{64,32},{96,0},{1,97},{33,65},{65,33},{97,1},{2,98}... | collective-permute-start | bytes 196616 | tf_op jit(solution)/shard_map/ppermute | solution.py:30
  27.7 0.0 collective-permute-start.6
  27.7 0.9 %collective-permute-done.4.two_ref = f32[16,8,128]{2,1,0:T(8,128)S(1)} collective-permute-done((f32[16,8,128]{2,1,0:T(8,128)S(1)}, f32[16,8,128]{2,1,0:T(8,128)S(1)}, u32[]{:S(2)}, u32[]{:S(2)}) %collective-permute-start.4) | collective-permute-done | bytes 65568 | tf_op jit(solution)/shard_map/ppermute | solution.py:30
  28.6 3.3 %collective-permute-done.5.three_ref = f32[16,8,128]{2,1,0:T(8,128)S(1)} collective-permute-done((f32[16,8,128]{2,1,0:T(8,128)S(1)}, f32[16,8,128]{2,1,0:T(8,128)S(1)}, u32[]{:S(2)}, u32[]{:S(2)}) %collective-permute-start.5) | collective-permute-done | bytes 65568 | tf_op jit(solution)/shard_map/ppermute | solution.py:30
  31.9 0.0 collective-permute-done.6.one_ref
  32.0 1.7 %collective-permute-start.7 = (f32[16,8,128]{2,1,0:T(8,128)S(1)}, f32[16,8,128]{2,1,0:T(8,128)S(1)}, u32[]{:S(2)}, u32[]{:S(2)}) collective-permute-start(f32[16,8,128]{2,1,0:T(8,128)S(1)} %sum_y.1.total_ref), channel_id=1, source_target_pairs={{0,6},{2,4},{4,2},{6,0},{1,7},{3,5},{5,3},{7,1},{8,14},{10,12},{12... | collective-permute-start | bytes 196616 | tf_op jit(solution)/shard_map/ppermute | solution.py:30
  33.7 0.3 collective-permute-start.8
  34.0 1.6 %collective-permute-start.9 = (f32[16,8,128]{2,1,0:T(8,128)S(1)}, f32[16,8,128]{2,1,0:T(8,128)S(1)}, u32[]{:S(2)}, u32[]{:S(2)}) collective-permute-start(f32[16,8,128]{2,1,0:T(8,128)S(1)} %sum_y.1.total_ref), channel_id=1, source_target_pairs={{0,2},{2,0},{4,6},{6,4},{1,3},{3,1},{5,7},{7,5},{8,10},{10,8},{12,... | collective-permute-start | bytes 196616 | tf_op jit(solution)/shard_map/ppermute | solution.py:30
  35.6 1.4 %collective-permute-done.7.three_ref = f32[16,8,128]{2,1,0:T(8,128)S(1)} collective-permute-done((f32[16,8,128]{2,1,0:T(8,128)S(1)}, f32[16,8,128]{2,1,0:T(8,128)S(1)}, u32[]{:S(2)}, u32[]{:S(2)}) %collective-permute-start.7) | collective-permute-done | bytes 65568 | tf_op jit(solution)/shard_map/ppermute | solution.py:30
  37.0 1.4 %collective-permute-done.8.two_ref = f32[16,8,128]{2,1,0:T(8,128)S(1)} collective-permute-done((f32[16,8,128]{2,1,0:T(8,128)S(1)}, f32[16,8,128]{2,1,0:T(8,128)S(1)}, u32[]{:S(2)}, u32[]{:S(2)}) %collective-permute-start.8) | collective-permute-done | bytes 65568 | tf_op jit(solution)/shard_map/ppermute | solution.py:30
  38.4 0.0 collective-permute-done.9.one_ref
  38.4 0.0 copy-done.2
  38.4 2.3 %collective-permute-start.10 = (bf16[256,128]{1,0:T(8,128)(2,1)S(1)}, bf16[256,128]{1,0:T(8,128)(2,1)S(1)}, u32[]{:S(2)}, u32[]{:S(2)}) collective-permute-start(bf16[256,128]{1,0:T(8,128)(2,1)S(1)} %hidden.1.after_ref.packet_ref), channel_id=1, source_target_pairs={{0,128},{128,0},{1,129},{129,1},{2,130},{130,2},{3,131},{131,3},{4... | collective-permute-start | bytes 196616 | tf_op jit(solution)/shard_map/ppermute | solution.py:30
  40.7 4.6 %collective-permute-start.11 = (f32[8,128]{1,0:T(8,128)S(1)}, f32[8,128]{1,0:T(8,128)S(1)}, u32[]{:S(2)}, u32[]{:S(2)}) collective-permute-start(f32[8,128]{1,0:T(8,128)S(1)} %get-tuple-element.57.pack_ref), channel_id=1, source_target_pairs={{0,1},{1,0},{2,3},{3,2},{4,5},{5,4},{6,7},{7,6},{8,9},{9,8},{10,11... | collective-permute-start | bytes 12296 | tf_op jit(solution)/shard_map/ppermute | solution.py:30
  45.3 0.0 collective-permute-start.12
  45.3 3.0 %fetch.1 = (bf16[2048,128]{1,0:T(8,128)(2,1)S(1)}, bf16[16384,128]{1,0:T(8,128)(2,1)S(1)}, bf16[512,2048]{1,0:T(8,128)(2,1)S(1)}) custom-call(bf16[256,128]{1,0:T(8,128)(2,1)S(1)} %hidden.1.after_ref.packet_ref, bf16[2048,128]{1,0:T(8,128)(2,1)} %router_hbm.1, bf16[16384,128]{1,0:T(8,128)(2,1)} %bitcast.35, bf16[512,2048]{1,0:T(8,128)(2,1)} %bitcast.36), custom_call_target="tpu_custom_call" | custom-call | tf_op jit(solution)/shard_map/fetch/pallas_call | solution.py:453
  48.3 0.0 copy-start.6
  48.3 0.0 copy-start.7
  48.3 0.0 copy-start.5
  48.3 0.0 collective-permute-done.11.beside_ref
  48.4 0.0 copy-done.4
  48.4 0.7 prepare.1
  49.1 0.0 collective-permute-done.10.theirs_ref
  49.1 1.8 %collective-permute-start.13 = (bf16[256,128]{1,0:T(8,128)(2,1)S(1)}, bf16[256,128]{1,0:T(8,128)(2,1)S(1)}, u32[]{:S(2)}, u32[]{:S(2)}) collective-permute-start(bf16[256,128]{1,0:T(8,128)(2,1)S(1)} %collective-permute-done.10.theirs_ref), channel_id=1, source_target_pairs={{0,1},{1,0},{2,3},{3,2},{4,5},{5,4},{6,7},{7,6},{8,9},{9,8},{10,11... | collective-permute-start | bytes 196616 | tf_op jit(solution)/shard_map/ppermute | solution.py:30
  50.9 0.0 collective-permute-done.12.next_ref
  50.9 0.9 %collective-permute-done.13.cross_ref = bf16[256,128]{1,0:T(8,128)(2,1)S(1)} collective-permute-done((bf16[256,128]{1,0:T(8,128)(2,1)S(1)}, bf16[256,128]{1,0:T(8,128)(2,1)S(1)}, u32[]{:S(2)}, u32[]{:S(2)}) %collective-permute-start.13) | collective-permute-done | bytes 65568 | tf_op jit(solution)/shard_map/ppermute | solution.py:30
  51.8 0.0 copy-done.3
  51.8 2.9 %experts.1 = (f32[256,128]{1,0:T(8,128)}, f32[8,128]{1,0:T(8,128)S(1)}) custom-call(bf16[8,64]{1,0:T(8,128)(2,1)S(1)} %get-tuple-element.46.own_rows_ref, bf16[16,64]{1,0:T(8,128)(2,1)S(1)} %get-tuple-element.47.chooser_ref, f32[8,128]{1,0:T(8,128)S(1)} %get-tuple-element.48.member_ref, bf16[128,1024]{1,0:T(8,128)(2,1)S(1)} %get-tuple-element.49.spread_ref, ...), custom_call_target="tpu_custom_call" | custom-call | tf_op jit(solution)/shard_map/experts/pallas_call | solution.py:486
  54.8 9.0 %all-to-all-start = ((f32[256,1,128]{2,1,0:T(1,128)}), f32[256,1,128]{2,1,0:T(1,128)S(1)}, u32[]{:S(2)}, u32[]{:S(2)}) async-start(f32[256,1,128]{2,1,0:T(1,128)} %bitcast.14), calls=%async_computation | async-start | bytes 262144 | tf_op jit(solution)/shard_map/all_to_all | solution.py:498
  63.7 0.0 copy-done.6
  63.8 0.0 copy-done.7
  63.8 0.0 copy-done.5
  63.8 1.0 %multiply_add_fusion = f32[8,1,128,128]{3,2,1,0:T(8,128)} fusion(f32[8,128]{1,0:T(8,128)S(1)} %get-tuple-element.61, f32[8,128]{1,0:T(8,128)S(1)} %get-tuple-element.60, bf16[8,1,128,128]{3,2,1,0:T(8,128)(2,1)S(1)} %copy-done.5, f32[8]{0:T(128)S(1)} %exponential_bitcast_fusion, pred[8]{0:T(512)(128)(4,1)S(1)} %bitcast_compare_fusion, bf16[128,128]{1,0:T(8,128)(2,1)S(1)} %slice.13), kind=kLoop, calls=%fused_computation | loop fusion | flops 655360 | bytes 827432 | tf_op jit(solution)/shard_map/add | solution.py:514
  64.8 11.4 %all-to-all-done = f32[256,1,128]{2,1,0:T(1,128)S(1)} async-done(((f32[256,1,128]{2,1,0:T(1,128)}), f32[256,1,128]{2,1,0:T(1,128)S(1)}, u32[]{:S(2)}, u32[]{:S(2)}) %all-to-all-start) | async-done | bytes 131104 | tf_op jit(solution)/shard_map/all_to_all | solution.py:498
  76.3 0.8 %finish.1 = bf16[8,32]{1,0:T(8,128)(2,1)} custom-call(f32[32,256]{1,0:T(8,128)S(1)} %get-tuple-element.45.use_ref, f32[256,128]{1,0:T(8,128)S(1)} %bitcast.32, f32[8,128]{1,0:T(8,128)S(1)} %get-tuple-element.55.own_ref), custom_call_target="tpu_custom_call" | custom-call | tf_op jit(solution)/shard_map/finish/pallas_call | solution.py:499
  (7 shorter events, 0.1 us)
Async XLA Ops:
  0.6 37.7 %copy-start.2 = (bf16[8,2048]{1,0:T(8,128)(2,1)S(1)}, bf16[8,2048]{1,0:T(8,128)(2,1)}, u32[]{:S(2)}) copy-start(bf16[8,2048]{1,0:T(8,128)(2,1)} %resid_ref.1) | copy-start | bytes 98308
  0.6 14.7 %copy-start = (bf16[1,2,2048,128]{3,2,1,0:T(8,128)(2,1)S(1)}, bf16[1,2,2048,128]{3,2,1,0:T(8,128)(2,1)}, u32[]{:S(2)}) copy-start(bf16[1,2,2048,128]{3,2,1,0:T(8,128)(2,1)} %param.17) | copy-start | bytes 3145732
  0.7 14.7 %copy-start.1 = (bf16[128,2048]{1,0:T(8,128)(2,1)S(1)}, bf16[128,2048]{1,0:T(8,128)(2,1)}, u32[]{:S(2)}) copy-start(bf16[128,2048]{1,0:T(8,128)(2,1)} %weight_ref.1) | copy-start | bytes 1572868
  2.4 12.9 %collective-permute-start = (f32[24,128]{1,0:T(8,128)S(1)}, f32[24,128]{1,0:T(8,128)S(1)}, u32[]{:S(2)}, u32[]{:S(2)}) collective-permute-start(f32[24,128]{1,0:T(8,128)S(1)} %message.1.message_ref), channel_id=1, source_target_pairs={{0,128},{128,0},{1,129},{129,1},{2,130},{130,2},{3,131},{131,3},{4... | collective-permute-start | bytes 36872 | tf_op jit(solution)/shard_map/ppermute | solution.py:30
  16.7 31.7 %copy-start.4 = (s32[32,8]{0,1:T(8,128)S(1)}, s32[32,8]{0,1:T(8,128)}, u32[]{:S(2)}) copy-start(s32[32,8]{0,1:T(8,128)} %param.31) | copy-start | bytes 3076
  16.7 35.1 %copy-start.3 = (f32[2048]{0:T(1024)S(1)}, f32[2048]{0:T(1024)}, u32[]{:S(2)}) copy-start(f32[2048]{0:T(1024)} %param.29) | copy-start | bytes 24580
  16.7 4.7 %collective-permute-start.1 = (f32[16,8,128]{2,1,0:T(8,128)S(1)}, f32[16,8,128]{2,1,0:T(8,128)S(1)}, u32[]{:S(2)}, u32[]{:S(2)}) collective-permute-start(f32[16,8,128]{2,1,0:T(8,128)S(1)} %get-tuple-element.33.total_ref), channel_id=1, source_target_pairs={{0,16},{8,24},{16,0},{24,8},{1,17},{9,25},{17,1},{25,9},{2,18},{10... | collective-permute-start | bytes 196616 | tf_op jit(solution)/shard_map/ppermute | solution.py:30
  19.5 4.3 %collective-permute-start.2 = (f32[16,8,128]{2,1,0:T(8,128)S(1)}, f32[16,8,128]{2,1,0:T(8,128)S(1)}, u32[]{:S(2)}, u32[]{:S(2)}) collective-permute-start(f32[16,8,128]{2,1,0:T(8,128)S(1)} %get-tuple-element.33.total_ref), channel_id=1, source_target_pairs={{0,24},{8,16},{16,8},{24,0},{1,25},{9,17},{17,9},{25,1},{2,26},{10... | collective-permute-start | bytes 196616 | tf_op jit(solution)/shard_map/ppermute | solution.py:30
  20.4 3.5 %collective-permute-start.3 = (f32[16,8,128]{2,1,0:T(8,128)S(1)}, f32[16,8,128]{2,1,0:T(8,128)S(1)}, u32[]{:S(2)}, u32[]{:S(2)}) collective-permute-start(f32[16,8,128]{2,1,0:T(8,128)S(1)} %get-tuple-element.33.total_ref), channel_id=1, source_target_pairs={{0,8},{8,0},{16,24},{24,16},{1,9},{9,1},{17,25},{25,17},{2,10},{10... | collective-permute-start | bytes 196616 | tf_op jit(solution)/shard_map/ppermute | solution.py:30
  23.9 4.7 %collective-permute-start.4 = (f32[16,8,128]{2,1,0:T(8,128)S(1)}, f32[16,8,128]{2,1,0:T(8,128)S(1)}, u32[]{:S(2)}, u32[]{:S(2)}) collective-permute-start(f32[16,8,128]{2,1,0:T(8,128)S(1)} %sum_x.1.total_ref), channel_id=1, source_target_pairs={{0,64},{32,96},{64,0},{96,32},{1,65},{33,97},{65,1},{97,33},{2,66}... | collective-permute-start | bytes 196616 | tf_op jit(solution)/shard_map/ppermute | solution.py:30
  26.9 5.0 %collective-permute-start.5 = (f32[16,8,128]{2,1,0:T(8,128)S(1)}, f32[16,8,128]{2,1,0:T(8,128)S(1)}, u32[]{:S(2)}, u32[]{:S(2)}) collective-permute-start(f32[16,8,128]{2,1,0:T(8,128)S(1)} %sum_x.1.total_ref), channel_id=1, source_target_pairs={{0,96},{32,64},{64,32},{96,0},{1,97},{33,65},{65,33},{97,1},{2,98}... | collective-permute-start | bytes 196616 | tf_op jit(solution)/shard_map/ppermute | solution.py:30
  27.7 4.3 %collective-permute-start.6 = (f32[16,8,128]{2,1,0:T(8,128)S(1)}, f32[16,8,128]{2,1,0:T(8,128)S(1)}, u32[]{:S(2)}, u32[]{:S(2)}) collective-permute-start(f32[16,8,128]{2,1,0:T(8,128)S(1)} %sum_x.1.total_ref), channel_id=1, source_target_pairs={{0,32},{32,0},{64,96},{96,64},{1,33},{33,1},{65,97},{97,65},{2,34}... | collective-permute-start | bytes 196616 | tf_op jit(solution)/shard_map/ppermute | solution.py:30
  32.0 5.0 %collective-permute-start.7 = (f32[16,8,128]{2,1,0:T(8,128)S(1)}, f32[16,8,128]{2,1,0:T(8,128)S(1)}, u32[]{:S(2)}, u32[]{:S(2)}) collective-permute-start(f32[16,8,128]{2,1,0:T(8,128)S(1)} %sum_y.1.total_ref), channel_id=1, source_target_pairs={{0,6},{2,4},{4,2},{6,0},{1,7},{3,5},{5,3},{7,1},{8,14},{10,12},{12... | collective-permute-start | bytes 196616 | tf_op jit(solution)/shard_map/ppermute | solution.py:30
  33.7 4.7 %collective-permute-start.8 = (f32[16,8,128]{2,1,0:T(8,128)S(1)}, f32[16,8,128]{2,1,0:T(8,128)S(1)}, u32[]{:S(2)}, u32[]{:S(2)}) collective-permute-start(f32[16,8,128]{2,1,0:T(8,128)S(1)} %sum_y.1.total_ref), channel_id=1, source_target_pairs={{0,4},{2,6},{4,0},{6,2},{1,5},{3,7},{5,1},{7,3},{8,12},{10,14},{12... | collective-permute-start | bytes 196616 | tf_op jit(solution)/shard_map/ppermute | solution.py:30
  34.0 4.4 %collective-permute-start.9 = (f32[16,8,128]{2,1,0:T(8,128)S(1)}, f32[16,8,128]{2,1,0:T(8,128)S(1)}, u32[]{:S(2)}, u32[]{:S(2)}) collective-permute-start(f32[16,8,128]{2,1,0:T(8,128)S(1)} %sum_y.1.total_ref), channel_id=1, source_target_pairs={{0,2},{2,0},{4,6},{6,4},{1,3},{3,1},{5,7},{7,5},{8,10},{10,8},{12,... | collective-permute-start | bytes 196616 | tf_op jit(solution)/shard_map/ppermute | solution.py:30
  38.4 10.7 %collective-permute-start.10 = (bf16[256,128]{1,0:T(8,128)(2,1)S(1)}, bf16[256,128]{1,0:T(8,128)(2,1)S(1)}, u32[]{:S(2)}, u32[]{:S(2)}) collective-permute-start(bf16[256,128]{1,0:T(8,128)(2,1)S(1)} %hidden.1.after_ref.packet_ref), channel_id=1, source_target_pairs={{0,128},{128,0},{1,129},{129,1},{2,130},{130,2},{3,131},{131,3},{4... | collective-permute-start | bytes 196616 | tf_op jit(solution)/shard_map/ppermute | solution.py:30
  40.7 7.7 %collective-permute-start.11 = (f32[8,128]{1,0:T(8,128)S(1)}, f32[8,128]{1,0:T(8,128)S(1)}, u32[]{:S(2)}, u32[]{:S(2)}) collective-permute-start(f32[8,128]{1,0:T(8,128)S(1)} %get-tuple-element.57.pack_ref), channel_id=1, source_target_pairs={{0,1},{1,0},{2,3},{3,2},{4,5},{5,4},{6,7},{7,6},{8,9},{9,8},{10,11... | collective-permute-start | bytes 12296 | tf_op jit(solution)/shard_map/ppermute | solution.py:30
  45.3 5.7 %collective-permute-start.12 = (bf16[256,128]{1,0:T(8,128)(2,1)S(1)}, bf16[256,128]{1,0:T(8,128)(2,1)S(1)}, u32[]{:S(2)}, u32[]{:S(2)}) collective-permute-start(bf16[256,128]{1,0:T(8,128)(2,1)S(1)} %hidden.1.after_ref.packet_ref), channel_id=1, source_target_pairs={{0,1},{1,0},{2,3},{3,2},{4,5},{5,4},{6,7},{7,6},{8,9},{9,8},{10,11... | collective-permute-start | bytes 196616 | tf_op jit(solution)/shard_map/ppermute | solution.py:30
  48.3 15.4 %copy-start.6 = (bf16[8,3,128]{2,0,1:T(8,128)(2,1)S(1)}, bf16[8,3,128]{2,0,1:T(8,128)(2,1)}, u32[]{:S(2)}) copy-start(bf16[8,3,128]{2,0,1:T(8,128)(2,1)} %param.22) | copy-start | bytes 18436
  48.3 15.5 %copy-start.7 = (f32[8,1]{0,1:T(1,128)S(1)}, f32[8,1]{0,1:T(1,128)}, u32[]{:S(2)}) copy-start(f32[8,1]{0,1:T(1,128)} %param.23) | copy-start | bytes 100
  48.3 15.5 %copy-start.5 = (bf16[8,1,128,128]{3,2,1,0:T(8,128)(2,1)S(1)}, bf16[8,1,128,128]{3,2,1,0:T(8,128)(2,1)}, u32[]{:S(2)}) copy-start(bf16[8,1,128,128]{3,2,1,0:T(8,128)(2,1)} %param.24) | copy-start | bytes 786436
  49.1 2.7 %collective-permute-start.13 = (bf16[256,128]{1,0:T(8,128)(2,1)S(1)}, bf16[256,128]{1,0:T(8,128)(2,1)S(1)}, u32[]{:S(2)}, u32[]{:S(2)}) collective-permute-start(bf16[256,128]{1,0:T(8,128)(2,1)S(1)} %collective-permute-done.10.theirs_ref), channel_id=1, source_target_pairs={{0,1},{1,0},{2,3},{3,2},{4,5},{5,4},{6,7},{7,6},{8,9},{9,8},{10,11... | collective-permute-start | bytes 196616 | tf_op jit(solution)/shard_map/ppermute | solution.py:30
  54.8 21.5 %all-to-all-start = ((f32[256,1,128]{2,1,0:T(1,128)}), f32[256,1,128]{2,1,0:T(1,128)S(1)}, u32[]{:S(2)}, u32[]{:S(2)}) async-start(f32[256,1,128]{2,1,0:T(1,128)} %bitcast.14), calls=%async_computation | async-start | bytes 262144 | tf_op jit(solution)/shard_map/all_to_all | solution.py:498

commit v5 on v4

--- a/solution.py
+++ b/solution.py
@@ -1,3 +1,5 @@
+import functools
+
 import jax
 import jax.numpy as jnp
 from jax import lax
@@ -271,11 +273,12 @@
         copy.wait()
 
 
-def sum_kernel(two_ref, three_ref, one_ref, total_ref, out_ref):
-    out_ref[...] = (total_ref[...] + one_ref[...]) + (two_ref[...] + three_ref[...])
-
-
-def hidden_kernel(three_ref, two_ref, one_ref, total_ref, message_ref, got_ref, resid_ref, fresh_ref, out_ref):
+def sum_kernel(flips, a_ref, b_ref, c_ref, total_ref, out_ref):
+    part = dict(zip(flips, (a_ref, b_ref, c_ref)))
+    out_ref[...] = (total_ref[...] + part[1][...]) + (part[2][...] + part[3][...])
+
+
+def hidden_kernel(two_ref, one_ref, three_ref, total_ref, message_ref, got_ref, resid_ref, fresh_ref, out_ref):
     taken = iota((8, 128), 0).astype(F32) == message_ref[4:5, :]
     for pair in range(8):
         parts = []
@@ -428,17 +431,17 @@
 
     expert_in = w_in[0].reshape(2048, 2, 4, 128).transpose(0, 2, 1, 3).reshape(16384, 128)
     total = partial
-    for axis in ("x", "y", "z"):
-        parts = [swap(total, axis, flip) for flip in (1, 2, 3)]
-        if axis != "z":
+    for axis, flips in (("x", (2, 1, 3)), ("z", (3, 2, 1)), ("y", (2, 1, 3))):
+        parts = [swap(total, axis, flip) for flip in flips]
+        if axis != "y":
             total = pl.pallas_call(
-                sum_kernel,
+                functools.partial(sum_kernel, flips),
                 out_shape=pltpu.VMEM((16, 8, 128), F32),
                 in_specs=[VMEM] * 4,
                 out_specs=VMEM,
                 compiler_params=params(2),
                 name="sum_" + axis,
-            )(parts[1], parts[2], parts[0], total)
+            )(*parts, total)
     packet = pl.pallas_call(
         hidden_kernel,
         out_shape=jax.ShapeDtypeStruct((256, 128), BF16),
@@ -446,7 +449,7 @@
         out_specs=VMEM,
         compiler_params=params(2),
         name="hidden",
-    )(*parts[::-1], total, message, got, resid, fresh_state)
+    )(*parts, total, message, got, resid, fresh_state)
     packet, pack = lax.optimization_barrier((packet, pack))
     theirs = swap(packet, "s", 1)
     next_door = swap(pack, "t", 1)

time: 77.3 us -> 75 us (0.970)
  starting transfers between devices: 36.6 us -> 33.9 us
    all_to_all x1, starting transfers between devices: 8.98 us -> 5.32 us  [on_device(): lax.all_to_all(term.reshape(256, 1, 128), ('s', 't', 'z', 'y', 'x'), 0, 0...]
    ppermute x14, starting transfers between devices: 27.6 us -> 28.6 us  [swap(): lax.ppermute(shard, axis, [(i, i ^ flip) for i in range(lax.axis_size(axi...]
  transfers between devices with their start and end apart: 15 -> 15, of which waited for: 8 -> 10; matrix products, arithmetic and copies ran while one was open for 1% -> 1% of each run, Pallas kernels for 11% -> 11%
where the time goes in v5:
time: 75 us; the launch traced here: 74.8 us
  starting transfers between devices  33.9 us (45%)
  waiting for transfers between devices  23.3 us (31%)
  Pallas kernels  14.3 us (19%)
  between operations  2.26 us (3%)
  other arithmetic  1.05 us (1%)
    ppermute x14, starting transfers between devices, swap(): lax.ppermute(shard, axis, [(i, i ^ flip) for i in range(lax.axis_size(axi...  28.6 us
    ppermute x14, waiting for transfers between devices, swap(): lax.ppermute(shard, axis, [(i, i ^ flip) for i in range(lax.axis_size(axi...  11.7 us
    all_to_all x1, waiting for transfers between devices, on_device(): lax.all_to_all(term.reshape(256, 1, 128), ('s', 't', 'z', 'y', 'x'), 0, 0...  11.6 us
    all_to_all x1, starting transfers between devices, on_device(): lax.all_to_all(term.reshape(256, 1, 128), ('s', 't', 'z', 'y', 'x'), 0, 0...  5.32 us
    pallas_call x1, Pallas kernels, on_device(): pl.pallas_call(own_rows_kernel, out_shape=(jax.ShapeDtypeStruct((8, 128),...  4.4 us
    pallas_call x1, Pallas kernels, on_device(): pl.pallas_call(fetch_kernel, out_shape=(pltpu.VMEM((2048, 128), BF16), pl...  3.04 us
    pallas_call x1, Pallas kernels, on_device(): pl.pallas_call(expert_kernel, out_shape=(jax.ShapeDtypeStruct((256, 128),...  2.93 us
  transfers between devices with their start and end apart: 15, of which 10 were waited for; matrix products, arithmetic and copies ran while one was open for 1% of the time, Pallas kernels for 11%

profile of v5, /device:TPU:1, one launch (start us, length us, event | category | flops | bytes accessed | tf_op | source)
XLA Modules:
  0.0 74.8 jit_solution(12919540641538523135)
XLA Ops:
  0.6 0.0 copy-start.2
  0.6 0.0 copy-start
  0.7 0.0 copy-start.1
  1.4 1.0 %message.1.message_ref = f32[24,128]{1,0:T(8,128)S(1)} custom-call(s32[1,1]{1,0:T(1,128)} %bitcast.29.owner_hbm, f32[1,8]{1,0:T(1,128)} %bitcast.41, bf16[3,8,128]{2,1,0:T(8,128)(2,1)} %bitcast.38, bf16[8,2048]{1,0:T(8,128)(2,1)} %resid_ref.1), custom_call_target="tpu_custom_call" | custom-call | tf_op jit(solution)/shard_map/message/pallas_call | solution.py:376
  2.4 7.8 %collective-permute-start = (f32[24,128]{1,0:T(8,128)S(1)}, f32[24,128]{1,0:T(8,128)S(1)}, u32[]{:S(2)}, u32[]{:S(2)}) collective-permute-start(f32[24,128]{1,0:T(8,128)S(1)} %message.1.message_ref), channel_id=1, source_target_pairs={{0,128},{128,0},{1,129},{129,1},{2,130},{130,2},{3,131},{131,3},{4... | collective-permute-start | bytes 36872 | tf_op jit(solution)/shard_map/ppermute | solution.py:32
  10.9 4.4 %own_rows.1 = (f32[8,128]{1,0:T(8,128)S(1)}, bf16[128,128]{1,0:T(8,128)(2,1)S(1)}) custom-call(s32[1]{0:T(128)S(6)} %copy.22.length_ref, s32[8]{0:T(128)} %live_hbm.1, f32[8]{0:T(128)} %bitcast.42, f32[16,128]{1,0:T(8,128)} %bitcast.40, bf16[3,8,128]{2,1,0:T(8,128)(2,1)} %bitcast.39, f32[2,128]{1,0:T(2,128)} %gain_hbm.3, bf16[2,2048,128]{2,1,0:T(8,128)(2,1)} %bitcast.30, ...), custom_call_target="tpu_custom_call" | custom-call | tf_op jit(solution)/shard_map/own_rows/pallas_call | solution.py:393
  15.3 0.0 collective-permute-done.got_ref
  15.3 0.0 copy-done
  15.3 0.0 copy-done.1
  15.3 1.4 %guest.1 = (f32[16,8,128]{2,1,0:T(8,128)S(1)}, f32[8,128]{1,0:T(8,128)S(1)}) custom-call(s32[1]{0:T(128)S(6)} %copy.22.length_ref, f32[24,128]{1,0:T(8,128)S(1)} %message.1.message_ref, f32[24,128]{1,0:T(8,128)S(1)} %collective-permute-done.got_ref, f32[8,128]{1,0:T(8,128)S(1)} %get-tuple-element.31.head_ref, ...), custom_call_target="tpu_custom_call" | custom-call | tf_op jit(solution)/shard_map/guest/pallas_call | solution.py:422
  16.7 0.0 copy-start.4
  16.7 0.0 copy-start.3
  16.7 2.8 %collective-permute-start.1 = (f32[16,8,128]{2,1,0:T(8,128)S(1)}, f32[16,8,128]{2,1,0:T(8,128)S(1)}, u32[]{:S(2)}, u32[]{:S(2)}) collective-permute-start(f32[16,8,128]{2,1,0:T(8,128)S(1)} %get-tuple-element.33.total_ref), channel_id=1, source_target_pairs={{0,16},{8,24},{16,0},{24,8},{1,17},{9,25},{17,1},{25,9},{2,18},{10... | collective-permute-start | bytes 196616 | tf_op jit(solution)/shard_map/ppermute | solution.py:32
  19.5 0.3 collective-permute-start.2
  19.9 0.6 collective-permute-start.3
  20.4 1.0 %collective-permute-done.1.a_ref = f32[16,8,128]{2,1,0:T(8,128)S(1)} collective-permute-done((f32[16,8,128]{2,1,0:T(8,128)S(1)}, f32[16,8,128]{2,1,0:T(8,128)S(1)}, u32[]{:S(2)}, u32[]{:S(2)}) %collective-permute-start.1) | collective-permute-done | bytes 65568 | tf_op jit(solution)/shard_map/ppermute | solution.py:32
  21.4 2.0 %collective-permute-done.2.b_ref = f32[16,8,128]{2,1,0:T(8,128)S(1)} collective-permute-done((f32[16,8,128]{2,1,0:T(8,128)S(1)}, f32[16,8,128]{2,1,0:T(8,128)S(1)}, u32[]{:S(2)}, u32[]{:S(2)}) %collective-permute-start.2) | collective-permute-done | bytes 65568 | tf_op jit(solution)/shard_map/ppermute | solution.py:32
  23.4 0.8 %collective-permute-done.3.c_ref = f32[16,8,128]{2,1,0:T(8,128)S(1)} collective-permute-done((f32[16,8,128]{2,1,0:T(8,128)S(1)}, f32[16,8,128]{2,1,0:T(8,128)S(1)}, u32[]{:S(2)}, u32[]{:S(2)}) %collective-permute-start.3) | collective-permute-done | bytes 65568 | tf_op jit(solution)/shard_map/ppermute | solution.py:32
  24.2 1.7 %collective-permute-start.4 = (f32[16,8,128]{2,1,0:T(8,128)S(1)}, f32[16,8,128]{2,1,0:T(8,128)S(1)}, u32[]{:S(2)}, u32[]{:S(2)}) collective-permute-start(f32[16,8,128]{2,1,0:T(8,128)S(1)} %sum_x.1.total_ref), channel_id=1, source_target_pairs={{0,6},{2,4},{4,2},{6,0},{1,7},{3,5},{5,3},{7,1},{8,14},{10,12},{12... | collective-permute-start | bytes 196616 | tf_op jit(solution)/shard_map/ppermute | solution.py:32
  25.9 0.3 collective-permute-start.5
  26.2 1.6 %collective-permute-start.6 = (f32[16,8,128]{2,1,0:T(8,128)S(1)}, f32[16,8,128]{2,1,0:T(8,128)S(1)}, u32[]{:S(2)}, u32[]{:S(2)}) collective-permute-start(f32[16,8,128]{2,1,0:T(8,128)S(1)} %sum_x.1.total_ref), channel_id=1, source_target_pairs={{0,2},{2,0},{4,6},{6,4},{1,3},{3,1},{5,7},{7,5},{8,10},{10,8},{12,... | collective-permute-start | bytes 196616 | tf_op jit(solution)/shard_map/ppermute | solution.py:32
  27.8 1.4 %collective-permute-done.4.a_ref = f32[16,8,128]{2,1,0:T(8,128)S(1)} collective-permute-done((f32[16,8,128]{2,1,0:T(8,128)S(1)}, f32[16,8,128]{2,1,0:T(8,128)S(1)}, u32[]{:S(2)}, u32[]{:S(2)}) %collective-permute-start.4) | collective-permute-done | bytes 65568 | tf_op jit(solution)/shard_map/ppermute | solution.py:32
  29.3 1.7 %collective-permute-done.5.b_ref = f32[16,8,128]{2,1,0:T(8,128)S(1)} collective-permute-done((f32[16,8,128]{2,1,0:T(8,128)S(1)}, f32[16,8,128]{2,1,0:T(8,128)S(1)}, u32[]{:S(2)}, u32[]{:S(2)}) %collective-permute-start.5) | collective-permute-done | bytes 65568 | tf_op jit(solution)/shard_map/ppermute | solution.py:32
  30.9 0.0 collective-permute-done.6.c_ref
  31.0 3.0 %collective-permute-start.7 = (f32[16,8,128]{2,1,0:T(8,128)S(1)}, f32[16,8,128]{2,1,0:T(8,128)S(1)}, u32[]{:S(2)}, u32[]{:S(2)}) collective-permute-start(f32[16,8,128]{2,1,0:T(8,128)S(1)} %sum_z.1.total_ref), channel_id=1, source_target_pairs={{0,64},{32,96},{64,0},{96,32},{1,65},{33,97},{65,1},{97,33},{2,66}... | collective-permute-start | bytes 196616 | tf_op jit(solution)/shard_map/ppermute | solution.py:32
  34.0 0.4 collective-permute-start.8
  34.4 0.4 collective-permute-start.9
  34.7 0.9 %collective-permute-done.7.two_ref = f32[16,8,128]{2,1,0:T(8,128)S(1)} collective-permute-done((f32[16,8,128]{2,1,0:T(8,128)S(1)}, f32[16,8,128]{2,1,0:T(8,128)S(1)}, u32[]{:S(2)}, u32[]{:S(2)}) %collective-permute-start.7) | collective-permute-done | bytes 65568 | tf_op jit(solution)/shard_map/ppermute | solution.py:32
  35.7 1.4 %collective-permute-done.8.one_ref = f32[16,8,128]{2,1,0:T(8,128)S(1)} collective-permute-done((f32[16,8,128]{2,1,0:T(8,128)S(1)}, f32[16,8,128]{2,1,0:T(8,128)S(1)}, u32[]{:S(2)}, u32[]{:S(2)}) %collective-permute-start.8) | collective-permute-done | bytes 65568 | tf_op jit(solution)/shard_map/ppermute | solution.py:32
  37.1 1.6 %collective-permute-done.9.three_ref = f32[16,8,128]{2,1,0:T(8,128)S(1)} collective-permute-done((f32[16,8,128]{2,1,0:T(8,128)S(1)}, f32[16,8,128]{2,1,0:T(8,128)S(1)}, u32[]{:S(2)}, u32[]{:S(2)}) %collective-permute-start.9) | collective-permute-done | bytes 65568 | tf_op jit(solution)/shard_map/ppermute | solution.py:32
  38.7 0.0 copy-done.2
  38.7 1.6 %collective-permute-start.10 = (bf16[256,128]{1,0:T(8,128)(2,1)S(1)}, bf16[256,128]{1,0:T(8,128)(2,1)S(1)}, u32[]{:S(2)}, u32[]{:S(2)}) collective-permute-start(bf16[256,128]{1,0:T(8,128)(2,1)S(1)} %hidden.1.after_ref.packet_ref), channel_id=1, source_target_pairs={{0,128},{128,0},{1,129},{129,1},{2,130},{130,2},{3,131},{131,3},{4... | collective-permute-start | bytes 196616 | tf_op jit(solution)/shard_map/ppermute | solution.py:32
  40.3 6.2 %collective-permute-start.11 = (f32[8,128]{1,0:T(8,128)S(1)}, f32[8,128]{1,0:T(8,128)S(1)}, u32[]{:S(2)}, u32[]{:S(2)}) collective-permute-start(f32[8,128]{1,0:T(8,128)S(1)} %get-tuple-element.57.pack_ref), channel_id=1, source_target_pairs={{0,1},{1,0},{2,3},{3,2},{4,5},{5,4},{6,7},{7,6},{8,9},{9,8},{10,11... | collective-permute-start | bytes 12296 | tf_op jit(solution)/shard_map/ppermute | solution.py:32
  46.5 0.0 collective-permute-start.12
  46.5 3.0 %fetch.1 = (bf16[2048,128]{1,0:T(8,128)(2,1)S(1)}, bf16[16384,128]{1,0:T(8,128)(2,1)S(1)}, bf16[512,2048]{1,0:T(8,128)(2,1)S(1)}) custom-call(bf16[256,128]{1,0:T(8,128)(2,1)S(1)} %hidden.1.after_ref.packet_ref, bf16[2048,128]{1,0:T(8,128)(2,1)} %router_hbm.1, bf16[16384,128]{1,0:T(8,128)(2,1)} %bitcast.35, bf16[512,2048]{1,0:T(8,128)(2,1)} %bitcast.36), custom_call_target="tpu_custom_call" | custom-call | tf_op jit(solution)/shard_map/fetch/pallas_call | solution.py:456
  49.6 0.0 copy-start.6
  49.6 0.0 copy-start.7
  49.6 0.0 copy-start.5
  49.6 0.0 collective-permute-done.11.beside_ref
  49.6 0.0 copy-done.4
  49.6 0.7 prepare.1
  50.3 0.0 collective-permute-done.10.theirs_ref
  50.3 1.8 %collective-permute-start.13 = (bf16[256,128]{1,0:T(8,128)(2,1)S(1)}, bf16[256,128]{1,0:T(8,128)(2,1)S(1)}, u32[]{:S(2)}, u32[]{:S(2)}) collective-permute-start(bf16[256,128]{1,0:T(8,128)(2,1)S(1)} %collective-permute-done.10.theirs_ref), channel_id=1, source_target_pairs={{0,1},{1,0},{2,3},{3,2},{4,5},{5,4},{6,7},{7,6},{8,9},{9,8},{10,11... | collective-permute-start | bytes 196616 | tf_op jit(solution)/shard_map/ppermute | solution.py:32
  52.2 0.0 collective-permute-done.12.next_ref
  52.2 0.9 %collective-permute-done.13.cross_ref = bf16[256,128]{1,0:T(8,128)(2,1)S(1)} collective-permute-done((bf16[256,128]{1,0:T(8,128)(2,1)S(1)}, bf16[256,128]{1,0:T(8,128)(2,1)S(1)}, u32[]{:S(2)}, u32[]{:S(2)}) %collective-permute-start.13) | collective-permute-done | bytes 65568 | tf_op jit(solution)/shard_map/ppermute | solution.py:32
  53.1 0.0 copy-done.3
  53.1 2.9 %experts.1 = (f32[256,128]{1,0:T(8,128)}, f32[8,128]{1,0:T(8,128)S(1)}) custom-call(bf16[8,64]{1,0:T(8,128)(2,1)S(1)} %get-tuple-element.46.own_rows_ref, bf16[16,64]{1,0:T(8,128)(2,1)S(1)} %get-tuple-element.47.chooser_ref, f32[8,128]{1,0:T(8,128)S(1)} %get-tuple-element.48.member_ref, bf16[128,1024]{1,0:T(8,128)(2,1)S(1)} %get-tuple-element.49.spread_ref, ...), custom_call_target="tpu_custom_call" | custom-call | tf_op jit(solution)/shard_map/experts/pallas_call | solution.py:489
  56.0 5.3 %all-to-all-start = ((f32[256,1,128]{2,1,0:T(1,128)}), f32[256,1,128]{2,1,0:T(1,128)S(1)}, u32[]{:S(2)}, u32[]{:S(2)}) async-start(f32[256,1,128]{2,1,0:T(1,128)} %bitcast.14), calls=%async_computation | async-start | bytes 262144 | tf_op jit(solution)/shard_map/all_to_all | solution.py:501
  61.4 0.0 copy-done.6
  61.4 0.0 copy-done.7
  61.4 0.0 copy-done.5
  61.4 1.0 %multiply_add_fusion = f32[8,1,128,128]{3,2,1,0:T(8,128)} fusion(f32[8,128]{1,0:T(8,128)S(1)} %get-tuple-element.61, f32[8,128]{1,0:T(8,128)S(1)} %get-tuple-element.60, bf16[8,1,128,128]{3,2,1,0:T(8,128)(2,1)S(1)} %copy-done.5, f32[8]{0:T(128)S(1)} %exponential_bitcast_fusion, pred[8]{0:T(512)(128)(4,1)S(1)} %bitcast_compare_fusion, bf16[128,128]{1,0:T(8,128)(2,1)S(1)} %slice.13), kind=kLoop, calls=%fused_computation | loop fusion | flops 655360 | bytes 827432 | tf_op jit(solution)/shard_map/add | solution.py:517
  62.5 11.6 %all-to-all-done = f32[256,1,128]{2,1,0:T(1,128)S(1)} async-done(((f32[256,1,128]{2,1,0:T(1,128)}), f32[256,1,128]{2,1,0:T(1,128)S(1)}, u32[]{:S(2)}, u32[]{:S(2)}) %all-to-all-start) | async-done | bytes 131104 | tf_op jit(solution)/shard_map/all_to_all | solution.py:501
  74.0 0.8 %finish.1 = bf16[8,32]{1,0:T(8,128)(2,1)} custom-call(f32[32,256]{1,0:T(8,128)S(1)} %get-tuple-element.45.use_ref, f32[256,128]{1,0:T(8,128)S(1)} %bitcast.32, f32[8,128]{1,0:T(8,128)S(1)} %get-tuple-element.55.own_ref), custom_call_target="tpu_custom_call" | custom-call | tf_op jit(solution)/shard_map/finish/pallas_call | solution.py:502
  (7 shorter events, 0.1 us)
Async XLA Ops:
  0.6 38.1 %copy-start.2 = (bf16[8,2048]{1,0:T(8,128)(2,1)S(1)}, bf16[8,2048]{1,0:T(8,128)(2,1)}, u32[]{:S(2)}) copy-start(bf16[8,2048]{1,0:T(8,128)(2,1)} %resid_ref.1) | copy-start | bytes 98308
  0.6 14.7 %copy-start = (bf16[1,2,2048,128]{3,2,1,0:T(8,128)(2,1)S(1)}, bf16[1,2,2048,128]{3,2,1,0:T(8,128)(2,1)}, u32[]{:S(2)}) copy-start(bf16[1,2,2048,128]{3,2,1,0:T(8,128)(2,1)} %param.17) | copy-start | bytes 3145732
  0.7 14.7 %copy-start.1 = (bf16[128,2048]{1,0:T(8,128)(2,1)S(1)}, bf16[128,2048]{1,0:T(8,128)(2,1)}, u32[]{:S(2)}) copy-start(bf16[128,2048]{1,0:T(8,128)(2,1)} %weight_ref.1) | copy-start | bytes 1572868
  2.4 12.9 %collective-permute-start = (f32[24,128]{1,0:T(8,128)S(1)}, f32[24,128]{1,0:T(8,128)S(1)}, u32[]{:S(2)}, u32[]{:S(2)}) collective-permute-start(f32[24,128]{1,0:T(8,128)S(1)} %message.1.message_ref), channel_id=1, source_target_pairs={{0,128},{128,0},{1,129},{129,1},{2,130},{130,2},{3,131},{131,3},{4... | collective-permute-start | bytes 36872 | tf_op jit(solution)/shard_map/ppermute | solution.py:32
  16.7 32.9 %copy-start.4 = (s32[32,8]{0,1:T(8,128)S(1)}, s32[32,8]{0,1:T(8,128)}, u32[]{:S(2)}) copy-start(s32[32,8]{0,1:T(8,128)} %param.31) | copy-start | bytes 3076
  16.7 36.4 %copy-start.3 = (f32[2048]{0:T(1024)S(1)}, f32[2048]{0:T(1024)}, u32[]{:S(2)}) copy-start(f32[2048]{0:T(1024)} %param.29) | copy-start | bytes 24580
  16.7 4.7 %collective-permute-start.1 = (f32[16,8,128]{2,1,0:T(8,128)S(1)}, f32[16,8,128]{2,1,0:T(8,128)S(1)}, u32[]{:S(2)}, u32[]{:S(2)}) collective-permute-start(f32[16,8,128]{2,1,0:T(8,128)S(1)} %get-tuple-element.33.total_ref), channel_id=1, source_target_pairs={{0,16},{8,24},{16,0},{24,8},{1,17},{9,25},{17,1},{25,9},{2,18},{10... | collective-permute-start | bytes 196616 | tf_op jit(solution)/shard_map/ppermute | solution.py:32
  19.5 3.9 %collective-permute-start.2 = (f32[16,8,128]{2,1,0:T(8,128)S(1)}, f32[16,8,128]{2,1,0:T(8,128)S(1)}, u32[]{:S(2)}, u32[]{:S(2)}) collective-permute-start(f32[16,8,128]{2,1,0:T(8,128)S(1)} %get-tuple-element.33.total_ref), channel_id=1, source_target_pairs={{0,8},{8,0},{16,24},{24,16},{1,9},{9,1},{17,25},{25,17},{2,10},{10... | collective-permute-start | bytes 196616 | tf_op jit(solution)/shard_map/ppermute | solution.py:32
  19.9 4.3 %collective-permute-start.3 = (f32[16,8,128]{2,1,0:T(8,128)S(1)}, f32[16,8,128]{2,1,0:T(8,128)S(1)}, u32[]{:S(2)}, u32[]{:S(2)}) collective-permute-start(f32[16,8,128]{2,1,0:T(8,128)S(1)} %get-tuple-element.33.total_ref), channel_id=1, source_target_pairs={{0,24},{8,16},{16,8},{24,0},{1,25},{9,17},{17,9},{25,1},{2,26},{10... | collective-permute-start | bytes 196616 | tf_op jit(solution)/shard_map/ppermute | solution.py:32
  24.2 5.0 %collective-permute-start.4 = (f32[16,8,128]{2,1,0:T(8,128)S(1)}, f32[16,8,128]{2,1,0:T(8,128)S(1)}, u32[]{:S(2)}, u32[]{:S(2)}) collective-permute-start(f32[16,8,128]{2,1,0:T(8,128)S(1)} %sum_x.1.total_ref), channel_id=1, source_target_pairs={{0,6},{2,4},{4,2},{6,0},{1,7},{3,5},{5,3},{7,1},{8,14},{10,12},{12... | collective-permute-start | bytes 196616 | tf_op jit(solution)/shard_map/ppermute | solution.py:32
  25.9 5.0 %collective-permute-start.5 = (f32[16,8,128]{2,1,0:T(8,128)S(1)}, f32[16,8,128]{2,1,0:T(8,128)S(1)}, u32[]{:S(2)}, u32[]{:S(2)}) collective-permute-start(f32[16,8,128]{2,1,0:T(8,128)S(1)} %sum_x.1.total_ref), channel_id=1, source_target_pairs={{0,4},{2,6},{4,0},{6,2},{1,5},{3,7},{5,1},{7,3},{8,12},{10,14},{12... | collective-permute-start | bytes 196616 | tf_op jit(solution)/shard_map/ppermute | solution.py:32
  26.2 4.7 %collective-permute-start.6 = (f32[16,8,128]{2,1,0:T(8,128)S(1)}, f32[16,8,128]{2,1,0:T(8,128)S(1)}, u32[]{:S(2)}, u32[]{:S(2)}) collective-permute-start(f32[16,8,128]{2,1,0:T(8,128)S(1)} %sum_x.1.total_ref), channel_id=1, source_target_pairs={{0,2},{2,0},{4,6},{6,4},{1,3},{3,1},{5,7},{7,5},{8,10},{10,8},{12,... | collective-permute-start | bytes 196616 | tf_op jit(solution)/shard_map/ppermute | solution.py:32
  31.0 4.7 %collective-permute-start.7 = (f32[16,8,128]{2,1,0:T(8,128)S(1)}, f32[16,8,128]{2,1,0:T(8,128)S(1)}, u32[]{:S(2)}, u32[]{:S(2)}) collective-permute-start(f32[16,8,128]{2,1,0:T(8,128)S(1)} %sum_z.1.total_ref), channel_id=1, source_target_pairs={{0,64},{32,96},{64,0},{96,32},{1,65},{33,97},{65,1},{97,33},{2,66}... | collective-permute-start | bytes 196616 | tf_op jit(solution)/shard_map/ppermute | solution.py:32
  34.0 3.1 %collective-permute-start.8 = (f32[16,8,128]{2,1,0:T(8,128)S(1)}, f32[16,8,128]{2,1,0:T(8,128)S(1)}, u32[]{:S(2)}, u32[]{:S(2)}) collective-permute-start(f32[16,8,128]{2,1,0:T(8,128)S(1)} %sum_z.1.total_ref), channel_id=1, source_target_pairs={{0,32},{32,0},{64,96},{96,64},{1,33},{33,1},{65,97},{97,65},{2,34}... | collective-permute-start | bytes 196616 | tf_op jit(solution)/shard_map/ppermute | solution.py:32
  34.4 4.3 %collective-permute-start.9 = (f32[16,8,128]{2,1,0:T(8,128)S(1)}, f32[16,8,128]{2,1,0:T(8,128)S(1)}, u32[]{:S(2)}, u32[]{:S(2)}) collective-permute-start(f32[16,8,128]{2,1,0:T(8,128)S(1)} %sum_z.1.total_ref), channel_id=1, source_target_pairs={{0,96},{32,64},{64,32},{96,0},{1,97},{33,65},{65,33},{97,1},{2,98}... | collective-permute-start | bytes 196616 | tf_op jit(solution)/shard_map/ppermute | solution.py:32
  38.7 11.6 %collective-permute-start.10 = (bf16[256,128]{1,0:T(8,128)(2,1)S(1)}, bf16[256,128]{1,0:T(8,128)(2,1)S(1)}, u32[]{:S(2)}, u32[]{:S(2)}) collective-permute-start(bf16[256,128]{1,0:T(8,128)(2,1)S(1)} %hidden.1.after_ref.packet_ref), channel_id=1, source_target_pairs={{0,128},{128,0},{1,129},{129,1},{2,130},{130,2},{3,131},{131,3},{4... | collective-permute-start | bytes 196616 | tf_op jit(solution)/shard_map/ppermute | solution.py:32
  40.3 9.3 %collective-permute-start.11 = (f32[8,128]{1,0:T(8,128)S(1)}, f32[8,128]{1,0:T(8,128)S(1)}, u32[]{:S(2)}, u32[]{:S(2)}) collective-permute-start(f32[8,128]{1,0:T(8,128)S(1)} %get-tuple-element.57.pack_ref), channel_id=1, source_target_pairs={{0,1},{1,0},{2,3},{3,2},{4,5},{5,4},{6,7},{7,6},{8,9},{9,8},{10,11... | collective-permute-start | bytes 12296 | tf_op jit(solution)/shard_map/ppermute | solution.py:32
  46.5 5.7 %collective-permute-start.12 = (bf16[256,128]{1,0:T(8,128)(2,1)S(1)}, bf16[256,128]{1,0:T(8,128)(2,1)S(1)}, u32[]{:S(2)}, u32[]{:S(2)}) collective-permute-start(bf16[256,128]{1,0:T(8,128)(2,1)S(1)} %hidden.1.after_ref.packet_ref), channel_id=1, source_target_pairs={{0,1},{1,0},{2,3},{3,2},{4,5},{5,4},{6,7},{7,6},{8,9},{9,8},{10,11... | collective-permute-start | bytes 196616 | tf_op jit(solution)/shard_map/ppermute | solution.py:32
  49.6 11.8 %copy-start.6 = (bf16[8,3,128]{2,0,1:T(8,128)(2,1)S(1)}, bf16[8,3,128]{2,0,1:T(8,128)(2,1)}, u32[]{:S(2)}) copy-start(bf16[8,3,128]{2,0,1:T(8,128)(2,1)} %param.22) | copy-start | bytes 18436
  49.6 11.8 %copy-start.7 = (f32[8,1]{0,1:T(1,128)S(1)}, f32[8,1]{0,1:T(1,128)}, u32[]{:S(2)}) copy-start(f32[8,1]{0,1:T(1,128)} %param.23) | copy-start | bytes 100
  49.6 11.8 %copy-start.5 = (bf16[8,1,128,128]{3,2,1,0:T(8,128)(2,1)S(1)}, bf16[8,1,128,128]{3,2,1,0:T(8,128)(2,1)}, u32[]{:S(2)}) copy-start(bf16[8,1,128,128]{3,2,1,0:T(8,128)(2,1)} %param.24) | copy-start | bytes 786436
  50.3 2.7 %collective-permute-start.13 = (bf16[256,128]{1,0:T(8,128)(2,1)S(1)}, bf16[256,128]{1,0:T(8,128)(2,1)S(1)}, u32[]{:S(2)}, u32[]{:S(2)}) collective-permute-start(bf16[256,128]{1,0:T(8,128)(2,1)S(1)} %collective-permute-done.10.theirs_ref), channel_id=1, source_target_pairs={{0,1},{1,0},{2,3},{3,2},{4,5},{5,4},{6,7},{7,6},{8,9},{9,8},{10,11... | collective-permute-start | bytes 196616 | tf_op jit(solution)/shard_map/ppermute | solution.py:32
  56.0 18.0 %all-to-all-start = ((f32[256,1,128]{2,1,0:T(1,128)}), f32[256,1,128]{2,1,0:T(1,128)S(1)}, u32[]{:S(2)}, u32[]{:S(2)}) async-start(f32[256,1,128]{2,1,0:T(1,128)} %bitcast.14), calls=%async_computation | async-start | bytes 262144 | tf_op jit(solution)/shard_map/all_to_all | solution.py:501

commit v6 on v5

--- a/solution.py
+++ b/solution.py
@@ -431,9 +431,9 @@
 
     expert_in = w_in[0].reshape(2048, 2, 4, 128).transpose(0, 2, 1, 3).reshape(16384, 128)
     total = partial
-    for axis, flips in (("x", (2, 1, 3)), ("z", (3, 2, 1)), ("y", (2, 1, 3))):
+    for axis, flips in (("y", (2, 1, 3)), ("z", (3, 2, 1)), ("x", (2, 1, 3))):
         parts = [swap(total, axis, flip) for flip in flips]
-        if axis != "y":
+        if axis != "x":
             total = pl.pallas_call(
                 functools.partial(sum_kernel, flips),
                 out_shape=pltpu.VMEM((16, 8, 128), F32),

time: 75 us -> 75 us (level)
  no operation moved by 1% of the time
where the time goes in v6:
time: 75 us; the launch traced here: 74.8 us
  starting transfers between devices  33.9 us (45%)
  waiting for transfers between devices  23.3 us (31%)
  Pallas kernels  14.3 us (19%)
  between operations  2.26 us (3%)
  other arithmetic  1.05 us (1%)
    ppermute x14, starting transfers between devices, swap(): lax.ppermute(shard, axis, [(i, i ^ flip) for i in range(lax.axis_size(axi...  28.6 us
    ppermute x14, waiting for transfers between devices, swap(): lax.ppermute(shard, axis, [(i, i ^ flip) for i in range(lax.axis_size(axi...  11.7 us
    all_to_all x1, waiting for transfers between devices, on_device(): lax.all_to_all(term.reshape(256, 1, 128), ('s', 't', 'z', 'y', 'x'), 0, 0...  11.6 us
    all_to_all x1, starting transfers between devices, on_device(): lax.all_to_all(term.reshape(256, 1, 128), ('s', 't', 'z', 'y', 'x'), 0, 0...  5.32 us
    pallas_call x1, Pallas kernels, on_device(): pl.pallas_call(own_rows_kernel, out_shape=(jax.ShapeDtypeStruct((8, 128),...  4.4 us
    pallas_call x1, Pallas kernels, on_device(): pl.pallas_call(fetch_kernel, out_shape=(pltpu.VMEM((2048, 128), BF16), pl...  3.04 us
    pallas_call x1, Pallas kernels, on_device(): pl.pallas_call(expert_kernel, out_shape=(jax.ShapeDtypeStruct((256, 128),...  2.93 us
  transfers between devices with their start and end apart: 15, of which 10 were waited for; matrix products, arithmetic and copies ran while one was open for 1% of the time, Pallas kernels for 11%

profile of v6, /device:TPU:1, one launch (start us, length us, event | category | flops | bytes accessed | tf_op | source)
XLA Modules:
  0.0 74.8 jit_solution(18001086687421194745)
XLA Ops:
  0.6 0.0 copy-start.2
  0.6 0.0 copy-start
  0.7 0.0 copy-start.1
  1.4 1.0 %message.1.message_ref = f32[24,128]{1,0:T(8,128)S(1)} custom-call(s32[1,1]{1,0:T(1,128)} %bitcast.29.owner_hbm, f32[1,8]{1,0:T(1,128)} %bitcast.41, bf16[3,8,128]{2,1,0:T(8,128)(2,1)} %bitcast.38, bf16[8,2048]{1,0:T(8,128)(2,1)} %resid_ref.1), custom_call_target="tpu_custom_call" | custom-call | tf_op jit(solution)/shard_map/message/pallas_call | solution.py:376
  2.4 7.8 %collective-permute-start = (f32[24,128]{1,0:T(8,128)S(1)}, f32[24,128]{1,0:T(8,128)S(1)}, u32[]{:S(2)}, u32[]{:S(2)}) collective-permute-start(f32[24,128]{1,0:T(8,128)S(1)} %message.1.message_ref), channel_id=1, source_target_pairs={{0,128},{128,0},{1,129},{129,1},{2,130},{130,2},{3,131},{131,3},{4... | collective-permute-start | bytes 36872 | tf_op jit(solution)/shard_map/ppermute | solution.py:32
  10.9 4.4 %own_rows.1 = (f32[8,128]{1,0:T(8,128)S(1)}, bf16[128,128]{1,0:T(8,128)(2,1)S(1)}) custom-call(s32[1]{0:T(128)S(6)} %copy.22.length_ref, s32[8]{0:T(128)} %live_hbm.1, f32[8]{0:T(128)} %bitcast.42, f32[16,128]{1,0:T(8,128)} %bitcast.40, bf16[3,8,128]{2,1,0:T(8,128)(2,1)} %bitcast.39, f32[2,128]{1,0:T(2,128)} %gain_hbm.3, bf16[2,2048,128]{2,1,0:T(8,128)(2,1)} %bitcast.30, ...), custom_call_target="tpu_custom_call" | custom-call | tf_op jit(solution)/shard_map/own_rows/pallas_call | solution.py:393
  15.3 0.0 collective-permute-done.got_ref
  15.3 0.0 copy-done
  15.3 0.0 copy-done.1
  15.3 1.4 %guest.1 = (f32[16,8,128]{2,1,0:T(8,128)S(1)}, f32[8,128]{1,0:T(8,128)S(1)}) custom-call(s32[1]{0:T(128)S(6)} %copy.22.length_ref, f32[24,128]{1,0:T(8,128)S(1)} %message.1.message_ref, f32[24,128]{1,0:T(8,128)S(1)} %collective-permute-done.got_ref, f32[8,128]{1,0:T(8,128)S(1)} %get-tuple-element.31.head_ref, ...), custom_call_target="tpu_custom_call" | custom-call | tf_op jit(solution)/shard_map/guest/pallas_call | solution.py:422
  16.7 0.0 copy-start.4
  16.7 0.0 copy-start.3
  16.7 3.0 %collective-permute-start.1 = (f32[16,8,128]{2,1,0:T(8,128)S(1)}, f32[16,8,128]{2,1,0:T(8,128)S(1)}, u32[]{:S(2)}, u32[]{:S(2)}) collective-permute-start(f32[16,8,128]{2,1,0:T(8,128)S(1)} %get-tuple-element.33.total_ref), channel_id=1, source_target_pairs={{0,64},{32,96},{64,0},{96,32},{1,65},{33,97},{65,1},{97,33},{2,66}... | collective-permute-start | bytes 196616 | tf_op jit(solution)/shard_map/ppermute | solution.py:32
  19.7 0.4 collective-permute-start.2
  20.1 0.4 collective-permute-start.3
  20.5 0.9 %collective-permute-done.1.a_ref = f32[16,8,128]{2,1,0:T(8,128)S(1)} collective-permute-done((f32[16,8,128]{2,1,0:T(8,128)S(1)}, f32[16,8,128]{2,1,0:T(8,128)S(1)}, u32[]{:S(2)}, u32[]{:S(2)}) %collective-permute-start.1) | collective-permute-done | bytes 65568 | tf_op jit(solution)/shard_map/ppermute | solution.py:32
  21.4 2.0 %collective-permute-done.2.b_ref = f32[16,8,128]{2,1,0:T(8,128)S(1)} collective-permute-done((f32[16,8,128]{2,1,0:T(8,128)S(1)}, f32[16,8,128]{2,1,0:T(8,128)S(1)}, u32[]{:S(2)}, u32[]{:S(2)}) %collective-permute-start.2) | collective-permute-done | bytes 65568 | tf_op jit(solution)/shard_map/ppermute | solution.py:32
  23.4 1.0 %collective-permute-done.3.c_ref = f32[16,8,128]{2,1,0:T(8,128)S(1)} collective-permute-done((f32[16,8,128]{2,1,0:T(8,128)S(1)}, f32[16,8,128]{2,1,0:T(8,128)S(1)}, u32[]{:S(2)}, u32[]{:S(2)}) %collective-permute-start.3) | collective-permute-done | bytes 65568 | tf_op jit(solution)/shard_map/ppermute | solution.py:32
  24.5 1.7 %collective-permute-start.4 = (f32[16,8,128]{2,1,0:T(8,128)S(1)}, f32[16,8,128]{2,1,0:T(8,128)S(1)}, u32[]{:S(2)}, u32[]{:S(2)}) collective-permute-start(f32[16,8,128]{2,1,0:T(8,128)S(1)} %sum_y.1.total_ref), channel_id=1, source_target_pairs={{0,6},{2,4},{4,2},{6,0},{1,7},{3,5},{5,3},{7,1},{8,14},{10,12},{12... | collective-permute-start | bytes 196616 | tf_op jit(solution)/shard_map/ppermute | solution.py:32
  26.2 0.3 collective-permute-start.5
  26.5 1.6 %collective-permute-start.6 = (f32[16,8,128]{2,1,0:T(8,128)S(1)}, f32[16,8,128]{2,1,0:T(8,128)S(1)}, u32[]{:S(2)}, u32[]{:S(2)}) collective-permute-start(f32[16,8,128]{2,1,0:T(8,128)S(1)} %sum_y.1.total_ref), channel_id=1, source_target_pairs={{0,2},{2,0},{4,6},{6,4},{1,3},{3,1},{5,7},{7,5},{8,10},{10,8},{12,... | collective-permute-start | bytes 196616 | tf_op jit(solution)/shard_map/ppermute | solution.py:32
  28.1 1.4 %collective-permute-done.4.a_ref = f32[16,8,128]{2,1,0:T(8,128)S(1)} collective-permute-done((f32[16,8,128]{2,1,0:T(8,128)S(1)}, f32[16,8,128]{2,1,0:T(8,128)S(1)}, u32[]{:S(2)}, u32[]{:S(2)}) %collective-permute-start.4) | collective-permute-done | bytes 65568 | tf_op jit(solution)/shard_map/ppermute | solution.py:32
  29.5 1.7 %collective-permute-done.5.b_ref = f32[16,8,128]{2,1,0:T(8,128)S(1)} collective-permute-done((f32[16,8,128]{2,1,0:T(8,128)S(1)}, f32[16,8,128]{2,1,0:T(8,128)S(1)}, u32[]{:S(2)}, u32[]{:S(2)}) %collective-permute-start.5) | collective-permute-done | bytes 65568 | tf_op jit(solution)/shard_map/ppermute | solution.py:32
  31.2 0.0 collective-permute-done.6.c_ref
  31.2 2.8 %collective-permute-start.7 = (f32[16,8,128]{2,1,0:T(8,128)S(1)}, f32[16,8,128]{2,1,0:T(8,128)S(1)}, u32[]{:S(2)}, u32[]{:S(2)}) collective-permute-start(f32[16,8,128]{2,1,0:T(8,128)S(1)} %sum_z.1.total_ref), channel_id=1, source_target_pairs={{0,16},{8,24},{16,0},{24,8},{1,17},{9,25},{17,1},{25,9},{2,18},{10... | collective-permute-start | bytes 196616 | tf_op jit(solution)/shard_map/ppermute | solution.py:32
  34.0 0.3 collective-permute-start.8
  34.4 0.6 collective-permute-start.9
  34.9 1.0 %collective-permute-done.7.two_ref = f32[16,8,128]{2,1,0:T(8,128)S(1)} collective-permute-done((f32[16,8,128]{2,1,0:T(8,128)S(1)}, f32[16,8,128]{2,1,0:T(8,128)S(1)}, u32[]{:S(2)}, u32[]{:S(2)}) %collective-permute-start.7) | collective-permute-done | bytes 65568 | tf_op jit(solution)/shard_map/ppermute | solution.py:32
  35.9 1.2 %collective-permute-done.8.one_ref = f32[16,8,128]{2,1,0:T(8,128)S(1)} collective-permute-done((f32[16,8,128]{2,1,0:T(8,128)S(1)}, f32[16,8,128]{2,1,0:T(8,128)S(1)}, u32[]{:S(2)}, u32[]{:S(2)}) %collective-permute-start.8) | collective-permute-done | bytes 65568 | tf_op jit(solution)/shard_map/ppermute | solution.py:32
  37.2 1.5 %collective-permute-done.9.three_ref = f32[16,8,128]{2,1,0:T(8,128)S(1)} collective-permute-done((f32[16,8,128]{2,1,0:T(8,128)S(1)}, f32[16,8,128]{2,1,0:T(8,128)S(1)}, u32[]{:S(2)}, u32[]{:S(2)}) %collective-permute-start.9) | collective-permute-done | bytes 65568 | tf_op jit(solution)/shard_map/ppermute | solution.py:32
  38.7 0.0 copy-done.2
  38.7 1.4 %collective-permute-start.10 = (bf16[256,128]{1,0:T(8,128)(2,1)S(1)}, bf16[256,128]{1,0:T(8,128)(2,1)S(1)}, u32[]{:S(2)}, u32[]{:S(2)}) collective-permute-start(bf16[256,128]{1,0:T(8,128)(2,1)S(1)} %hidden.1.after_ref.packet_ref), channel_id=1, source_target_pairs={{0,128},{128,0},{1,129},{129,1},{2,130},{130,2},{3,131},{131,3},{4... | collective-permute-start | bytes 196616 | tf_op jit(solution)/shard_map/ppermute | solution.py:32
  40.1 6.4 %collective-permute-start.11 = (f32[8,128]{1,0:T(8,128)S(1)}, f32[8,128]{1,0:T(8,128)S(1)}, u32[]{:S(2)}, u32[]{:S(2)}) collective-permute-start(f32[8,128]{1,0:T(8,128)S(1)} %get-tuple-element.57.pack_ref), channel_id=1, source_target_pairs={{0,1},{1,0},{2,3},{3,2},{4,5},{5,4},{6,7},{7,6},{8,9},{9,8},{10,11... | collective-permute-start | bytes 12296 | tf_op jit(solution)/shard_map/ppermute | solution.py:32
  46.5 0.0 collective-permute-start.12
  46.5 3.0 %fetch.1 = (bf16[2048,128]{1,0:T(8,128)(2,1)S(1)}, bf16[16384,128]{1,0:T(8,128)(2,1)S(1)}, bf16[512,2048]{1,0:T(8,128)(2,1)S(1)}) custom-call(bf16[256,128]{1,0:T(8,128)(2,1)S(1)} %hidden.1.after_ref.packet_ref, bf16[2048,128]{1,0:T(8,128)(2,1)} %router_hbm.1, bf16[16384,128]{1,0:T(8,128)(2,1)} %bitcast.35, bf16[512,2048]{1,0:T(8,128)(2,1)} %bitcast.36), custom_call_target="tpu_custom_call" | custom-call | tf_op jit(solution)/shard_map/fetch/pallas_call | solution.py:456
  49.6 0.0 copy-start.6
  49.6 0.0 copy-start.7
  49.6 0.0 copy-start.5
  49.6 0.0 collective-permute-done.11.beside_ref
  49.6 0.0 copy-done.4
  49.6 0.7 prepare.1
  50.3 0.0 collective-permute-done.10.theirs_ref
  50.3 1.8 %collective-permute-start.13 = (bf16[256,128]{1,0:T(8,128)(2,1)S(1)}, bf16[256,128]{1,0:T(8,128)(2,1)S(1)}, u32[]{:S(2)}, u32[]{:S(2)}) collective-permute-start(bf16[256,128]{1,0:T(8,128)(2,1)S(1)} %collective-permute-done.10.theirs_ref), channel_id=1, source_target_pairs={{0,1},{1,0},{2,3},{3,2},{4,5},{5,4},{6,7},{7,6},{8,9},{9,8},{10,11... | collective-permute-start | bytes 196616 | tf_op jit(solution)/shard_map/ppermute | solution.py:32
  52.2 0.0 collective-permute-done.12.next_ref
  52.2 0.9 %collective-permute-done.13.cross_ref = bf16[256,128]{1,0:T(8,128)(2,1)S(1)} collective-permute-done((bf16[256,128]{1,0:T(8,128)(2,1)S(1)}, bf16[256,128]{1,0:T(8,128)(2,1)S(1)}, u32[]{:S(2)}, u32[]{:S(2)}) %collective-permute-start.13) | collective-permute-done | bytes 65568 | tf_op jit(solution)/shard_map/ppermute | solution.py:32
  53.1 0.0 copy-done.3
  53.1 2.9 %experts.1 = (f32[256,128]{1,0:T(8,128)}, f32[8,128]{1,0:T(8,128)S(1)}) custom-call(bf16[8,64]{1,0:T(8,128)(2,1)S(1)} %get-tuple-element.46.own_rows_ref, bf16[16,64]{1,0:T(8,128)(2,1)S(1)} %get-tuple-element.47.chooser_ref, f32[8,128]{1,0:T(8,128)S(1)} %get-tuple-element.48.member_ref, bf16[128,1024]{1,0:T(8,128)(2,1)S(1)} %get-tuple-element.49.spread_ref, ...), custom_call_target="tpu_custom_call" | custom-call | tf_op jit(solution)/shard_map/experts/pallas_call | solution.py:489
  56.0 5.3 %all-to-all-start = ((f32[256,1,128]{2,1,0:T(1,128)}), f32[256,1,128]{2,1,0:T(1,128)S(1)}, u32[]{:S(2)}, u32[]{:S(2)}) async-start(f32[256,1,128]{2,1,0:T(1,128)} %bitcast.14), calls=%async_computation | async-start | bytes 262144 | tf_op jit(solution)/shard_map/all_to_all | solution.py:501
  61.4 0.0 copy-done.6
  61.4 0.0 copy-done.7
  61.4 0.0 copy-done.5
  61.4 1.0 %multiply_add_fusion = f32[8,1,128,128]{3,2,1,0:T(8,128)} fusion(f32[8,128]{1,0:T(8,128)S(1)} %get-tuple-element.61, f32[8,128]{1,0:T(8,128)S(1)} %get-tuple-element.60, bf16[8,1,128,128]{3,2,1,0:T(8,128)(2,1)S(1)} %copy-done.5, f32[8]{0:T(128)S(1)} %exponential_bitcast_fusion, pred[8]{0:T(512)(128)(4,1)S(1)} %bitcast_compare_fusion, bf16[128,128]{1,0:T(8,128)(2,1)S(1)} %slice.13), kind=kLoop, calls=%fused_computation | loop fusion | flops 655360 | bytes 827432 | tf_op jit(solution)/shard_map/add | solution.py:517
  62.5 11.6 %all-to-all-done = f32[256,1,128]{2,1,0:T(1,128)S(1)} async-done(((f32[256,1,128]{2,1,0:T(1,128)}), f32[256,1,128]{2,1,0:T(1,128)S(1)}, u32[]{:S(2)}, u32[]{:S(2)}) %all-to-all-start) | async-done | bytes 131104 | tf_op jit(solution)/shard_map/all_to_all | solution.py:501
  74.0 0.8 %finish.1 = bf16[8,32]{1,0:T(8,128)(2,1)} custom-call(f32[32,256]{1,0:T(8,128)S(1)} %get-tuple-element.45.use_ref, f32[256,128]{1,0:T(8,128)S(1)} %bitcast.32, f32[8,128]{1,0:T(8,128)S(1)} %get-tuple-element.55.own_ref), custom_call_target="tpu_custom_call" | custom-call | tf_op jit(solution)/shard_map/finish/pallas_call | solution.py:502
  (7 shorter events, 0.1 us)
Async XLA Ops:
  0.6 38.1 %copy-start.2 = (bf16[8,2048]{1,0:T(8,128)(2,1)S(1)}, bf16[8,2048]{1,0:T(8,128)(2,1)}, u32[]{:S(2)}) copy-start(bf16[8,2048]{1,0:T(8,128)(2,1)} %resid_ref.1) | copy-start | bytes 98308
  0.6 14.7 %copy-start = (bf16[1,2,2048,128]{3,2,1,0:T(8,128)(2,1)S(1)}, bf16[1,2,2048,128]{3,2,1,0:T(8,128)(2,1)}, u32[]{:S(2)}) copy-start(bf16[1,2,2048,128]{3,2,1,0:T(8,128)(2,1)} %param.17) | copy-start | bytes 3145732
  0.7 14.7 %copy-start.1 = (bf16[128,2048]{1,0:T(8,128)(2,1)S(1)}, bf16[128,2048]{1,0:T(8,128)(2,1)}, u32[]{:S(2)}) copy-start(bf16[128,2048]{1,0:T(8,128)(2,1)} %weight_ref.1) | copy-start | bytes 1572868
  2.4 12.9 %collective-permute-start = (f32[24,128]{1,0:T(8,128)S(1)}, f32[24,128]{1,0:T(8,128)S(1)}, u32[]{:S(2)}, u32[]{:S(2)}) collective-permute-start(f32[24,128]{1,0:T(8,128)S(1)} %message.1.message_ref), channel_id=1, source_target_pairs={{0,128},{128,0},{1,129},{129,1},{2,130},{130,2},{3,131},{131,3},{4... | collective-permute-start | bytes 36872 | tf_op jit(solution)/shard_map/ppermute | solution.py:32
  16.7 32.9 %copy-start.4 = (s32[32,8]{0,1:T(8,128)S(1)}, s32[32,8]{0,1:T(8,128)}, u32[]{:S(2)}) copy-start(s32[32,8]{0,1:T(8,128)} %param.31) | copy-start | bytes 3076
  16.7 36.4 %copy-start.3 = (f32[2048]{0:T(1024)S(1)}, f32[2048]{0:T(1024)}, u32[]{:S(2)}) copy-start(f32[2048]{0:T(1024)} %param.29) | copy-start | bytes 24580
  16.7 4.7 %collective-permute-start.1 = (f32[16,8,128]{2,1,0:T(8,128)S(1)}, f32[16,8,128]{2,1,0:T(8,128)S(1)}, u32[]{:S(2)}, u32[]{:S(2)}) collective-permute-start(f32[16,8,128]{2,1,0:T(8,128)S(1)} %get-tuple-element.33.total_ref), channel_id=1, source_target_pairs={{0,64},{32,96},{64,0},{96,32},{1,65},{33,97},{65,1},{97,33},{2,66}... | collective-permute-start | bytes 196616 | tf_op jit(solution)/shard_map/ppermute | solution.py:32
  19.7 3.7 %collective-permute-start.2 = (f32[16,8,128]{2,1,0:T(8,128)S(1)}, f32[16,8,128]{2,1,0:T(8,128)S(1)}, u32[]{:S(2)}, u32[]{:S(2)}) collective-permute-start(f32[16,8,128]{2,1,0:T(8,128)S(1)} %get-tuple-element.33.total_ref), channel_id=1, source_target_pairs={{0,32},{32,0},{64,96},{96,64},{1,33},{33,1},{65,97},{97,65},{2,34}... | collective-permute-start | bytes 196616 | tf_op jit(solution)/shard_map/ppermute | solution.py:32
  20.1 4.3 %collective-permute-start.3 = (f32[16,8,128]{2,1,0:T(8,128)S(1)}, f32[16,8,128]{2,1,0:T(8,128)S(1)}, u32[]{:S(2)}, u32[]{:S(2)}) collective-permute-start(f32[16,8,128]{2,1,0:T(8,128)S(1)} %get-tuple-element.33.total_ref), channel_id=1, source_target_pairs={{0,96},{32,64},{64,32},{96,0},{1,97},{33,65},{65,33},{97,1},{2,98}... | collective-permute-start | bytes 196616 | tf_op jit(solution)/shard_map/ppermute | solution.py:32
  24.5 5.0 %collective-permute-start.4 = (f32[16,8,128]{2,1,0:T(8,128)S(1)}, f32[16,8,128]{2,1,0:T(8,128)S(1)}, u32[]{:S(2)}, u32[]{:S(2)}) collective-permute-start(f32[16,8,128]{2,1,0:T(8,128)S(1)} %sum_y.1.total_ref), channel_id=1, source_target_pairs={{0,6},{2,4},{4,2},{6,0},{1,7},{3,5},{5,3},{7,1},{8,14},{10,12},{12... | collective-permute-start | bytes 196616 | tf_op jit(solution)/shard_map/ppermute | solution.py:32
  26.2 5.0 %collective-permute-start.5 = (f32[16,8,128]{2,1,0:T(8,128)S(1)}, f32[16,8,128]{2,1,0:T(8,128)S(1)}, u32[]{:S(2)}, u32[]{:S(2)}) collective-permute-start(f32[16,8,128]{2,1,0:T(8,128)S(1)} %sum_y.1.total_ref), channel_id=1, source_target_pairs={{0,4},{2,6},{4,0},{6,2},{1,5},{3,7},{5,1},{7,3},{8,12},{10,14},{12... | collective-permute-start | bytes 196616 | tf_op jit(solution)/shard_map/ppermute | solution.py:32
  26.5 4.7 %collective-permute-start.6 = (f32[16,8,128]{2,1,0:T(8,128)S(1)}, f32[16,8,128]{2,1,0:T(8,128)S(1)}, u32[]{:S(2)}, u32[]{:S(2)}) collective-permute-start(f32[16,8,128]{2,1,0:T(8,128)S(1)} %sum_y.1.total_ref), channel_id=1, source_target_pairs={{0,2},{2,0},{4,6},{6,4},{1,3},{3,1},{5,7},{7,5},{8,10},{10,8},{12,... | collective-permute-start | bytes 196616 | tf_op jit(solution)/shard_map/ppermute | solution.py:32
  31.2 4.7 %collective-permute-start.7 = (f32[16,8,128]{2,1,0:T(8,128)S(1)}, f32[16,8,128]{2,1,0:T(8,128)S(1)}, u32[]{:S(2)}, u32[]{:S(2)}) collective-permute-start(f32[16,8,128]{2,1,0:T(8,128)S(1)} %sum_z.1.total_ref), channel_id=1, source_target_pairs={{0,16},{8,24},{16,0},{24,8},{1,17},{9,25},{17,1},{25,9},{2,18},{10... | collective-permute-start | bytes 196616 | tf_op jit(solution)/shard_map/ppermute | solution.py:32
  34.0 3.1 %collective-permute-start.8 = (f32[16,8,128]{2,1,0:T(8,128)S(1)}, f32[16,8,128]{2,1,0:T(8,128)S(1)}, u32[]{:S(2)}, u32[]{:S(2)}) collective-permute-start(f32[16,8,128]{2,1,0:T(8,128)S(1)} %sum_z.1.total_ref), channel_id=1, source_target_pairs={{0,8},{8,0},{16,24},{24,16},{1,9},{9,1},{17,25},{25,17},{2,10},{10... | collective-permute-start | bytes 196616 | tf_op jit(solution)/shard_map/ppermute | solution.py:32
  34.4 4.3 %collective-permute-start.9 = (f32[16,8,128]{2,1,0:T(8,128)S(1)}, f32[16,8,128]{2,1,0:T(8,128)S(1)}, u32[]{:S(2)}, u32[]{:S(2)}) collective-permute-start(f32[16,8,128]{2,1,0:T(8,128)S(1)} %sum_z.1.total_ref), channel_id=1, source_target_pairs={{0,24},{8,16},{16,8},{24,0},{1,25},{9,17},{17,9},{25,1},{2,26},{10... | collective-permute-start | bytes 196616 | tf_op jit(solution)/shard_map/ppermute | solution.py:32
  38.7 11.6 %collective-permute-start.10 = (bf16[256,128]{1,0:T(8,128)(2,1)S(1)}, bf16[256,128]{1,0:T(8,128)(2,1)S(1)}, u32[]{:S(2)}, u32[]{:S(2)}) collective-permute-start(bf16[256,128]{1,0:T(8,128)(2,1)S(1)} %hidden.1.after_ref.packet_ref), channel_id=1, source_target_pairs={{0,128},{128,0},{1,129},{129,1},{2,130},{130,2},{3,131},{131,3},{4... | collective-permute-start | bytes 196616 | tf_op jit(solution)/shard_map/ppermute | solution.py:32
  40.1 9.5 %collective-permute-start.11 = (f32[8,128]{1,0:T(8,128)S(1)}, f32[8,128]{1,0:T(8,128)S(1)}, u32[]{:S(2)}, u32[]{:S(2)}) collective-permute-start(f32[8,128]{1,0:T(8,128)S(1)} %get-tuple-element.57.pack_ref), channel_id=1, source_target_pairs={{0,1},{1,0},{2,3},{3,2},{4,5},{5,4},{6,7},{7,6},{8,9},{9,8},{10,11... | collective-permute-start | bytes 12296 | tf_op jit(solution)/shard_map/ppermute | solution.py:32
  46.5 5.7 %collective-permute-start.12 = (bf16[256,128]{1,0:T(8,128)(2,1)S(1)}, bf16[256,128]{1,0:T(8,128)(2,1)S(1)}, u32[]{:S(2)}, u32[]{:S(2)}) collective-permute-start(bf16[256,128]{1,0:T(8,128)(2,1)S(1)} %hidden.1.after_ref.packet_ref), channel_id=1, source_target_pairs={{0,1},{1,0},{2,3},{3,2},{4,5},{5,4},{6,7},{7,6},{8,9},{9,8},{10,11... | collective-permute-start | bytes 196616 | tf_op jit(solution)/shard_map/ppermute | solution.py:32
  49.6 11.8 %copy-start.6 = (bf16[8,3,128]{2,0,1:T(8,128)(2,1)S(1)}, bf16[8,3,128]{2,0,1:T(8,128)(2,1)}, u32[]{:S(2)}) copy-start(bf16[8,3,128]{2,0,1:T(8,128)(2,1)} %param.22) | copy-start | bytes 18436
  49.6 11.8 %copy-start.7 = (f32[8,1]{0,1:T(1,128)S(1)}, f32[8,1]{0,1:T(1,128)}, u32[]{:S(2)}) copy-start(f32[8,1]{0,1:T(1,128)} %param.23) | copy-start | bytes 100
  49.6 11.8 %copy-start.5 = (bf16[8,1,128,128]{3,2,1,0:T(8,128)(2,1)S(1)}, bf16[8,1,128,128]{3,2,1,0:T(8,128)(2,1)}, u32[]{:S(2)}) copy-start(bf16[8,1,128,128]{3,2,1,0:T(8,128)(2,1)} %param.24) | copy-start | bytes 786436
  50.3 2.7 %collective-permute-start.13 = (bf16[256,128]{1,0:T(8,128)(2,1)S(1)}, bf16[256,128]{1,0:T(8,128)(2,1)S(1)}, u32[]{:S(2)}, u32[]{:S(2)}) collective-permute-start(bf16[256,128]{1,0:T(8,128)(2,1)S(1)} %collective-permute-done.10.theirs_ref), channel_id=1, source_target_pairs={{0,1},{1,0},{2,3},{3,2},{4,5},{5,4},{6,7},{7,6},{8,9},{9,8},{10,11... | collective-permute-start | bytes 196616 | tf_op jit(solution)/shard_map/ppermute | solution.py:32
  56.0 18.0 %all-to-all-start = ((f32[256,1,128]{2,1,0:T(1,128)}), f32[256,1,128]{2,1,0:T(1,128)S(1)}, u32[]{:S(2)}, u32[]{:S(2)}) async-start(f32[256,1,128]{2,1,0:T(1,128)} %bitcast.14), calls=%async_computation | async-start | bytes 262144 | tf_op jit(solution)/shard_map/all_to_all | solution.py:501
